TPU v7x, 512 devices: a whole 4x4x16 slice. The times are simulated.
512 devices in a mesh: row: 32 (over z_lo, y, core), col: 16 (over x, z_hi).
Axes of the slice: x: 4, y: 4, z: 16 (z_hi: 4, z_lo: 4; z = z_hi * 4 + z_lo), core: 2. Of those that a mesh axis runs over, the one named last changes fastest.
Arguments:
- pair_input: bfloat16 [384, 384, 128], P('row', 'col'), may hold values from -6 to 6
- pair_mask: int32 [384, 384], P('row', 'col'), may hold values from 0 to 1, as said below
- out_norm_gain: float32 [128], replicated, may hold values from 0.1 to 1.9
- out_w_in: bfloat16 [128, 640], replicated, may hold values from -0.5 to 0.5
- out_final_gain: float32 [128], replicated, may hold values from 0.1 to 1.9
- out_w_out: bfloat16 [128, 128], replicated, may hold values from -0.5 to 0.5
- in_norm_gain: float32 [128], replicated, may hold values from 0.1 to 1.9
- in_w_in: bfloat16 [128, 640], replicated, may hold values from -0.5 to 0.5
- in_final_gain: float32 [128], replicated, may hold values from 0.1 to 1.9
- in_w_out: bfloat16 [128, 128], replicated, may hold values from -0.5 to 0.5
Outputs:
- pair_output: bfloat16 [384, 384, 128], P('row', 'col')
Inputs may be any that keep to these rules, and one draw needn't show every extreme that they name: pair_mask[i, j] = m[i] m[j] for a 0/1 mask m over the 384 tokens; token 0 is real and the last token is padding.
All inputs are finite; a program needn't handle non-finite values.
Results may differ from a plain program's by a relative error of at most 0.017.
Values may be sent and summed in bfloat16 or wider, within the bound.
No kernel may reach another device: no remote copies, remote signals or barrier semaphores. Data moves between devices by JAX's collectives and lax.ppermute only.
A program may use at most 64 MiB of HBM per device.

v0:
```python
import jax
import jax.numpy as jnp
from jax import lax
from jax.sharding import PartitionSpec as P


def spread_2(block, axis, owner):
    block = jnp.where(lax.axis_index(axis) == owner, block, jnp.zeros_like(block))
    return lax.psum(block, axis)


def layer_norm(values, gain):
    center = values - jnp.mean(values, axis=-1, keepdims=True)
    spread = jnp.mean(center * center, axis=-1, keepdims=True)
    return center * lax.rsqrt(spread + 1e-05) * gain


def project(pair, pair_mask, norm_gain, w_in):
    width = pair.shape[-1]
    normed = layer_norm(pair.astype(jnp.float32), norm_gain).astype(jnp.bfloat16)
    proj = jnp.dot(normed, w_in, preferred_element_type=jnp.float32)
    weight = pair_mask.astype(jnp.float32)[..., None]
    left_proj = (
        proj[..., :width] * jax.nn.sigmoid(proj[..., 2 * width : 3 * width]) * weight
    ).astype(jnp.bfloat16)
    right_proj = (
        proj[..., width : 2 * width] * jax.nn.sigmoid(proj[..., 3 * width : 4 * width]) * weight
    ).astype(jnp.bfloat16)
    out_gate = jax.nn.sigmoid(proj[..., 4 * width :])
    return (left_proj, right_proj, out_gate)


def finish(pair, tri_sum, out_gate, final_gain, w_out):
    final = layer_norm(tri_sum, final_gain).astype(jnp.bfloat16)
    update = jnp.dot(final, w_out, preferred_element_type=jnp.float32) * out_gate
    return (pair.astype(jnp.float32) + update).astype(jnp.bfloat16)


def per_device(
    pair_input,
    pair_mask,
    out_norm_gain,
    out_w_in,
    out_final_gain,
    out_w_out,
    in_norm_gain,
    in_w_in,
    in_final_gain,
    in_w_out,
):
    rows_here, cols_here, width = pair_input.shape
    ratio = lax.axis_size("row") // lax.axis_size("col")
    left_proj, right_proj, out_gate = project(pair_input, pair_mask, out_norm_gain, out_w_in)
    left_rows, right_rows = (
        lax.all_gather(left_proj, "col", axis=1, tiled=True),
        lax.all_gather(right_proj, "col", axis=1, tiled=True),
    )
    col_index = lax.axis_index("col")
    blocks = []
    for member in range(ratio):
        blocks.append(spread_2(right_rows, "row", col_index * ratio + member))
    right_strip = jnp.concatenate(blocks, axis=0)
    tri_sum = jnp.einsum("ikc,jkc->ijc", left_rows, right_strip, preferred_element_type=jnp.float32)
    middle = finish(pair_input, tri_sum, out_gate, out_final_gain, out_w_out)
    left_proj, right_proj, out_gate = project(middle, pair_mask, in_norm_gain, in_w_in)
    row_index = lax.axis_index("row")
    left_cols, right_cols = (
        lax.all_gather(left_proj, "row", axis=0, tiled=True),
        lax.all_gather(right_proj, "row", axis=0, tiled=True),
    )
    chosen = lax.dynamic_slice_in_dim(left_cols, row_index % ratio * rows_here, rows_here, 1)
    left_strip = spread_2(chosen, "col", row_index // ratio)
    tri_sum = jnp.einsum("kic,kjc->ijc", left_strip, right_cols, preferred_element_type=jnp.float32)
    return finish(middle, tri_sum, out_gate, in_final_gain, in_w_out)


def solution(mesh):
    placed = (P("row", "col", None), P("row", "col"), P(), P(), P(), P(), P(), P(), P(), P())
    return jax.shard_map(
        per_device, mesh=mesh, in_specs=placed, out_specs=P("row", "col", None), check_vma=False
    )
```

profile of v0, /device:TPU:1, one launch (start us, length us, event | category | flops | bytes accessed | tf_op | source)
XLA Modules:
  0.0 879.8 jit_solution(6509913979946884734)
XLA Ops:
  6.5 0.0 copy-start
  6.5 0.0 all-gather.5.cloned.1.call-start
  6.5 0.7 convert_element_type.44
  7.3 1.0 convert_reduce_fusion
  8.3 1.1 fusion.11
  9.4 0.0 copy-done
  9.4 1.2 fusion.9
  10.6 0.8 fusion.41
  11.4 0.0 all-gather.5.cloned.1.call-update
  11.4 0.0 all-gather.7.cloned.1.call-start
  11.5 0.7 all-gather.7.cloned.1.call-update
  12.2 0.0 all-reduce.6.cloned.1.call-start
  12.2 90.0 %all-gather.5.cloned.1.call-done = bf16[12,384,128]{2,1,0:T(8,128)(2,1)} async-done(((bf16[12,24,128]{2,1,0:T(8,128)(2,1)}), bf16[12,384,128]{2,1,0:T(8,128)(2,1)}) %all-gather.5.cloned.1.call-update) | async-done | bytes 1179664 | tf_op jit(solution)/shard_map/all_gather | solution.py:56
  102.2 2.9 broadcast_select_fusion.2
  105.1 0.0 all-reduce.6.cloned.1.call-update
  105.1 0.0 all-gather.11.cloned.1.call-start
  105.2 80.1 %all-gather.7.cloned.1.call-done = bf16[12,384,128]{2,1,0:T(8,128)(2,1)} async-done(((bf16[12,24,128]{2,1,0:T(8,128)(2,1)}), bf16[12,384,128]{2,1,0:T(8,128)(2,1)}) %all-gather.7.cloned.1.call-update) | async-done | bytes 1179664 | tf_op jit(solution)/shard_map/all_gather | solution.py:55
  185.2 3.0 copy.24
  188.2 288.4 %all-reduce.6.cloned.1.call-done = (bf16[12,384,128]{2,1,0:T(8,128)(2,1)}, bf16[12,384,128]{2,1,0:T(8,128)(2,1)}) async-done(((bf16[12,384,128]{2,1,0:T(8,128)(2,1)}, bf16[12,384,128]{2,1,0:T(8,128)(2,1)}), (bf16[12,384,128]{2,1,0:T(8,128)(2,1)}, bf16[12,384,128]{2,1,0:T(8,128)(2,1)})) %all-reduce.6.cloned.1.call-update) | async-done | bytes 2359312 | tf_op jit(solution)/shard_map/psum | solution.py:9
  476.6 1.8 pad_maximum_fusion
  478.5 2.9 copy.23
  481.4 0.0 copy-start.2
  481.4 0.0 copy-start.5
  481.4 0.0 copy-start.7
  481.4 3.2 fusion.60
  484.5 0.0 copy-start.3
  484.5 0.0 copy-start.4
  484.5 0.3 copy.25
  484.9 0.1 bitcast_reduce_fusion.1
  485.0 0.2 multiply_reduce_fusion.2
  485.2 0.0 copy-done.2
  485.2 0.0 copy-done.5
  485.2 0.0 copy-done.7
  485.2 0.4 fusion.59
  485.6 0.2 multiply_reduce_fusion.1
  485.8 0.0 copy-done.3
  485.8 0.0 copy-done.4
  485.8 0.4 fusion.7
  486.2 0.0 copy-start.1
  486.2 0.9 copy-done.1
  487.1 0.8 fusion.43
  487.9 0.0 all-gather.11.cloned.1.call-update
  487.9 0.0 all-gather.9.cloned.1.call-start
  488.0 0.5 all-gather.9.cloned.1.call-update
  488.5 0.0 all-reduce.4.cloned.1.call-start
  488.6 64.5 %all-gather.11.cloned.1.call-done = bf16[384,24,128]{2,1,0:T(8,128)(2,1)} async-done(((bf16[12,24,128]{2,1,0:T(8,128)(2,1)}), bf16[384,24,128]{2,1,0:T(8,128)(2,1)}) %all-gather.11.cloned.1.call-update) | async-done | bytes 2359312 | tf_op jit(solution)/shard_map/all_gather | solution.py:68
  553.1 2.2 constant_dynamic-slice_fusion
  555.3 1.6 copy.29
  556.9 1.3 broadcast_select_fusion
  558.2 0.0 all-reduce.4.cloned.1.call-update
  558.2 61.7 %all-gather.9.cloned.1.call-done = bf16[384,24,128]{2,1,0:T(8,128)(2,1)} async-done(((bf16[12,24,128]{2,1,0:T(8,128)(2,1)}), bf16[384,24,128]{2,1,0:T(8,128)(2,1)}) %all-gather.9.cloned.1.call-update) | async-done | bytes 2359312 | tf_op jit(solution)/shard_map/all_gather | solution.py:69
  619.9 10.9 %copy.27 = bf16[384,24,128]{1,0,2:T(8,128)(2,1)} copy(bf16[384,24,128]{2,1,0:T(8,128)(2,1)} %all-gather.9.cloned.1.call-done) | data formatting | bytes 4718592 | tf_op jit(solution)/shard_map/all_gather | solution.py:69
  630.8 0.0 copy-start.6
  630.8 0.0 copy-start.8
  630.8 232.4 %all-reduce.4.cloned.1.call-done = bf16[384,12,128]{0,1,2:T(8,128)(2,1)} async-done(((bf16[384,12,128]{0,1,2:T(8,128)(2,1)}), bf16[384,12,128]{0,1,2:T(8,128)(2,1)}) %all-reduce.4.cloned.1.call-update) | async-done | bytes 1179664 | tf_op jit(solution)/shard_map/psum | solution.py:9
  863.1 7.3 fusion.61
  870.4 0.3 copy.28
  870.7 0.1 bitcast_reduce_fusion
  870.9 0.2 multiply_reduce_fusion
  871.1 0.0 copy-done.6
  871.1 0.0 copy-done.8
  871.1 1.8 fusion.3
  (8 shorter events, 0.0 us)
Async XLA Ops:
  6.5 2.8 copy-start
  6.5 95.7 %all-gather.5.cloned.1.call-start = ((), (), s32[]{:S(2)}) async-start(), calls=%async_computation | async-start | bytes 1253376 | tf_op jit(solution)/shard_map/all_gather | solution.py:56
  11.4 173.8 %all-gather.7.cloned.1.call-start = ((), (), s32[]{:S(2)}) async-start(), calls=%async_computation.1 | async-start | bytes 1253376 | tf_op jit(solution)/shard_map/all_gather | solution.py:55
  12.2 464.5 %all-reduce.6.cloned.1.call-start = ((), (), s32[]{:S(2)}) async-start(), calls=%async_computation.5 | async-start | bytes 4718592 | tf_op jit(solution)/shard_map/psum | solution.py:9
  105.1 448.0 %all-gather.11.cloned.1.call-start = ((), (), s32[]{:S(2)}) async-start(), calls=%async_computation.3 | async-start | bytes 2433024 | tf_op jit(solution)/shard_map/all_gather | solution.py:68
  481.4 3.9 copy-start.2
  481.4 3.9 copy-start.5
  481.4 3.9 copy-start.7
  484.5 1.3 copy-start.3
  484.5 1.3 copy-start.4
  486.2 0.9 copy-start.1
  487.9 132.0 %all-gather.9.cloned.1.call-start = ((), (), s32[]{:S(2)}) async-start(), calls=%async_computation.2 | async-start | bytes 2433024 | tf_op jit(solution)/shard_map/all_gather | solution.py:69
  488.5 374.6 %all-reduce.4.cloned.1.call-start = ((), (), s32[]{:S(2)}) async-start(), calls=%async_computation.4 | async-start | bytes 3145728 | tf_op jit(solution)/shard_map/psum | solution.py:9
  630.8 240.3 %copy-start.6 = (bf16[128,128]{1,0:T(8,128)(2,1)S(1)}, bf16[128,128]{1,0:T(8,128)(2,1)}, u32[]{:S(2)}) copy-start(bf16[128,128]{1,0:T(8,128)(2,1)} %param.19) | copy-start | bytes 98308
  630.8 240.3 %copy-start.8 = (f32[128]{0:T(128)S(1)}, f32[128]{0:T(128)}, u32[]{:S(2)}) copy-start(f32[128]{0:T(128)} %param.18) | copy-start | bytes 1540
Sparse Core Ops, SparseCore 0:
  11.6 90.6 all-gather.4
  105.2 80.0 all-gather.6
  188.2 288.3 all-reduce.5
  488.0 65.0 all-gather.10
  555.1 64.7 all-gather.8
  622.7 240.3 all-reduce.3
where the time goes:
time: 892 us; the launch traced here: 880 us
  waiting for transfers between devices  818 us (92%)
  local copies, waits for them, and re-layouts  22.2 us (2%)
  matrix products  14.2 us (2%)
  between operations  13.7 us (2%)
  other arithmetic  11.2 us (1%)
    psum x2, waiting for transfers between devices, spread_2(): return lax.psum(block, axis)  521 us
    all_gather x1, waiting for transfers between devices, per_device(): lax.all_gather(right_proj, 'col', axis=1, tiled=True)  90 us
    all_gather x1, waiting for transfers between devices, per_device(): lax.all_gather(left_proj, 'col', axis=1, tiled=True)  80.1 us
    all_gather x1, waiting for transfers between devices, per_device(): lax.all_gather(left_proj, 'row', axis=0, tiled=True)  64.5 us
    all_gather x1, waiting for transfers between devices, per_device(): lax.all_gather(right_proj, 'row', axis=0, tiled=True)  61.7 us
  transfers between devices with their start and end apart: 6, of which 6 were waited for; matrix products, arithmetic and copies ran while one was open for 2% of the time, Pallas kernels for 0%

commit v1 on v0

v1 whole, which is shorter than its diff:
```python
import jax
import jax.numpy as jnp
import numpy as np
from jax import lax
from jax.experimental import pallas as pl
from jax.experimental.pallas import tpu as pltpu
from jax.sharding import Mesh
from jax.sharding import PartitionSpec as P

ROW = ("zl", "y", "core")
COL = ("x", "zh")
SIZES = {"zl": 4, "y": 4, "core": 2, "x": 4, "zh": 4}
CHANNEL = ("zl", "x", "y", "core")
LINE = ("zl", "zh")
PLANE = ("x", "y", "core")

ROWS, COLS, WIDTH = 12, 24, 128
TILE = ROWS * COLS
N = 384
F32, BF16 = jnp.float32, jnp.bfloat16


def one_hot(places):
    table = np.zeros((len(places), len(places)), np.float32)
    table[np.arange(len(places)), places] = 1
    return table


def sender_order(names):
    index = np.arange(128).reshape([SIZES[a] for a in CHANNEL])
    return index.transpose([CHANNEL.index(a) for a in names]).reshape(-1)


def layer_norm(values, gain):
    center = values - jnp.mean(values, axis=-1, keepdims=True)
    spread = jnp.mean(center * center, axis=-1, keepdims=True)
    return center * lax.rsqrt(spread + 1e-05) * gain


def flat_mask(mask):
    return jnp.concatenate([mask[i : i + 1] for i in range(ROWS)], axis=1)


def project(normed, mask, w_in):
    proj = lax.dot_general(
        w_in[:, : 4 * WIDTH], normed, (((0,), (1,)), ((), ())), preferred_element_type=F32
    )
    left = proj[:WIDTH] * jax.nn.sigmoid(proj[2 * WIDTH : 3 * WIDTH]) * mask
    right = proj[WIDTH : 2 * WIDTH] * jax.nn.sigmoid(proj[3 * WIDTH : 4 * WIDTH]) * mask
    return jnp.concatenate([left, right], axis=1).astype(BF16)


def update(pair, tri, norm_gain, w_in, final_gain, w_out):
    tri = tri.astype(F32)
    tri = jnp.concatenate([tri[:, i * TILE : (i + 1) * TILE] for i in range(4)], axis=0)
    final = layer_norm(tri.T, final_gain).astype(BF16)
    normed = layer_norm(pair, norm_gain).astype(BF16)
    gate = jax.nn.sigmoid(jnp.dot(normed, w_in[:, 4 * WIDTH :], preferred_element_type=F32))
    return (pair + jnp.dot(final, w_out, preferred_element_type=F32) * gate).astype(BF16)


def first_kernel(pair_ref, norm_gain, w_in, sent):
    pair = pair_ref[:TILE].astype(F32)
    mask = flat_mask(pair_ref[TILE : TILE + 16, :].astype(F32)[:ROWS, :COLS])
    normed = layer_norm(pair, norm_gain[...]).astype(BF16)
    sent[...] = project(normed, mask, w_in)


def middle_kernel(
    pair_ref, tri, norm_gain, w_in, final_gain, w_out, next_gain, next_w_in, middle, sent
):
    pair = pair_ref[:TILE].astype(F32)
    mask = flat_mask(pair_ref[TILE : TILE + 16, :].astype(F32)[:ROWS, :COLS])
    new = update(pair, tri[...], norm_gain[...], w_in, final_gain[...], w_out[...])
    middle[...] = new
    normed = layer_norm(new.astype(F32), next_gain[...]).astype(BF16)
    sent[...] = project(normed, mask, next_w_in)


def last_kernel(pair_ref, tri, norm_gain, w_in, final_gain, w_out, out):
    pair = pair_ref[...].astype(F32)
    out[...] = update(pair, tri[...], norm_gain[...], w_in, final_gain[...], w_out[...])


def pack(sums, swapped, out):
    for zh in range(4):
        strips = []
        for x in range(4):
            at = (x * 4 + zh) * COLS
            strips.append(
                jnp.concatenate(
                    [sums[i * 32 : (i + 1) * 32, at : at + COLS] for i in range(ROWS)], axis=1
                )
            )
        for zl in range(4):
            piece = jnp.concatenate([s[zl * 8 : (zl + 1) * 8] for s in strips], axis=0)
            rest = jnp.concatenate([piece[g * 8 : (g + 1) * 8, 256:] for g in range(4)], axis=1)
            place = zh * 4 + zl if swapped else zl * 4 + zh
            out[place] = jnp.concatenate([piece[:, :128], piece[:, 128:256], rest], axis=0).astype(BF16)


def outgoing_kernel(got, senders, rows, out):
    got = jnp.dot(senders[...], got[...], preferred_element_type=F32)

    def operand(at):
        return jnp.concatenate(
            [
                jnp.concatenate(
                    [got[x * 32 : (x + 1) * 32, at + i * COLS : at + (i + 1) * COLS] for x in range(4)],
                    axis=1,
                )
                for i in range(ROWS)
            ],
            axis=0,
        ).astype(BF16)

    left, right = operand(0), operand(TILE)
    right = jnp.dot(rows[...], right, preferred_element_type=F32).astype(BF16)
    sums = lax.dot_general(left, right, (((1,), (1,)), ((), ())), preferred_element_type=F32)
    pack(sums, True, out)


def incoming_kernel(got, senders, rows, out):
    got = jnp.dot(senders[...], got[...], preferred_element_type=F32)

    def operand(at):
        return jnp.concatenate(
            [
                jnp.concatenate(
                    [got[g * 8 : (g + 1) * 8, at + k * COLS : at + (k + 1) * COLS] for g in range(16)],
                    axis=1,
                )
                for k in range(ROWS)
            ],
            axis=0,
        ).astype(BF16)

    left, right = operand(0), operand(TILE)
    left = lax.dot_general(
        rows[...], left, (((1,), (1,)), ((), ())), preferred_element_type=F32
    ).astype(BF16)
    sums = jnp.dot(left, right, preferred_element_type=F32)
    pack(sums, False, out)


def add_kernel(got, out):
    parts = []
    for zl in range(4):
        total = got[zl * 4].astype(F32)
        for zh in range(1, 4):
            total += got[zl * 4 + zh].astype(F32)
        rest = jnp.concatenate([total[64:72, g * 32 : (g + 1) * 32] for g in range(4)], axis=0)
        parts.append(jnp.concatenate([total[:32], total[32:64], rest], axis=1))
    out[...] = jnp.concatenate(parts, axis=1).astype(BF16)


def call(kernel, name, *shapes):
    out = [jax.ShapeDtypeStruct(s, BF16) for s in shapes]
    return pl.pallas_call(
        kernel,
        out_shape=out if len(out) > 1 else out[0],
        name=name,
        compiler_params=pltpu.CompilerParams(vmem_limit_bytes=32 * 1024 * 1024),
    )


def per_device(
    pair_input,
    pair_mask,
    out_norm_gain,
    out_w_in,
    out_final_gain,
    out_w_out,
    in_norm_gain,
    in_w_in,
    in_final_gain,
    in_w_out,
):
    out_norm_gain, out_final_gain, in_norm_gain, in_final_gain = (
        g.reshape(1, WIDTH) for g in (out_norm_gain, out_final_gain, in_norm_gain, in_final_gain)
    )
    by_row = np.arange(N).reshape(ROWS, 32).T.reshape(-1)
    by_place = np.arange(N).reshape(32, ROWS).T.reshape(-1)
    out_senders = jnp.asarray(one_hot(sender_order(("x", "zl", "y", "core"))), BF16)
    in_senders = jnp.asarray(one_hot(sender_order(("x", "zl", "y", "core"))), BF16)
    out_rows = jnp.asarray(one_hot(by_row), BF16)
    in_rows = jnp.asarray(one_hot(by_place), BF16)

    mask = jnp.pad(pair_mask.astype(BF16), ((0, 16 - ROWS), (0, WIDTH - COLS)))
    pair = jnp.concatenate([pair_input.reshape(TILE, WIDTH), mask], axis=0)
    swap = [(zl * 4 + zh, zh * 4 + zl) for zl in range(4) for zh in range(4)]

    def spread(sent):
        return lax.all_to_all(sent, CHANNEL, 0, 0, tiled=True)

    def collect(pieces):
        got = lax.all_to_all(pieces, LINE, 0, 0, tiled=True)
        sums = call(add_kernel, "add_parts", (32, 4 * TILE))(got)
        return lax.all_to_all(sums, PLANE, 0, 0, tiled=True)

    swapped_pair = lax.ppermute(pair, LINE, swap)
    sent = call(first_kernel, "project_first", (WIDTH, 2 * TILE))(pair, out_norm_gain, out_w_in)
    pieces = call(outgoing_kernel, "outgoing", (16, 72, 128))(spread(sent), out_senders, out_rows)
    tri = collect(pieces)
    swapped_middle, sent = call(middle_kernel, "middle", (TILE, WIDTH), (WIDTH, 2 * TILE))(
        swapped_pair, tri, out_norm_gain, out_w_in, out_final_gain, out_w_out, in_norm_gain, in_w_in
    )
    middle = lax.ppermute(swapped_middle, LINE, swap)
    pieces = call(incoming_kernel, "incoming", (16, 72, 128))(spread(sent), in_senders, in_rows)
    tri = collect(pieces)
    out = call(last_kernel, "last", (TILE, WIDTH))(
        middle, tri, in_norm_gain, in_w_in, in_final_gain, in_w_out
    )
    return out.reshape(ROWS, COLS, WIDTH)


def solution(mesh):
    fine = Mesh(
        mesh.devices.reshape([SIZES[a] for a in ROW + COL]), ROW + COL
    )
    placed = (P(ROW, COL, None), P(ROW, COL), P(), P(), P(), P(), P(), P(), P(), P())
    return jax.shard_map(
        per_device, mesh=fine, in_specs=placed, out_specs=P(ROW, COL, None), check_vma=False
    )
```

time: 892 us -> 150 us (0.17); the launches traced: 880 us -> 147 us
  waiting for transfers between devices: 818 us -> 29.9 us
  blocking collectives: 0 us -> 80.8 us
  starting transfers between devices: 0.2 us -> 18.1 us
  local copies, waits for them, and re-layouts: 22.2 us -> 6.19 us
  matrix products: 14.2 us -> 0 us
  between operations: 13.7 us -> 0.26 us
    psum x2 -> x0, waiting for transfers between devices: 521 us -> none  [spread_2(): return lax.psum(block, axis)]
    all_gather x4 -> x0, waiting for transfers between devices: 296 us -> none  [the longest x1 90 us: per_device(): lax.all_gather(right_proj, 'col', axis=1, tiled=True)]
    all_to_all x0 -> x4, blocking collectives: none -> 80.8 us  [the longest x2 46.4 us: spread(): return lax.all_to_all(sent, CHANNEL, 0, 0, tiled=True)]
    all_to_all x0 -> x2, waiting for transfers between devices: none -> 29.9 us  [collect(): got = lax.all_to_all(pieces, LINE, 0, 0, tiled=True)]
    all_to_all x0 -> x2, starting transfers between devices: none -> 16.8 us  [collect(): got = lax.all_to_all(pieces, LINE, 0, 0, tiled=True)]
    dot_general x6 -> x0, matrix products: 14.2 us -> none  [the longest x1 7.26 us: per_device(): jnp.einsum('kic,kjc->ijc', left_strip, right_cols, preferred_element_type...]
    all_gather x2 -> x0, local copies, waits for them, and re-layouts: 13.8 us -> none  [the longest x1 10.9 us: per_device(): lax.all_gather(right_proj, 'row', axis=0, tiled=True)]
  transfers between devices with their start and end apart: 6 -> 4, of which waited for: 6 -> 2; matrix products, arithmetic and copies ran while one was open for 2% -> 1% of each run, Pallas kernels for 0% -> 0%
where the time goes in v1:
time: 150 us; the launch traced here: 147 us
  blocking collectives  80.8 us (54%)
  waiting for transfers between devices  29.9 us (20%)
  starting transfers between devices  18.1 us (12%)
  Pallas kernels  7.29 us (5%)
  local copies, waits for them, and re-layouts  6.19 us (4%)
  other arithmetic  4.33 us (3%)
    all_to_all x2, blocking collectives, spread(): return lax.all_to_all(sent, CHANNEL, 0, 0, tiled=True)  46.4 us
    all_to_all x2, blocking collectives, collect(): return lax.all_to_all(sums, PLANE, 0, 0, tiled=True)  34.4 us
    all_to_all x2, waiting for transfers between devices, collect(): got = lax.all_to_all(pieces, LINE, 0, 0, tiled=True)  29.9 us
    all_to_all x2, starting transfers between devices, collect(): got = lax.all_to_all(pieces, LINE, 0, 0, tiled=True)  16.8 us
    unnamed x32, local copies, waits for them, and re-layouts  5.63 us
  transfers between devices with their start and end apart: 4, of which 2 were waited for; matrix products, arithmetic and copies ran while one was open for 1% of the time, Pallas kernels for 0%

profile of v1, /device:TPU:1, one launch (start us, length us, event | category | flops | bytes accessed | tf_op | source)
XLA Modules:
  0.0 146.8 jit_solution(14263104094571903067)
XLA Ops:
  0.0 0.0 copy-start
  0.0 0.7 convert_element_type.5
  0.7 0.9 fusion.1.pair_ref
  1.6 0.0 copy-start.7
  1.6 0.0 copy-done
  1.7 0.6 copy-done.7
  2.3 0.5 project_first.1
  2.8 0.5 broadcast.6
  3.3 0.7 reduce
  4.0 0.2 reshape.32
  4.2 25.4 %all_to_all.54 = bf16[128,2,288]{2,1,0:T(2,128)(2,1)S(1)} all-to-all(bf16[128,2,288]{2,1,0:T(2,128)(2,1)S(1)} %reshape.32), channel_id=1, replica_groups=mesh['zl'=4,'y'=4,'core'=2,'x'=4,'zh'=4] {'zl','x','y','core'}, dimensions={0} | all-to-all | bytes 294912 | tf_op jit(solution)/shard_map/all_to_all | solution.py:194
  29.6 0.3 reshape.33
  29.9 0.0 copy-start.3
  29.9 0.0 copy-start.4
  30.0 0.9 copy-done.3
  30.9 0.0 copy-done.4
  30.9 2.0 %outgoing.1 = bf16[16,72,128]{2,1,0:T(8,128)(2,1)} custom-call(bf16[128,576]{1,0:T(8,128)(2,1)S(1)} %bitcast.26, bf16[128,128]{1,0:T(8,128)(2,1)S(1)} %copy-done.4, bf16[384,384]{1,0:T(8,128)(2,1)S(1)} %copy-done.3), custom_call_target="tpu_custom_call" | custom-call | tf_op jit(solution)/shard_map/outgoing/pallas_call | solution.py:203
  32.9 12.2 %all-to-all-start.1 = ((bf16[16,72,128]{2,1,0:T(8,128)(2,1)}), bf16[16,72,128]{2,1,0:T(8,128)(2,1)S(1)}, u32[]{:S(2)}, u32[]{:S(2)}) async-start(bf16[16,72,128]{2,1,0:T(8,128)(2,1)} %outgoing.1), calls=%async_computation.1 | async-start | bytes 589824 | tf_op jit(solution)/shard_map/all_to_all | solution.py:197
  45.1 0.7 collective-permute-start
  45.8 15.0 %all-to-all-done.1.got = bf16[16,72,128]{2,1,0:T(8,128)(2,1)S(1)} async-done(((bf16[16,72,128]{2,1,0:T(8,128)(2,1)}), bf16[16,72,128]{2,1,0:T(8,128)(2,1)S(1)}, u32[]{:S(2)}, u32[]{:S(2)}) %all-to-all-start.1) | async-done | bytes 294944 | tf_op jit(solution)/shard_map/all_to_all | solution.py:197
  60.7 0.2 add_parts.2
  60.9 0.7 reduce.1
  61.6 0.1 reshape.34
  61.7 17.2 %all_to_all.55 = bf16[32,2,576]{2,1,0:T(2,128)(2,1)S(1)} all-to-all(bf16[32,2,576]{2,1,0:T(2,128)(2,1)S(1)} %reshape.34), channel_id=1, replica_groups=mesh['zl'=4,'y'=4,'core'=2,'x'=4,'zh'=4] {'x','y','core'}, dimensions={0} | all-to-all | bytes 147456 | tf_op jit(solution)/shard_map/all_to_all | solution.py:199
  78.9 0.1 reshape.35
  79.1 0.0 copy-start.1
  79.1 0.0 copy-start.5
  79.1 0.0 collective-permute-done.pair_ref
  79.1 0.0 copy-start.8
  79.1 0.0 copy-start.9
  79.2 0.8 copy-done.1
  80.0 0.0 copy-done.5
  80.0 0.0 copy-done.8
  80.0 0.0 copy-done.9
  80.0 1.1 middle.1
  81.1 0.7 reduce.2
  81.8 0.2 reshape.36
  82.0 21.0 %all_to_all.56 = bf16[128,2,288]{2,1,0:T(2,128)(2,1)S(1)} all-to-all(bf16[128,2,288]{2,1,0:T(2,128)(2,1)S(1)} %reshape.36), channel_id=1, replica_groups=mesh['zl'=4,'y'=4,'core'=2,'x'=4,'zh'=4] {'zl','x','y','core'}, dimensions={0} | all-to-all | bytes 294912 | tf_op jit(solution)/shard_map/all_to_all | solution.py:194
  103.0 0.3 reshape.37
  103.3 0.0 copy-start.2
  103.3 0.9 copy-done.2
  104.3 2.2 %incoming.1 = bf16[16,72,128]{2,1,0:T(8,128)(2,1)} custom-call(bf16[128,576]{1,0:T(8,128)(2,1)S(1)} %bitcast.25, bf16[128,128]{1,0:T(8,128)(2,1)S(1)} %copy-done.4, bf16[384,384]{1,0:T(8,128)(2,1)S(1)} %copy-done.2), custom_call_target="tpu_custom_call" | custom-call | tf_op jit(solution)/shard_map/incoming/pallas_call | solution.py:209
  106.4 4.6 %all-to-all-start.4 = ((bf16[16,72,128]{2,1,0:T(8,128)(2,1)}), bf16[16,72,128]{2,1,0:T(8,128)(2,1)S(1)}, u32[]{:S(2)}, u32[]{:S(2)}) async-start(bf16[16,72,128]{2,1,0:T(8,128)(2,1)} %incoming.1), calls=%async_computation.4 | async-start | bytes 589824 | tf_op jit(solution)/shard_map/all_to_all | solution.py:197
  111.0 0.7 collective-permute-start.1
  111.7 15.0 %all-to-all-done.4.got = bf16[16,72,128]{2,1,0:T(8,128)(2,1)S(1)} async-done(((bf16[16,72,128]{2,1,0:T(8,128)(2,1)}), bf16[16,72,128]{2,1,0:T(8,128)(2,1)S(1)}, u32[]{:S(2)}, u32[]{:S(2)}) %all-to-all-start.4) | async-done | bytes 294944 | tf_op jit(solution)/shard_map/all_to_all | solution.py:197
  126.6 0.2 add_parts.3
  126.8 0.7 reduce.3
  127.4 0.1 reshape.38
  127.6 17.2 %all_to_all.57 = bf16[32,2,576]{2,1,0:T(2,128)(2,1)S(1)} all-to-all(bf16[32,2,576]{2,1,0:T(2,128)(2,1)S(1)} %reshape.38), channel_id=1, replica_groups=mesh['zl'=4,'y'=4,'core'=2,'x'=4,'zh'=4] {'x','y','core'}, dimensions={0} | all-to-all | bytes 147456 | tf_op jit(solution)/shard_map/all_to_all | solution.py:199
  144.8 0.1 reshape.39
  144.9 0.0 copy-start.6
  144.9 0.0 collective-permute-done.1.pair_ref
  144.9 0.0 copy-start.10
  145.0 0.7 copy-done.6
  145.7 0.0 copy-done.10
  145.7 1.2 last.1
  (4 shorter events, 0.1 us)
Async XLA Ops:
  0.0 1.6 %copy-start = (bf16[128,640]{1,0:T(8,128)(2,1)S(1)}, bf16[128,640]{1,0:T(8,128)(2,1)}, u32[]{:S(2)}) copy-start(bf16[128,640]{1,0:T(8,128)(2,1)} %w_in.4) | copy-start | bytes 491524
  1.6 0.7 copy-start.7
  29.9 1.0 copy-start.3
  29.9 1.0 copy-start.4
  32.9 27.8 %all-to-all-start.1 = ((bf16[16,72,128]{2,1,0:T(8,128)(2,1)}), bf16[16,72,128]{2,1,0:T(8,128)(2,1)S(1)}, u32[]{:S(2)}, u32[]{:S(2)}) async-start(bf16[16,72,128]{2,1,0:T(8,128)(2,1)} %outgoing.1), calls=%async_computation.1 | async-start | bytes 589824 | tf_op jit(solution)/shard_map/all_to_all | solution.py:197
  45.1 34.0 %collective-permute-start = (bf16[304,128]{1,0:T(8,128)(2,1)S(1)}, bf16[304,128]{1,0:T(8,128)(2,1)S(1)}, u32[]{:S(2)}, u32[]{:S(2)}) collective-permute-start(bf16[304,128]{1,0:T(8,128)(2,1)S(1)} %fusion.1.pair_ref), channel_id=1, source_target_pairs={{0,0},{1,128},{2,256},{3,384},{128,1},{129,129},{130,257},{131,385... | collective-permute-start | bytes 233480 | tf_op jit(solution)/shard_map/ppermute | solution.py:201
  79.1 0.9 copy-start.1
  79.1 0.9 copy-start.5
  79.1 0.9 copy-start.8
  79.1 0.9 copy-start.9
  103.3 1.0 copy-start.2
  106.4 20.2 %all-to-all-start.4 = ((bf16[16,72,128]{2,1,0:T(8,128)(2,1)}), bf16[16,72,128]{2,1,0:T(8,128)(2,1)S(1)}, u32[]{:S(2)}, u32[]{:S(2)}) async-start(bf16[16,72,128]{2,1,0:T(8,128)(2,1)} %incoming.1), calls=%async_computation.4 | async-start | bytes 589824 | tf_op jit(solution)/shard_map/all_to_all | solution.py:197
  111.0 34.0 %collective-permute-start.1 = (bf16[288,128]{1,0:T(8,128)(2,1)S(1)}, bf16[288,128]{1,0:T(8,128)(2,1)S(1)}, u32[]{:S(2)}, u32[]{:S(2)}) collective-permute-start(bf16[288,128]{1,0:T(8,128)(2,1)S(1)} %get-tuple-element.7), channel_id=1, source_target_pairs={{0,0},{1,128},{2,256},{3,384},{128,1},{129,129},{130,257},{131,385... | collective-permute-start | bytes 221192 | tf_op jit(solution)/shard_map/ppermute | solution.py:208
  144.9 0.8 copy-start.6
  144.9 0.7 copy-start.10

commit v2 on v1

--- a/solution.py
+++ b/solution.py
@@ -10,9 +10,9 @@
 ROW = ("zl", "y", "core")
 COL = ("x", "zh")
 SIZES = {"zl": 4, "y": 4, "core": 2, "x": 4, "zh": 4}
-CHANNEL = ("zl", "x", "y", "core")
-LINE = ("zl", "zh")
-PLANE = ("x", "y", "core")
+CHANNEL = ("y", "zh", "zl", "core")
+PLANE = ("x", "y")
+LINE = ("zh", "zl", "core")
 
 ROWS, COLS, WIDTH = 12, 24, 128
 TILE = ROWS * COLS
@@ -83,19 +83,19 @@
 
 
 def pack(sums, swapped, out):
-    for zh in range(4):
+    for x in range(4):
         strips = []
-        for x in range(4):
+        for zh in range(4):
             at = (x * 4 + zh) * COLS
             strips.append(
                 jnp.concatenate(
                     [sums[i * 32 : (i + 1) * 32, at : at + COLS] for i in range(ROWS)], axis=1
                 )
             )
-        for zl in range(4):
-            piece = jnp.concatenate([s[zl * 8 : (zl + 1) * 8] for s in strips], axis=0)
+        for y in range(4):
+            piece = jnp.concatenate([s[y * 8 : (y + 1) * 8] for s in strips], axis=0)
             rest = jnp.concatenate([piece[g * 8 : (g + 1) * 8, 256:] for g in range(4)], axis=1)
-            place = zh * 4 + zl if swapped else zl * 4 + zh
+            place = y * 4 + x if swapped else x * 4 + y
             out[place] = jnp.concatenate([piece[:, :128], piece[:, 128:256], rest], axis=0).astype(BF16)
 
 
@@ -106,7 +106,7 @@
         return jnp.concatenate(
             [
                 jnp.concatenate(
-                    [got[x * 32 : (x + 1) * 32, at + i * COLS : at + (i + 1) * COLS] for x in range(4)],
+                    [got[g * 32 : (g + 1) * 32, at + i * COLS : at + (i + 1) * COLS] for g in range(4)],
                     axis=1,
                 )
                 for i in range(ROWS)
@@ -120,8 +120,8 @@
     pack(sums, True, out)
 
 
-def incoming_kernel(got, senders, rows, out):
-    got = jnp.dot(senders[...], got[...], preferred_element_type=F32)
+def incoming_kernel(got, rows, out):
+    got = got[...].astype(F32)
 
     def operand(at):
         return jnp.concatenate(
@@ -145,10 +145,10 @@
 
 def add_kernel(got, out):
     parts = []
-    for zl in range(4):
-        total = got[zl * 4].astype(F32)
-        for zh in range(1, 4):
-            total += got[zl * 4 + zh].astype(F32)
+    for y in range(4):
+        total = got[y].astype(F32)
+        for x in range(1, 4):
+            total += got[x * 4 + y].astype(F32)
         rest = jnp.concatenate([total[64:72, g * 32 : (g + 1) * 32] for g in range(4)], axis=0)
         parts.append(jnp.concatenate([total[:32], total[32:64], rest], axis=1))
     out[...] = jnp.concatenate(parts, axis=1).astype(BF16)
@@ -179,34 +179,33 @@
     out_norm_gain, out_final_gain, in_norm_gain, in_final_gain = (
         g.reshape(1, WIDTH) for g in (out_norm_gain, out_final_gain, in_norm_gain, in_final_gain)
     )
-    by_row = np.arange(N).reshape(ROWS, 32).T.reshape(-1)
-    by_place = np.arange(N).reshape(32, ROWS).T.reshape(-1)
-    out_senders = jnp.asarray(one_hot(sender_order(("x", "zl", "y", "core"))), BF16)
-    in_senders = jnp.asarray(one_hot(sender_order(("x", "zl", "y", "core"))), BF16)
-    out_rows = jnp.asarray(one_hot(by_row), BF16)
+    by_array = np.arange(N).reshape(ROWS, 4, 4, 2).transpose(2, 1, 3, 0).reshape(-1)
+    by_place = np.arange(N).reshape(4, 4, 2, ROWS).transpose(3, 1, 0, 2).reshape(-1)
+    out_senders = jnp.asarray(one_hot(sender_order(("zh", "y", "zl", "core"))), BF16)
+    out_rows = jnp.asarray(one_hot(by_array), BF16)
     in_rows = jnp.asarray(one_hot(by_place), BF16)
 
     mask = jnp.pad(pair_mask.astype(BF16), ((0, 16 - ROWS), (0, WIDTH - COLS)))
     pair = jnp.concatenate([pair_input.reshape(TILE, WIDTH), mask], axis=0)
-    swap = [(zl * 4 + zh, zh * 4 + zl) for zl in range(4) for zh in range(4)]
+    swap = [(x * 4 + y, y * 4 + x) for x in range(4) for y in range(4)]
 
     def spread(sent):
         return lax.all_to_all(sent, CHANNEL, 0, 0, tiled=True)
 
     def collect(pieces):
-        got = lax.all_to_all(pieces, LINE, 0, 0, tiled=True)
+        got = lax.all_to_all(pieces, PLANE, 0, 0, tiled=True)
         sums = call(add_kernel, "add_parts", (32, 4 * TILE))(got)
-        return lax.all_to_all(sums, PLANE, 0, 0, tiled=True)
-
-    swapped_pair = lax.ppermute(pair, LINE, swap)
+        return lax.all_to_all(sums, LINE, 0, 0, tiled=True)
+
+    swapped_pair = lax.ppermute(pair, ("y", "x"), swap)
     sent = call(first_kernel, "project_first", (WIDTH, 2 * TILE))(pair, out_norm_gain, out_w_in)
     pieces = call(outgoing_kernel, "outgoing", (16, 72, 128))(spread(sent), out_senders, out_rows)
     tri = collect(pieces)
     swapped_middle, sent = call(middle_kernel, "middle", (TILE, WIDTH), (WIDTH, 2 * TILE))(
         swapped_pair, tri, out_norm_gain, out_w_in, out_final_gain, out_w_out, in_norm_gain, in_w_in
     )
-    middle = lax.ppermute(swapped_middle, LINE, swap)
-    pieces = call(incoming_kernel, "incoming", (16, 72, 128))(spread(sent), in_senders, in_rows)
+    middle = lax.ppermute(swapped_middle, ("y", "x"), swap)
+    pieces = call(incoming_kernel, "incoming", (16, 72, 128))(spread(sent), in_rows)
     tri = collect(pieces)
     out = call(last_kernel, "last", (TILE, WIDTH))(
         middle, tri, in_norm_gain, in_w_in, in_final_gain, in_w_out

time: 150 us -> 153 us (1.020); the launches traced: 147 us -> 153 us
  blocking collectives: 80.8 us -> 94.6 us
  starting transfers between devices: 18.1 us -> 14.2 us
  waiting for transfers between devices: 29.9 us -> 26.2 us
  Pallas kernels: 7.29 us -> 5.66 us
    all_to_all x2, blocking collectives: 46.4 us -> 70.9 us  [spread(): return lax.all_to_all(sent, CHANNEL, 0, 0, tiled=True)]
    all_to_all x2, blocking collectives: 34.4 us -> 23.6 us  [collect(): got = lax.all_to_all(pieces, PLANE, 0, 0, tiled=True)]
    all_to_all x2, starting transfers between devices: 16.8 us -> 12.9 us  [collect(): return lax.all_to_all(sums, LINE, 0, 0, tiled=True)]
    all_to_all x2, waiting for transfers between devices: 29.9 us -> 26.2 us  [collect(): return lax.all_to_all(sums, LINE, 0, 0, tiled=True)]
  transfers between devices with their start and end apart: 4 -> 4, of which waited for: 2 -> 2; matrix products, arithmetic and copies ran while one was open for 1% -> 0% of each run, Pallas kernels for 0% -> 0%
where the time goes in v2:
time: 153 us
  blocking collectives  94.6 us (62%)
  waiting for transfers between devices  26.2 us (17%)
  starting transfers between devices  14.2 us (9%)
  local copies, waits for them, and re-layouts  7.45 us (5%)
  Pallas kernels  5.66 us (4%)
  other arithmetic  4.33 us (3%)
    all_to_all x2, blocking collectives, spread(): return lax.all_to_all(sent, CHANNEL, 0, 0, tiled=True)  70.9 us
    all_to_all x2, waiting for transfers between devices, collect(): return lax.all_to_all(sums, LINE, 0, 0, tiled=True)  26.2 us
    all_to_all x2, blocking collectives, collect(): got = lax.all_to_all(pieces, PLANE, 0, 0, tiled=True)  23.6 us
    all_to_all x2, starting transfers between devices, collect(): return lax.all_to_all(sums, LINE, 0, 0, tiled=True)  12.9 us
    unnamed x32, local copies, waits for them, and re-layouts  6.89 us
  transfers between devices with their start and end apart: 4, of which 2 were waited for; matrix products, arithmetic and copies ran while one was open for 0% of the time, Pallas kernels for 0%

profile of v2, /device:TPU:1, one launch (start us, length us, event | category | flops | bytes accessed | tf_op | source)
XLA Modules:
  0.0 152.7 jit_solution(16707005739499482398)
XLA Ops:
  0.0 0.0 copy-start
  0.0 0.7 convert_element_type.5
  0.7 0.9 fusion.1.pair_ref
  1.6 0.0 copy-start.7
  1.6 0.0 copy-done
  1.7 0.6 copy-done.7
  2.3 0.5 project_first.1
  2.8 0.5 broadcast.6
  3.3 0.7 reduce
  4.0 0.2 reshape.32
  4.2 40.3 %all_to_all.54 = bf16[128,2,288]{2,1,0:T(2,128)(2,1)S(1)} all-to-all(bf16[128,2,288]{2,1,0:T(2,128)(2,1)S(1)} %reshape.32), channel_id=1, replica_groups=mesh['zl'=4,'y'=4,'core'=2,'x'=4,'zh'=4] {'y','zh','zl','core'}, dimensions={0} | all-to-all | bytes 294912 | tf_op jit(solution)/shard_map/all_to_all | solution.py:193
  44.5 0.3 reshape.33
  44.8 0.0 copy-start.2
  44.8 0.0 copy-start.6
  44.8 0.9 copy-done.2
  45.7 0.0 copy-done.6
  45.7 1.3 outgoing.1
  47.1 13.0 %all_to_all.55.got = bf16[16,72,128]{2,1,0:T(8,128)(2,1)S(1)} all-to-all(bf16[16,72,128]{2,1,0:T(8,128)(2,1)S(1)} %outgoing.1), channel_id=1, replica_groups=mesh['zl'=4,'y'=4,'core'=2,'x'=4,'zh'=4] {'x','y'}, dimensions={0} | all-to-all | bytes 589824 | tf_op jit(solution)/shard_map/all_to_all | solution.py:196
  60.1 0.2 add_parts.2
  60.2 0.7 reduce.1
  60.9 0.8 reshape.34
  61.7 6.5 %all-to-all-start.2 = ((bf16[32,2,576]{2,1,0:T(2,128)(2,1)}), bf16[32,2,576]{2,1,0:T(2,128)(2,1)S(1)}, u32[]{:S(2)}, u32[]{:S(2)}) async-start(bf16[32,2,576]{2,1,0:T(2,128)(2,1)} %reshape.34), calls=%async_computation.2 | async-start | bytes 163840 | tf_op jit(solution)/shard_map/all_to_all | solution.py:198
  68.1 0.7 collective-permute-start
  68.8 13.1 %all-to-all-done.2 = bf16[32,2,576]{2,1,0:T(2,128)(2,1)S(1)} async-done(((bf16[32,2,576]{2,1,0:T(2,128)(2,1)}), bf16[32,2,576]{2,1,0:T(2,128)(2,1)S(1)}, u32[]{:S(2)}, u32[]{:S(2)}) %all-to-all-start.2) | async-done | bytes 73760 | tf_op jit(solution)/shard_map/all_to_all | solution.py:198
  81.9 0.1 reshape.35
  82.1 0.0 copy-start.1
  82.1 0.0 copy-start.4
  82.1 0.0 collective-permute-done.pair_ref
  82.1 0.0 copy-start.8
  82.1 0.0 copy-start.9
  82.1 0.8 copy-done.1
  83.0 0.0 copy-done.4
  83.0 0.0 copy-done.8
  83.0 0.0 copy-done.9
  83.0 1.1 middle.1
  84.1 0.7 reduce.2
  84.8 0.2 reshape.36
  85.0 30.7 %all_to_all.56 = bf16[128,2,288]{2,1,0:T(2,128)(2,1)S(1)} all-to-all(bf16[128,2,288]{2,1,0:T(2,128)(2,1)S(1)} %reshape.36), channel_id=1, replica_groups=mesh['zl'=4,'y'=4,'core'=2,'x'=4,'zh'=4] {'y','zh','zl','core'}, dimensions={0} | all-to-all | bytes 294912 | tf_op jit(solution)/shard_map/all_to_all | solution.py:193
  115.7 0.3 reshape.37
  116.0 0.0 copy-start.3
  116.0 0.9 copy-done.3
  116.9 1.2 incoming.1
  118.2 10.6 %all_to_all.57.got = bf16[16,72,128]{2,1,0:T(8,128)(2,1)S(1)} all-to-all(bf16[16,72,128]{2,1,0:T(8,128)(2,1)S(1)} %incoming.1), channel_id=1, replica_groups=mesh['zl'=4,'y'=4,'core'=2,'x'=4,'zh'=4] {'x','y'}, dimensions={0} | all-to-all | bytes 589824 | tf_op jit(solution)/shard_map/all_to_all | solution.py:196
  128.8 0.2 add_parts.3
  129.0 0.7 reduce.3
  129.6 0.8 reshape.38
  130.4 6.5 %all-to-all-start.5 = ((bf16[32,2,576]{2,1,0:T(2,128)(2,1)}), bf16[32,2,576]{2,1,0:T(2,128)(2,1)S(1)}, u32[]{:S(2)}, u32[]{:S(2)}) async-start(bf16[32,2,576]{2,1,0:T(2,128)(2,1)} %reshape.38), calls=%async_computation.5 | async-start | bytes 163840 | tf_op jit(solution)/shard_map/all_to_all | solution.py:198
  136.9 0.7 collective-permute-start.1
  137.5 13.1 %all-to-all-done.5 = bf16[32,2,576]{2,1,0:T(2,128)(2,1)S(1)} async-done(((bf16[32,2,576]{2,1,0:T(2,128)(2,1)}), bf16[32,2,576]{2,1,0:T(2,128)(2,1)S(1)}, u32[]{:S(2)}, u32[]{:S(2)}) %all-to-all-start.5) | async-done | bytes 73760 | tf_op jit(solution)/shard_map/all_to_all | solution.py:198
  150.7 0.1 reshape.39
  150.8 0.0 copy-start.5
  150.8 0.0 collective-permute-done.1.pair_ref
  150.8 0.0 copy-start.10
  150.9 0.7 copy-done.5
  151.6 0.0 copy-done.10
  151.6 1.2 last.1
  (4 shorter events, 0.1 us)
Async XLA Ops:
  0.0 1.6 %copy-start = (bf16[128,640]{1,0:T(8,128)(2,1)S(1)}, bf16[128,640]{1,0:T(8,128)(2,1)}, u32[]{:S(2)}) copy-start(bf16[128,640]{1,0:T(8,128)(2,1)} %w_in.4) | copy-start | bytes 491524
  1.6 0.7 copy-start.7
  44.8 1.0 copy-start.2
  44.8 1.0 copy-start.6
  61.7 20.3 %all-to-all-start.2 = ((bf16[32,2,576]{2,1,0:T(2,128)(2,1)}), bf16[32,2,576]{2,1,0:T(2,128)(2,1)S(1)}, u32[]{:S(2)}, u32[]{:S(2)}) async-start(bf16[32,2,576]{2,1,0:T(2,128)(2,1)} %reshape.34), calls=%async_computation.2 | async-start | bytes 163840 | tf_op jit(solution)/shard_map/all_to_all | solution.py:198
  68.1 14.0 %collective-permute-start = (bf16[304,128]{1,0:T(8,128)(2,1)S(1)}, bf16[304,128]{1,0:T(8,128)(2,1)S(1)}, u32[]{:S(2)}, u32[]{:S(2)}) collective-permute-start(bf16[304,128]{1,0:T(8,128)(2,1)S(1)} %fusion.1.pair_ref), channel_id=1, source_target_pairs={{0,0},{4,32},{8,64},{12,96},{32,4},{36,36},{40,68},{44,100},{64,8}... | collective-permute-start | bytes 233480 | tf_op jit(solution)/shard_map/ppermute | solution.py:200
  82.1 0.9 copy-start.1
  82.1 0.9 copy-start.4
  82.1 0.9 copy-start.8
  82.1 0.9 copy-start.9
  116.0 1.0 copy-start.3
  130.4 20.2 %all-to-all-start.5 = ((bf16[32,2,576]{2,1,0:T(2,128)(2,1)}), bf16[32,2,576]{2,1,0:T(2,128)(2,1)S(1)}, u32[]{:S(2)}, u32[]{:S(2)}) async-start(bf16[32,2,576]{2,1,0:T(2,128)(2,1)} %reshape.38), calls=%async_computation.5 | async-start | bytes 163840 | tf_op jit(solution)/shard_map/all_to_all | solution.py:198
  136.9 14.0 %collective-permute-start.1 = (bf16[288,128]{1,0:T(8,128)(2,1)S(1)}, bf16[288,128]{1,0:T(8,128)(2,1)S(1)}, u32[]{:S(2)}, u32[]{:S(2)}) collective-permute-start(bf16[288,128]{1,0:T(8,128)(2,1)S(1)} %get-tuple-element.7), channel_id=1, source_target_pairs={{0,0},{4,32},{8,64},{12,96},{32,4},{36,36},{40,68},{44,100},{64,8}... | collective-permute-start | bytes 221192 | tf_op jit(solution)/shard_map/ppermute | solution.py:207
  150.8 0.8 copy-start.5
  150.8 0.7 copy-start.10

commit v3 on v1

v3 whole, which is shorter than its diff:
```python
import jax
import jax.numpy as jnp
import numpy as np
from jax import lax
from jax.experimental import pallas as pl
from jax.experimental.pallas import tpu as pltpu
from jax.sharding import Mesh
from jax.sharding import PartitionSpec as P

ROW = ("zl", "y", "core")
COL = ("x", "zh")
SIZES = {"zl": 4, "y": 4, "core": 2, "x": 4, "zh": 4}
CHANNEL = ("zl", "x", "y", "core")
LINE = ("zh", "zl")
PLANE = ("x", "y", "core")

ROWS, COLS, WIDTH = 12, 24, 128
TILE = ROWS * COLS
N = 384
F32, BF16 = jnp.float32, jnp.bfloat16


def one_hot(places):
    table = np.zeros((len(places), len(places)), np.float32)
    table[np.arange(len(places)), places] = 1
    return table


def sender_order(names):
    index = np.arange(128).reshape([SIZES[a] for a in CHANNEL])
    return index.transpose([CHANNEL.index(a) for a in names]).reshape(-1)


def layer_norm(values, gain):
    center = values - jnp.mean(values, axis=-1, keepdims=True)
    spread = jnp.mean(center * center, axis=-1, keepdims=True)
    return center * lax.rsqrt(spread + 1e-05) * gain


def flat_mask(mask):
    return jnp.concatenate([mask[i : i + 1] for i in range(ROWS)], axis=1)


def project(normed, mask, w_in):
    proj = lax.dot_general(
        w_in[:, : 4 * WIDTH], normed, (((0,), (1,)), ((), ())), preferred_element_type=F32
    )
    left = proj[:WIDTH] * jax.nn.sigmoid(proj[2 * WIDTH : 3 * WIDTH]) * mask
    right = proj[WIDTH : 2 * WIDTH] * jax.nn.sigmoid(proj[3 * WIDTH : 4 * WIDTH]) * mask
    return left.astype(BF16), right.astype(BF16)


def update(pair, tri, norm_gain, w_in, final_gain, w_out):
    tri = jnp.concatenate(tri, axis=0)
    final = layer_norm(tri.T, final_gain).astype(BF16)
    normed = layer_norm(pair, norm_gain).astype(BF16)
    gate = jax.nn.sigmoid(jnp.dot(normed, w_in[:, 4 * WIDTH :], preferred_element_type=F32))
    return (pair + jnp.dot(final, w_out, preferred_element_type=F32) * gate).astype(BF16)


def sums_of(tri):
    rows = [tri[:, i, :].astype(F32) for i in range(2)]
    return [r[:, i * TILE : (i + 1) * TILE] for r in rows for i in range(2)]


def first_kernel(pair_ref, mask_ref, norm_gain, w_in, kept, sent):
    pair = pair_ref[...]
    mask = mask_ref[...].astype(F32)
    kept[:TILE] = pair
    wide = jnp.concatenate([mask, jnp.zeros((ROWS, WIDTH - COLS), F32)], axis=1)
    kept[TILE:] = jnp.concatenate([wide, jnp.zeros((16 - ROWS, WIDTH), F32)], axis=0).astype(BF16)
    normed = layer_norm(pair.astype(F32), norm_gain[...]).astype(BF16)
    sent[:, 0, :], sent[:, 1, :] = project(normed, flat_mask(mask), w_in)


def middle_kernel(
    pair_ref, tri, norm_gain, w_in, final_gain, w_out, next_gain, next_w_in, middle, sent
):
    pair = pair_ref[:TILE].astype(F32)
    mask = flat_mask(pair_ref[TILE : TILE + 16, :].astype(F32)[:ROWS, :COLS])
    new = update(pair, sums_of(tri), norm_gain[...], w_in, final_gain[...], w_out[...])
    middle[...] = new
    normed = layer_norm(new.astype(F32), next_gain[...]).astype(BF16)
    sent[:, 0, :], sent[:, 1, :] = project(normed, mask, next_w_in)


def last_kernel(pair_ref, tri, norm_gain, w_in, final_gain, w_out, out):
    pair = pair_ref[...].astype(F32)
    out[...] = update(pair, sums_of(tri), norm_gain[...], w_in, final_gain[...], w_out[...])


def pack(sums, swapped, out):
    for zh in range(4):
        strips = []
        for x in range(4):
            at = (x * 4 + zh) * COLS
            strips.append(
                jnp.concatenate(
                    [sums[i * 32 : (i + 1) * 32, at : at + COLS] for i in range(ROWS)], axis=1
                )
            )
        for zl in range(4):
            piece = jnp.concatenate([s[zl * 8 : (zl + 1) * 8] for s in strips], axis=0)
            rest = jnp.concatenate([piece[g * 8 : (g + 1) * 8, 256:] for g in range(4)], axis=1)
            place = zl * 4 + zh if swapped else zh * 4 + zl
            out[place] = jnp.concatenate([piece[:, :128], piece[:, 128:256], rest], axis=0).astype(BF16)


def outgoing_kernel(got, senders, rows, moved, out):
    sides = [jnp.dot(senders[...], got[:, i, :], preferred_element_type=F32) for i in range(2)]

    def operand(got):
        return jnp.concatenate(
            [
                jnp.concatenate(
                    [got[x * 32 : (x + 1) * 32, i * COLS : (i + 1) * COLS] for x in range(4)],
                    axis=1,
                )
                for i in range(ROWS)
            ],
            axis=0,
        ).astype(BF16)

    left, right = operand(sides[0]), operand(sides[1])
    right = jnp.dot(rows[...], right, preferred_element_type=F32).astype(BF16)
    sums = lax.dot_general(left, right, (((1,), (1,)), ((), ())), preferred_element_type=F32)
    pack(sums, True, out)


def incoming_kernel(got, senders, rows, moved, out):
    sides = [jnp.dot(senders[...], got[:, i, :], preferred_element_type=F32) for i in range(2)]

    def operand(got):
        return jnp.concatenate(
            [
                jnp.concatenate(
                    [got[g * 8 : (g + 1) * 8, k * COLS : (k + 1) * COLS] for g in range(16)],
                    axis=1,
                )
                for k in range(ROWS)
            ],
            axis=0,
        ).astype(BF16)

    left, right = operand(sides[0]), operand(sides[1])
    left = lax.dot_general(
        rows[...], left, (((1,), (1,)), ((), ())), preferred_element_type=F32
    ).astype(BF16)
    sums = jnp.dot(left, right, preferred_element_type=F32)
    pack(sums, False, out)


def add_kernel(got, out):
    parts = []
    for zl in range(4):
        total = got[zl].astype(F32)
        for zh in range(1, 4):
            total += got[zh * 4 + zl].astype(F32)
        rest = jnp.concatenate([total[64:72, g * 32 : (g + 1) * 32] for g in range(4)], axis=0)
        parts.append(jnp.concatenate([total[:32], total[32:64], rest], axis=1))
    for i in range(2):
        out[:, i, :] = jnp.concatenate(parts[2 * i : 2 * i + 2], axis=1).astype(BF16)


def call(kernel, name, n_in, *shapes, unread=False):
    out = [jax.ShapeDtypeStruct(s, BF16) for s in shapes]
    specs = [pl.BlockSpec(memory_space=pltpu.VMEM)] * n_in
    if unread:
        specs[-1] = pl.BlockSpec(memory_space=pl.ANY)
    return pl.pallas_call(
        kernel,
        in_specs=specs,
        out_shape=out if len(out) > 1 else out[0],
        name=name,
        compiler_params=pltpu.CompilerParams(vmem_limit_bytes=32 * 1024 * 1024),
    )


def per_device(
    pair_input,
    pair_mask,
    out_norm_gain,
    out_w_in,
    out_final_gain,
    out_w_out,
    in_norm_gain,
    in_w_in,
    in_final_gain,
    in_w_out,
):
    out_norm_gain, out_final_gain, in_norm_gain, in_final_gain = (
        g.reshape(1, WIDTH) for g in (out_norm_gain, out_final_gain, in_norm_gain, in_final_gain)
    )
    by_row = np.arange(N).reshape(ROWS, 32).T.reshape(-1)
    by_place = np.arange(N).reshape(32, ROWS).T.reshape(-1)
    out_senders = jnp.asarray(one_hot(sender_order(("x", "zl", "y", "core"))), BF16)
    in_senders = jnp.asarray(one_hot(sender_order(("x", "zl", "y", "core"))), BF16)
    out_rows = jnp.asarray(one_hot(by_row), BF16)
    in_rows = jnp.asarray(one_hot(by_place), BF16)

    swap = [(zl * 4 + zh, zh * 4 + zl) for zl in range(4) for zh in range(4)]

    def spread(sent):
        return lax.all_to_all(sent, CHANNEL, 0, 0, tiled=True)

    def collect(pieces):
        got = lax.all_to_all(pieces, LINE, 0, 0, tiled=True)
        sums = call(add_kernel, "add_parts", 1, (32, 2, 2 * TILE))(got)
        return lax.all_to_all(sums, PLANE, 0, 0, tiled=True)

    pair, sent = call(
        first_kernel, "project_first", 4, (TILE + 16, WIDTH), (WIDTH, 2, TILE)
    )(pair_input.reshape(TILE, WIDTH), pair_mask, out_norm_gain, out_w_in)
    swapped_pair = lax.ppermute(pair, ("zl", "zh"), swap)
    pieces = call(outgoing_kernel, "outgoing", 4, (16, 72, 128), unread=True)(
        spread(sent), out_senders, out_rows, swapped_pair
    )
    swapped_middle, sent = call(middle_kernel, "middle", 8, (TILE, WIDTH), (WIDTH, 2, TILE))(
        swapped_pair, collect(pieces), out_norm_gain, out_w_in, out_final_gain, out_w_out, in_norm_gain, in_w_in
    )
    middle = lax.ppermute(swapped_middle, ("zl", "zh"), swap)
    pieces = call(incoming_kernel, "incoming", 4, (16, 72, 128), unread=True)(
        spread(sent), in_senders, in_rows, middle
    )
    out = call(last_kernel, "last", 6, (TILE, WIDTH))(
        middle, collect(pieces), in_norm_gain, in_w_in, in_final_gain, in_w_out
    )
    return out.reshape(ROWS, COLS, WIDTH)


def solution(mesh):
    fine = Mesh(
        mesh.devices.reshape([SIZES[a] for a in ROW + COL]), ROW + COL
    )
    placed = (P(ROW, COL, None), P(ROW, COL), P(), P(), P(), P(), P(), P(), P(), P())
    return jax.shard_map(
        per_device, mesh=fine, in_specs=placed, out_specs=P(ROW, COL, None), check_vma=False
    )
```

time: 150 us -> 151 us (level); the launches traced: 147 us -> 151 us
  blocking collectives: 80.8 us -> 92.6 us
  waiting for transfers between devices: 29.9 us -> 22.1 us
  starting transfers between devices: 18.1 us -> 23.2 us
  other arithmetic: 4.33 us -> 0 us
  local copies, waits for them, and re-layouts: 6.19 us -> 4.49 us
    all_to_all x2, waiting for transfers between devices: 29.9 us -> 22.1 us  [spread(): return lax.all_to_all(sent, CHANNEL, 0, 0, tiled=True)]
    all_to_all x2, blocking collectives: 34.4 us -> 40.5 us  [collect(): return lax.all_to_all(sums, PLANE, 0, 0, tiled=True)]
    all_to_all x2, blocking collectives: 46.4 us -> 52 us  [collect(): got = lax.all_to_all(pieces, LINE, 0, 0, tiled=True)]
    all_to_all x2, starting transfers between devices: 16.8 us -> 21.9 us  [spread(): return lax.all_to_all(sent, CHANNEL, 0, 0, tiled=True)]
    all_to_all x4 -> x0, other arithmetic: 2.7 us -> none  [the longest x2 1.37 us: spread(): return lax.all_to_all(sent, CHANNEL, 0, 0, tiled=True)]
    unnamed x32 -> x28, local copies, waits for them, and re-layouts: 5.63 us -> 4.49 us
  transfers between devices with their start and end apart: 4 -> 4, of which waited for: 2 -> 2; matrix products, arithmetic and copies ran while one was open for 1% -> 0% of each run, Pallas kernels for 0% -> 0%
where the time goes in v3:
time: 151 us
  blocking collectives  92.6 us (61%)
  starting transfers between devices  23.2 us (15%)
  waiting for transfers between devices  22.1 us (15%)
  Pallas kernels  8 us (5%)
  local copies, waits for them, and re-layouts  4.49 us (3%)
    all_to_all x2, blocking collectives, collect(): got = lax.all_to_all(pieces, LINE, 0, 0, tiled=True)  52 us
    all_to_all x2, blocking collectives, collect(): return lax.all_to_all(sums, PLANE, 0, 0, tiled=True)  40.5 us
    all_to_all x2, waiting for transfers between devices, spread(): return lax.all_to_all(sent, CHANNEL, 0, 0, tiled=True)  22.1 us
    all_to_all x2, starting transfers between devices, spread(): return lax.all_to_all(sent, CHANNEL, 0, 0, tiled=True)  21.9 us
    unnamed x28, local copies, waits for them, and re-layouts  4.49 us
  transfers between devices with their start and end apart: 4, of which 2 were waited for; matrix products, arithmetic and copies ran while one was open for 0% of the time, Pallas kernels for 0%

profile of v3, /device:TPU:1, one launch (start us, length us, event | category | flops | bytes accessed | tf_op | source)
XLA Modules:
  0.0 150.5 jit_solution(7071871584136844361)
XLA Ops:
  0.0 0.0 copy-start.10
  0.0 0.7 copy-done.10
  0.7 0.0 copy-start.1
  0.7 0.9 copy-done.1
  1.6 0.0 copy-start.6
  1.6 0.9 copy-done.6
  2.5 0.0 copy-start.9
  2.5 0.7 copy-done.9
  3.2 0.0 copy-start.4
  3.2 1.3 project_first.1
  4.4 0.0 copy-start.5
  4.4 14.0 %all-to-all-start = ((bf16[128,2,288]{2,1,0:T(2,128)(2,1)}), bf16[128,2,288]{2,1,0:T(2,128)(2,1)S(1)}, u32[]{:S(2)}, u32[]{:S(2)}) async-start(bf16[128,2,288]{2,1,0:T(2,128)(2,1)} %get-tuple-element.10), calls=%async_computation | async-start | bytes 393216 | tf_op jit(solution)/shard_map/all_to_all | solution.py:204
  18.4 0.7 collective-permute-start
  19.1 0.0 collective-permute-done.moved.pair_ref
  19.1 11.1 %all-to-all-done.got = bf16[128,2,288]{2,1,0:T(2,128)(2,1)S(1)} async-done(((bf16[128,2,288]{2,1,0:T(2,128)(2,1)}), bf16[128,2,288]{2,1,0:T(2,128)(2,1)S(1)}, u32[]{:S(2)}, u32[]{:S(2)}) %all-to-all-start) | async-done | bytes 147488 | tf_op jit(solution)/shard_map/all_to_all | solution.py:204
  30.1 0.0 copy-done.4
  30.2 0.0 copy-done.5
  30.2 1.7 %outgoing.1 = bf16[16,72,128]{2,1,0:T(8,128)(2,1)S(1)} custom-call(bf16[128,2,288]{2,1,0:T(2,128)(2,1)S(1)} %all-to-all-done.got, bf16[128,128]{1,0:T(8,128)(2,1)S(1)} %copy-done.5, bf16[384,384]{1,0:T(8,128)(2,1)S(1)} %copy-done.4, bf16[304,128]{1,0:T(8,128)(2,1)S(1)} %collective-permute-done.moved.pair_ref), custom_call_target="tpu_custom_call" | custom-call | tf_op jit(solution)/shard_map/outgoing/pallas_call | solution.py:215
  31.9 29.0 %all_to_all.30.got = bf16[16,72,128]{2,1,0:T(8,128)(2,1)S(1)} all-to-all(bf16[16,72,128]{2,1,0:T(8,128)(2,1)S(1)} %outgoing.1), channel_id=1, replica_groups=mesh['zl'=4,'y'=4,'core'=2,'x'=4,'zh'=4] {'zh','zl'}, dimensions={0} | all-to-all | bytes 589824 | tf_op jit(solution)/shard_map/all_to_all | solution.py:207
  60.9 0.0 copy-start.2
  60.9 0.0 copy-start.7
  60.9 0.2 add_parts.2
  61.1 0.0 copy-start
  61.1 20.1 %all_to_all.31.tri = bf16[32,2,576]{2,1,0:T(2,128)(2,1)S(1)} all-to-all(bf16[32,2,576]{2,1,0:T(2,128)(2,1)S(1)} %add_parts.2), channel_id=1, replica_groups=mesh['zl'=4,'y'=4,'core'=2,'x'=4,'zh'=4] {'x','y','core'}, dimensions={0} | all-to-all | bytes 147456 | tf_op jit(solution)/shard_map/all_to_all | solution.py:209
  81.3 0.0 copy-start.11
  81.3 0.0 copy-start.12
  81.3 0.0 copy-done.2
  81.3 0.0 copy-done.7
  81.3 0.0 copy-done
  81.3 0.6 copy-done.11
  81.9 0.0 copy-done.12
  81.9 1.9 %middle.1 = (bf16[288,128]{1,0:T(8,128)(2,1)S(1)}, bf16[128,2,288]{2,1,0:T(2,128)(2,1)}) custom-call(bf16[304,128]{1,0:T(8,128)(2,1)S(1)} %collective-permute-done.moved.pair_ref, bf16[32,2,576]{2,1,0:T(2,128)(2,1)S(1)} %all_to_all.31.tri, f32[1,128]{1,0:T(1,128)S(1)} %bitcast.8, bf16[128,640]{1,0:T(8,128)(2,1)S(1)} %copy-done.2, f32[1,128]{1,0:T(1,128)S(1)} %bitcast.11, ...), custom_call_target="tpu_custom_call" | custom-call | tf_op jit(solution)/shard_map/middle/pallas_call | solution.py:218
  83.8 0.0 copy-start.3
  83.8 7.9 %all-to-all-start.3 = ((bf16[128,2,288]{2,1,0:T(2,128)(2,1)}), bf16[128,2,288]{2,1,0:T(2,128)(2,1)S(1)}, u32[]{:S(2)}, u32[]{:S(2)}) async-start(bf16[128,2,288]{2,1,0:T(2,128)(2,1)} %get-tuple-element.12), calls=%async_computation.3 | async-start | bytes 393216 | tf_op jit(solution)/shard_map/all_to_all | solution.py:204
  91.8 0.7 collective-permute-start.1
  92.4 0.0 collective-permute-done.1.moved.pair_ref
  92.4 11.1 %all-to-all-done.3.got = bf16[128,2,288]{2,1,0:T(2,128)(2,1)S(1)} async-done(((bf16[128,2,288]{2,1,0:T(2,128)(2,1)}), bf16[128,2,288]{2,1,0:T(2,128)(2,1)S(1)}, u32[]{:S(2)}, u32[]{:S(2)}) %all-to-all-start.3) | async-done | bytes 147488 | tf_op jit(solution)/shard_map/all_to_all | solution.py:204
  103.5 0.0 copy-done.3
  103.5 1.6 %incoming.1 = bf16[16,72,128]{2,1,0:T(8,128)(2,1)S(1)} custom-call(bf16[128,2,288]{2,1,0:T(2,128)(2,1)S(1)} %all-to-all-done.3.got, bf16[128,128]{1,0:T(8,128)(2,1)S(1)} %copy-done.5, bf16[384,384]{1,0:T(8,128)(2,1)S(1)} %copy-done.3, bf16[288,128]{1,0:T(8,128)(2,1)S(1)} %collective-permute-done.1.moved.pair_ref), custom_call_target="tpu_custom_call" | custom-call | tf_op jit(solution)/shard_map/incoming/pallas_call | solution.py:222
  105.1 23.0 %all_to_all.32.got = bf16[16,72,128]{2,1,0:T(8,128)(2,1)S(1)} all-to-all(bf16[16,72,128]{2,1,0:T(8,128)(2,1)S(1)} %incoming.1), channel_id=1, replica_groups=mesh['zl'=4,'y'=4,'core'=2,'x'=4,'zh'=4] {'zh','zl'}, dimensions={0} | all-to-all | bytes 589824 | tf_op jit(solution)/shard_map/all_to_all | solution.py:207
  128.1 0.2 add_parts.3
  128.3 0.0 copy-start.8
  128.3 20.4 %all_to_all.33.tri = bf16[32,2,576]{2,1,0:T(2,128)(2,1)S(1)} all-to-all(bf16[32,2,576]{2,1,0:T(2,128)(2,1)S(1)} %add_parts.3), channel_id=1, replica_groups=mesh['zl'=4,'y'=4,'core'=2,'x'=4,'zh'=4] {'x','y','core'}, dimensions={0} | all-to-all | bytes 147456 | tf_op jit(solution)/shard_map/all_to_all | solution.py:209
  148.7 0.0 copy-start.13
  148.7 0.0 copy-done.8
  148.7 0.7 copy-done.13
  149.3 1.2 last.1
Async XLA Ops:
  0.0 0.7 copy-start.10
  0.7 0.9 copy-start.1
  1.6 0.9 copy-start.6
  2.5 0.7 copy-start.9
  3.2 27.0 %copy-start.4 = (bf16[384,384]{1,0:T(8,128)(2,1)S(1)}, bf16[384,384]{1,0:T(8,128)(2,1)}, u32[]{:S(2)}) copy-start(bf16[384,384]{1,0:T(8,128)(2,1)} %constant.7.clone.rows) | copy-start | bytes 884740
  4.4 25.7 %copy-start.5 = (bf16[128,128]{1,0:T(8,128)(2,1)S(1)}, bf16[128,128]{1,0:T(8,128)(2,1)}, u32[]{:S(2)}) copy-start(bf16[128,128]{1,0:T(8,128)(2,1)} %constant.6.clone.senders) | copy-start | bytes 98308
  4.4 25.7 %all-to-all-start = ((bf16[128,2,288]{2,1,0:T(2,128)(2,1)}), bf16[128,2,288]{2,1,0:T(2,128)(2,1)S(1)}, u32[]{:S(2)}, u32[]{:S(2)}) async-start(bf16[128,2,288]{2,1,0:T(2,128)(2,1)} %get-tuple-element.10), calls=%async_computation | async-start | bytes 393216 | tf_op jit(solution)/shard_map/all_to_all | solution.py:204
  18.4 0.7 collective-permute-start
  60.9 20.4 %copy-start.2 = (bf16[128,640]{1,0:T(8,128)(2,1)S(1)}, bf16[128,640]{1,0:T(8,128)(2,1)}, u32[]{:S(2)}) copy-start(bf16[128,640]{1,0:T(8,128)(2,1)} %w_in.4) | copy-start | bytes 491524
  60.9 20.4 %copy-start.7 = (bf16[128,128]{1,0:T(8,128)(2,1)S(1)}, bf16[128,128]{1,0:T(8,128)(2,1)}, u32[]{:S(2)}) copy-start(bf16[128,128]{1,0:T(8,128)(2,1)} %w_out.2) | copy-start | bytes 98308
  61.1 20.2 %copy-start = (bf16[128,640]{1,0:T(8,128)(2,1)S(1)}, bf16[128,640]{1,0:T(8,128)(2,1)}, u32[]{:S(2)}) copy-start(bf16[128,640]{1,0:T(8,128)(2,1)} %w_in.5) | copy-start | bytes 491524
  81.3 0.7 copy-start.11
  81.3 0.7 copy-start.12
  83.8 19.7 %copy-start.3 = (bf16[384,384]{1,0:T(8,128)(2,1)S(1)}, bf16[384,384]{1,0:T(8,128)(2,1)}, u32[]{:S(2)}) copy-start(bf16[384,384]{1,0:T(8,128)(2,1)} %constant.8.clone.rows) | copy-start | bytes 884740
  83.8 19.7 %all-to-all-start.3 = ((bf16[128,2,288]{2,1,0:T(2,128)(2,1)}), bf16[128,2,288]{2,1,0:T(2,128)(2,1)S(1)}, u32[]{:S(2)}, u32[]{:S(2)}) async-start(bf16[128,2,288]{2,1,0:T(2,128)(2,1)} %get-tuple-element.12), calls=%async_computation.3 | async-start | bytes 393216 | tf_op jit(solution)/shard_map/all_to_all | solution.py:204
  91.8 0.7 collective-permute-start.1
  128.3 20.4 %copy-start.8 = (bf16[128,128]{1,0:T(8,128)(2,1)S(1)}, bf16[128,128]{1,0:T(8,128)(2,1)}, u32[]{:S(2)}) copy-start(bf16[128,128]{1,0:T(8,128)(2,1)} %w_out.3) | copy-start | bytes 98308
  148.7 0.7 copy-start.13

commit v4 on v1

v4 whole, which is shorter than its diff:
```python
import jax
import jax.numpy as jnp
import numpy as np
from jax import lax
from jax.experimental import pallas as pl
from jax.experimental.pallas import tpu as pltpu
from jax.sharding import Mesh
from jax.sharding import PartitionSpec as P

ROW = ("zl", "y", "core")
COL = ("x", "zh")
SIZES = {"zl": 4, "y": 4, "core": 2, "x": 4, "zh": 4}
OUT_CHANNEL = ("zl", "x", "y", "core")
IN_CHANNEL = ("x", "y", "zl", "core")
LINE = ("zl", "zh")
PLANE = ("x", "y", "core")

ROWS, COLS, WIDTH = 12, 24, 128
TILE = ROWS * COLS
N = 384
F32, BF16 = jnp.float32, jnp.bfloat16


def one_hot(places):
    table = np.zeros((len(places), len(places)), np.float32)
    table[np.arange(len(places)), places] = 1
    return table


def sender_order(names):
    index = np.arange(128).reshape([SIZES[a] for a in OUT_CHANNEL])
    return index.transpose([OUT_CHANNEL.index(a) for a in names]).reshape(-1)


def layer_norm(values, gain):
    center = values - jnp.mean(values, axis=-1, keepdims=True)
    spread = jnp.mean(center * center, axis=-1, keepdims=True)
    return center * lax.rsqrt(spread + 1e-05) * gain


def flat_mask(mask):
    return jnp.concatenate([mask[i : i + 1] for i in range(ROWS)], axis=1)


def project(normed, mask, w_in):
    proj = lax.dot_general(
        w_in[:, : 4 * WIDTH], normed, (((0,), (1,)), ((), ())), preferred_element_type=F32
    )
    left = proj[:WIDTH] * jax.nn.sigmoid(proj[2 * WIDTH : 3 * WIDTH]) * mask
    right = proj[WIDTH : 2 * WIDTH] * jax.nn.sigmoid(proj[3 * WIDTH : 4 * WIDTH]) * mask
    return left.astype(BF16), right.astype(BF16)


def update(pair, tri, norm_gain, w_in, final_gain, w_out):
    final = layer_norm(tri.T, final_gain).astype(BF16)
    normed = layer_norm(pair, norm_gain).astype(BF16)
    gate = jax.nn.sigmoid(jnp.dot(normed, w_in[:, 4 * WIDTH :], preferred_element_type=F32))
    return (pair + jnp.dot(final, w_out, preferred_element_type=F32) * gate).astype(BF16)


def sums_of(tri):
    rows = [tri[:, i, :].astype(F32) for i in range(2)]
    return jnp.concatenate([r[:, i * TILE : (i + 1) * TILE] for r in rows for i in range(2)], axis=0)


def first_kernel(pair_ref, mask_ref, g0, g1, g2, g3, w_in, sent, gains, pair, mask, weights, sems):
    copies = [
        pltpu.make_async_copy(pair_ref, pair, sems.at[0]),
        pltpu.make_async_copy(mask_ref, mask, sems.at[1]),
        pltpu.make_async_copy(w_in.at[:, pl.ds(0, 4 * WIDTH)], weights, sems.at[2]),
    ]
    for i, gain in enumerate((g0, g1, g2, g3)):
        copies.append(pltpu.make_async_copy(gain, gains.at[pl.ds(i, 1)], sems.at[3 + i]))
    for copy in copies:
        copy.start()
    for copy in copies:
        copy.wait()
    normed = layer_norm(pair[...].astype(F32), gains[0:1]).astype(BF16)
    sent[:, 0, :], sent[:, 1, :] = project(normed, flat_mask(mask[...].astype(F32)), weights[...])


def middle_kernel(pair_ref, mask, tri, gains, w_in, w_out, next_w_in, middle, sent):
    pair = pair_ref[...].astype(F32)
    new = update(pair, sums_of(tri), gains[0:1], w_in, gains[1:2], w_out[...])
    middle[...] = new
    normed = layer_norm(new.astype(F32), gains[2:3]).astype(BF16)
    sent[:, 0, :], sent[:, 1, :] = project(normed, flat_mask(mask[...].astype(F32)), next_w_in)


def last_kernel(pair_ref, tri, gains, w_in, w_out, out):
    pair = pair_ref[...].astype(F32)
    sums = jnp.concatenate([tri[:, half, :].astype(F32) for half in range(2)], axis=1)
    out[...] = update(pair, sums, gains[2:3], w_in, gains[3:4], w_out[...])


def pack(sums, out):
    for zh in range(4):
        strips = []
        for x in range(4):
            at = (x * 4 + zh) * COLS
            strips.append(
                jnp.concatenate(
                    [sums[i * 32 : (i + 1) * 32, at : at + COLS] for i in range(ROWS)], axis=1
                )
            )
        for zl in range(4):
            piece = jnp.concatenate([s[zl * 8 : (zl + 1) * 8] for s in strips], axis=0)
            rest = jnp.concatenate([piece[g * 8 : (g + 1) * 8, 256:] for g in range(4)], axis=1)
            out[zl * 4 + zh] = jnp.concatenate([piece[:, :128], piece[:, 128:256], rest], axis=0).astype(BF16)


def outgoing_kernel(got, senders, rows, out):
    sides = [jnp.dot(senders[...], got[:, i, :], preferred_element_type=F32) for i in range(2)]

    def operand(got):
        return jnp.concatenate(
            [
                jnp.concatenate(
                    [got[x * 32 : (x + 1) * 32, i * COLS : (i + 1) * COLS] for x in range(4)],
                    axis=1,
                )
                for i in range(ROWS)
            ],
            axis=0,
        ).astype(BF16)

    left, right = operand(sides[0]), operand(sides[1])
    right = jnp.dot(rows[...], right, preferred_element_type=F32).astype(BF16)
    sums = lax.dot_general(left, right, (((1,), (1,)), ((), ())), preferred_element_type=F32)
    pack(sums, out)


def split_kernel(got, left):
    side = got[:, 0, :].astype(F32)
    rest = jnp.concatenate([side[g * 32 : (g + 1) * 32, 256:] for g in range(4)], axis=1)
    left[...] = jnp.concatenate([side[:, :128], side[:, 128:256], rest], axis=0).astype(BF16)


def incoming_kernel(got, lefts, rows, out):
    def operand(side):
        return jnp.concatenate(
            [
                jnp.concatenate(
                    [side[x * 32 : (x + 1) * 32, k * COLS : (k + 1) * COLS] for x in range(4)], axis=1
                )
                for k in range(ROWS)
            ],
            axis=0,
        ).astype(BF16)

    right = operand(got[:, 1, :].astype(F32))
    for zh in range(4):
        left = lefts[zh].astype(F32)
        rest = jnp.concatenate([left[256:, g * 32 : (g + 1) * 32] for g in range(4)], axis=0)
        left = operand(jnp.concatenate([left[:128], left[128:256], rest], axis=1))
        left = lax.dot_general(
            rows[...], left, (((1,), (1,)), ((), ())), preferred_element_type=F32
        ).astype(BF16)
        sums = jnp.dot(left, right, preferred_element_type=F32)
        for x in range(4):
            piece = [sums[i * 8 : (i + 1) * 8, x * COLS : (x + 1) * COLS] for i in range(ROWS)]
            at = x * 32 + zh * 8
            for half in range(2):
                part = jnp.concatenate(piece[half * 6 : half * 6 + 6], axis=1)
                out[at : at + 8, half, :] = part.astype(BF16)


def add_kernel(got, out):
    parts = []
    for zl in range(4):
        total = got[zl * 4].astype(F32)
        for zh in range(1, 4):
            total += got[zl * 4 + zh].astype(F32)
        rest = jnp.concatenate([total[64:72, g * 32 : (g + 1) * 32] for g in range(4)], axis=0)
        parts.append(jnp.concatenate([total[:32], total[32:64], rest], axis=1))
    for i in range(2):
        out[:, i, :] = jnp.concatenate(parts[2 * i : 2 * i + 2], axis=1).astype(BF16)


def call(kernel, name, *shapes):
    out = [jax.ShapeDtypeStruct(s, BF16) for s in shapes]
    return pl.pallas_call(
        kernel,
        out_shape=out if len(out) > 1 else out[0],
        name=name,
        compiler_params=pltpu.CompilerParams(vmem_limit_bytes=32 * 1024 * 1024),
    )


def call_first(*operands):
    return pl.pallas_call(
        first_kernel,
        in_specs=[pl.BlockSpec(memory_space=pltpu.HBM)] * len(operands),
        out_shape=[
            jax.ShapeDtypeStruct((WIDTH, 2, TILE), BF16),
            jax.ShapeDtypeStruct((4, WIDTH), F32),
        ],
        scratch_shapes=[
            pltpu.VMEM((TILE, WIDTH), BF16),
            pltpu.VMEM((ROWS, COLS), jnp.int32),
            pltpu.VMEM((WIDTH, 4 * WIDTH), BF16),
            pltpu.SemaphoreType.DMA((7,)),
        ],
        name="project_first",
        compiler_params=pltpu.CompilerParams(vmem_limit_bytes=60 * 1024 * 1024),
    )(*operands)


def gather_lefts(left):
    return lax.all_gather(left, "zh")


def per_device(
    pair_input,
    pair_mask,
    out_norm_gain,
    out_w_in,
    out_final_gain,
    out_w_out,
    in_norm_gain,
    in_w_in,
    in_final_gain,
    in_w_out,
):
    out_norm_gain, out_final_gain, in_norm_gain, in_final_gain = (
        g.reshape(1, WIDTH) for g in (out_norm_gain, out_final_gain, in_norm_gain, in_final_gain)
    )
    by_row = np.arange(N).reshape(ROWS, 32).T.reshape(-1)
    by_place = np.arange(96).reshape(8, ROWS).T.reshape(-1)
    out_senders = jnp.asarray(one_hot(sender_order(("x", "zl", "y", "core"))), BF16)
    out_rows = jnp.asarray(one_hot(by_row), BF16)
    in_rows = jnp.asarray(one_hot(by_place), BF16)

    pair = pair_input.reshape(TILE, WIDTH)
    sent, gains = call_first(
        pair,
        pair_mask,
        out_norm_gain,
        out_final_gain,
        in_norm_gain,
        in_final_gain,
        out_w_in,
    )
    got = lax.all_to_all(sent, OUT_CHANNEL, 0, 0, tiled=True)
    pieces = call(outgoing_kernel, "outgoing", (16, 72, 128))(got, out_senders, out_rows)
    got = lax.all_to_all(pieces, LINE, 0, 0, tiled=True)
    sums = call(add_kernel, "add_parts", (32, 2, 2 * TILE))(got)
    tri = lax.all_to_all(sums, PLANE, 0, 0, tiled=True)

    middle, sent = call(middle_kernel, "middle", (TILE, WIDTH), (WIDTH, 2, TILE))(
        pair, pair_mask, tri, gains, out_w_in, out_w_out, in_w_in
    )
    got = lax.all_to_all(sent, IN_CHANNEL, 0, 0, tiled=True)
    left = call(split_kernel, "split", (TILE, WIDTH))(got)
    lefts = gather_lefts(left)
    sums = call(incoming_kernel, "incoming", (WIDTH, 2, TILE // 2))(got, lefts, in_rows)
    tri = lax.all_to_all(sums, IN_CHANNEL, 0, 0, tiled=True)
    out = call(last_kernel, "last", (TILE, WIDTH))(middle, tri, gains, in_w_in, in_w_out)
    return out.reshape(ROWS, COLS, WIDTH)


def solution(mesh):
    fine = Mesh(
        mesh.devices.reshape([SIZES[a] for a in ROW + COL]), ROW + COL
    )
    placed = (P(ROW, COL, None), P(ROW, COL), P(), P(), P(), P(), P(), P(), P(), P())
    return jax.shard_map(
        per_device, mesh=fine, in_specs=placed, out_specs=P(ROW, COL, None), check_vma=False
    )
```

time: 150 us -> 136 us (0.907); the launches traced: 147 us -> 136 us
  blocking collectives: 80.8 us -> 127 us
  waiting for transfers between devices: 29.9 us -> 0 us
  starting transfers between devices: 18.1 us -> 0 us
  local copies, waits for them, and re-layouts: 6.19 us -> 0.05 us
  other arithmetic: 4.33 us -> 0 us
    all_to_all x2 -> x0, waiting for transfers between devices: 29.9 us -> none  [collect(): got = lax.all_to_all(pieces, LINE, 0, 0, tiled=True)]
    all_to_all x4 -> x5, blocking collectives: 80.8 us -> 109 us  [the longest x1 27.6 us: per_device(): got = lax.all_to_all(pieces, LINE, 0, 0, tiled=True)]
    all_gather x0 -> x1, blocking collectives: none -> 18 us  [gather_lefts(): return lax.all_gather(left, 'zh')]
    all_to_all x2 -> x0, starting transfers between devices: 16.8 us -> none  [collect(): got = lax.all_to_all(pieces, LINE, 0, 0, tiled=True)]
    unnamed x32 -> x20, local copies, waits for them, and re-layouts: 5.63 us -> 0.05 us
    all_to_all x4 -> x0, other arithmetic: 2.7 us -> none  [the longest x2 1.37 us: spread(): return lax.all_to_all(sent, CHANNEL, 0, 0, tiled=True)]
  transfers between devices with their start and end apart: 4 -> 0, of which waited for: 2 -> 0; matrix products, arithmetic and copies ran while one was open for 1% -> 0% of each run, Pallas kernels for 0% -> 0%
where the time goes in v4:
time: 136 us
  blocking collectives  127 us (93%)
  Pallas kernels  8.3 us (6%)
    all_to_all x1, blocking collectives, per_device(): got = lax.all_to_all(pieces, LINE, 0, 0, tiled=True)  27.6 us
    all_to_all x1, blocking collectives, per_device(): got = lax.all_to_all(sent, OUT_CHANNEL, 0, 0, tiled=True)  25.6 us
    all_to_all x1, blocking collectives, per_device(): got = lax.all_to_all(sent, IN_CHANNEL, 0, 0, tiled=True)  21.8 us
    all_to_all x1, blocking collectives, per_device(): tri = lax.all_to_all(sums, IN_CHANNEL, 0, 0, tiled=True)  19.5 us
    all_gather x1, blocking collectives, gather_lefts(): return lax.all_gather(left, 'zh')  18 us
    all_to_all x1, blocking collectives, per_device(): tri = lax.all_to_all(sums, PLANE, 0, 0, tiled=True)  14.7 us

profile of v4, /device:TPU:1, one launch (start us, length us, event | category | flops | bytes accessed | tf_op | source)
XLA Modules:
  0.0 135.7 jit_solution(7253729022627998053)
XLA Ops:
  0.0 0.0 copy-start.2
  0.0 2.4 %project_first.1 = (bf16[128,2,288]{2,1,0:T(2,128)(2,1)}, f32[4,128]{1,0:T(4,128)}) custom-call(bf16[288,128]{1,0:T(8,128)(2,1)} %bitcast.8, s32[12,24]{1,0:T(8,128)} %mask.1, f32[1,128]{1,0:T(1,128)} %bitcast.10, f32[1,128]{1,0:T(1,128)} %bitcast.11, f32[1,128]{1,0:T(1,128)} %bitcast.12, f32[1,128]{1,0:T(1,128)} %bitcast.13, bf16[128,640]{1,0:T(8,128)(2,1)} %w_in.4), custom_call_target="tpu_custom_call" | custom-call | tf_op jit(solution)/shard_map/project_first/pallas_call | solution.py:191
  2.4 0.0 copy-start.6
  2.4 25.6 %all_to_all.25.got = bf16[128,2,288]{2,1,0:T(2,128)(2,1)S(1)} all-to-all(bf16[128,2,288]{2,1,0:T(2,128)(2,1)} %get-tuple-element.9), channel_id=1, replica_groups=mesh['zl'=4,'y'=4,'core'=2,'x'=4,'zh'=4] {'zl','x','y','core'}, dimensions={0} | all-to-all | bytes 294912 | tf_op jit(solution)/shard_map/all_to_all | solution.py:244
  28.0 0.0 copy-done.2
  28.0 0.0 copy-done.6
  28.0 1.7 %outgoing.1 = bf16[16,72,128]{2,1,0:T(8,128)(2,1)S(1)} custom-call(bf16[128,2,288]{2,1,0:T(2,128)(2,1)S(1)} %all_to_all.25.got, bf16[128,128]{1,0:T(8,128)(2,1)S(1)} %copy-done.6, bf16[384,384]{1,0:T(8,128)(2,1)S(1)} %copy-done.2), custom_call_target="tpu_custom_call" | custom-call | tf_op jit(solution)/shard_map/outgoing/pallas_call | solution.py:245
  29.7 27.6 %all_to_all.26.got = bf16[16,72,128]{2,1,0:T(8,128)(2,1)S(1)} all-to-all(bf16[16,72,128]{2,1,0:T(8,128)(2,1)S(1)} %outgoing.1), channel_id=1, replica_groups=mesh['zl'=4,'y'=4,'core'=2,'x'=4,'zh'=4] {'zl','zh'}, dimensions={0} | all-to-all | bytes 589824 | tf_op jit(solution)/shard_map/all_to_all | solution.py:246
  57.3 0.0 copy-start.1
  57.3 0.0 copy-start.3
  57.3 0.0 copy-start.4
  57.3 0.0 copy-start.5
  57.3 0.0 copy-start.9
  57.4 0.2 add_parts.1
  57.5 0.0 copy-start
  57.6 14.7 %all_to_all.27.tri = bf16[32,2,576]{2,1,0:T(2,128)(2,1)S(1)} all-to-all(bf16[32,2,576]{2,1,0:T(2,128)(2,1)S(1)} %add_parts.1), channel_id=1, replica_groups=mesh['zl'=4,'y'=4,'core'=2,'x'=4,'zh'=4] {'x','y','core'}, dimensions={0} | all-to-all | bytes 147456 | tf_op jit(solution)/shard_map/all_to_all | solution.py:248
  72.3 0.0 copy-done.1
  72.3 0.0 copy-done.3
  72.3 0.0 copy-done.4
  72.3 0.0 copy-done.5
  72.3 0.0 copy-done.9
  72.3 0.0 copy-done
  72.3 1.2 middle.1
  73.6 21.8 %all_to_all.28.got = bf16[128,2,288]{2,1,0:T(2,128)(2,1)S(1)} all-to-all(bf16[128,2,288]{2,1,0:T(2,128)(2,1)S(1)} %get-tuple-element.12), channel_id=1, replica_groups=mesh['zl'=4,'y'=4,'core'=2,'x'=4,'zh'=4] {'x','y','zl','core'}, dimensions={0} | all-to-all | bytes 294912 | tf_op jit(solution)/shard_map/all_to_all | solution.py:253
  95.4 0.1 split.1
  95.5 0.0 copy-start.8
  95.5 18.0 %all-gather = bf16[1152,128]{1,0:T(8,128)(2,1)S(1)} all-gather(bf16[288,128]{1,0:T(8,128)(2,1)S(1)} %split.1), channel_id=2, replica_groups=mesh['zl'=4,'y'=4,'core'=2,'x'=4,'zh'=4] {'zh'}, dimensions={0}, use_global_device_ids=true | all-gather | bytes 368640 | tf_op jit(solution)/shard_map/all_gather | solution.py:210
  113.5 0.0 copy-done.8
  113.5 1.4 %incoming.1 = bf16[128,2,144]{2,1,0:T(2,128)(2,1)S(1)} custom-call(bf16[128,2,288]{2,1,0:T(2,128)(2,1)S(1)} %all_to_all.28.got, bf16[4,288,128]{2,1,0:T(8,128)(2,1)S(1)} %bitcast.7, bf16[96,96]{1,0:T(8,128)(2,1)S(1)} %copy-done.8), custom_call_target="tpu_custom_call" | custom-call | tf_op jit(solution)/shard_map/incoming/pallas_call | solution.py:256
  115.0 0.0 copy-start.7
  115.0 19.5 %all_to_all.29.tri = bf16[128,2,144]{2,1,0:T(2,128)(2,1)S(1)} all-to-all(bf16[128,2,144]{2,1,0:T(2,128)(2,1)S(1)} %incoming.1), channel_id=1, replica_groups=mesh['zl'=4,'y'=4,'core'=2,'x'=4,'zh'=4] {'x','y','zl','core'}, dimensions={0} | all-to-all | bytes 147456 | tf_op jit(solution)/shard_map/all_to_all | solution.py:257
  134.5 0.0 copy-done.7
  134.5 1.3 last.1
Async XLA Ops:
  0.0 28.0 %copy-start.2 = (bf16[384,384]{1,0:T(8,128)(2,1)S(1)}, bf16[384,384]{1,0:T(8,128)(2,1)}, u32[]{:S(2)}) copy-start(bf16[384,384]{1,0:T(8,128)(2,1)} %constant.7.clone.rows) | copy-start | bytes 884740
  2.4 25.6 %copy-start.6 = (bf16[128,128]{1,0:T(8,128)(2,1)S(1)}, bf16[128,128]{1,0:T(8,128)(2,1)}, u32[]{:S(2)}) copy-start(bf16[128,128]{1,0:T(8,128)(2,1)} %constant.6.clone.senders) | copy-start | bytes 98308
  57.3 15.0 %copy-start.1 = (bf16[128,640]{1,0:T(8,128)(2,1)S(1)}, bf16[128,640]{1,0:T(8,128)(2,1)}, u32[]{:S(2)}) copy-start(bf16[128,640]{1,0:T(8,128)(2,1)} %w_in.5) | copy-start | bytes 491524
  57.3 15.0 %copy-start.3 = (bf16[12,24,128]{2,1,0:T(8,128)(2,1)S(1)}, bf16[12,24,128]{2,1,0:T(8,128)(2,1)}, u32[]{:S(2)}) copy-start(bf16[12,24,128]{2,1,0:T(8,128)(2,1)} %param.13) | copy-start | bytes 221188
  57.3 15.0 %copy-start.4 = (s32[12,24]{1,0:T(8,128)S(1)}, s32[12,24]{1,0:T(8,128)}, u32[]{:S(2)}) copy-start(s32[12,24]{1,0:T(8,128)} %mask.1) | copy-start | bytes 3460
  57.3 15.0 %copy-start.5 = (bf16[128,128]{1,0:T(8,128)(2,1)S(1)}, bf16[128,128]{1,0:T(8,128)(2,1)}, u32[]{:S(2)}) copy-start(bf16[128,128]{1,0:T(8,128)(2,1)} %w_out.2) | copy-start | bytes 98308
  57.3 15.0 %copy-start.9 = (f32[4,128]{1,0:T(4,128)S(1)}, f32[4,128]{1,0:T(4,128)}, u32[]{:S(2)}) copy-start(f32[4,128]{1,0:T(4,128)} %get-tuple-element.10.gains) | copy-start | bytes 6148
  57.5 14.8 %copy-start = (bf16[128,640]{1,0:T(8,128)(2,1)S(1)}, bf16[128,640]{1,0:T(8,128)(2,1)}, u32[]{:S(2)}) copy-start(bf16[128,640]{1,0:T(8,128)(2,1)} %w_in.4) | copy-start | bytes 491524
  95.5 18.1 %copy-start.8 = (bf16[96,96]{1,0:T(8,128)(2,1)S(1)}, bf16[96,96]{1,0:T(8,128)(2,1)}, u32[]{:S(2)}) copy-start(bf16[96,96]{1,0:T(8,128)(2,1)} %constant.8.clone.rows) | copy-start | bytes 55300
  115.0 19.5 %copy-start.7 = (bf16[128,128]{1,0:T(8,128)(2,1)S(1)}, bf16[128,128]{1,0:T(8,128)(2,1)}, u32[]{:S(2)}) copy-start(bf16[128,128]{1,0:T(8,128)(2,1)} %w_out.3) | copy-start | bytes 98308

commit v5 on v4

v5 whole, which is shorter than its diff:
```python
import jax
import jax.numpy as jnp
import ml_dtypes
import numpy as np
from jax import lax
from jax.experimental import pallas as pl
from jax.experimental.pallas import tpu as pltpu
from jax.sharding import Mesh
from jax.sharding import PartitionSpec as P

ROW = ("zl", "y", "core")
COL = ("x", "zh")
SIZES = {"zl": 4, "y": 4, "core": 2, "x": 4, "zh": 4}
OUT_CHANNEL = ("zl", "x", "y")
IN_CHANNEL = ("x", "y", "zl")
LINE = ("zl", "zh")
PLANE = ("x", "y")

ROWS, COLS, WIDTH = 12, 24, 128
TILE = ROWS * COLS
PAIRS = WIDTH // 2
N = 384
F32, BF16 = jnp.float32, jnp.bfloat16


def one_hot(places, width=None):
    places = np.asarray(places).reshape(-1)
    table = np.zeros((len(places), width or len(places)), np.float32)
    table[np.arange(len(places))[places >= 0], places[places >= 0]] = 1
    return table.astype(ml_dtypes.bfloat16)


def reorder(sizes, order):
    return np.arange(np.prod(sizes)).reshape(sizes).transpose(order)


def layer_norm(values, gain):
    center = values - jnp.mean(values, axis=-1, keepdims=True)
    spread = jnp.mean(center * center, axis=-1, keepdims=True)
    return center * lax.rsqrt(spread + 1e-05) * gain


def flat_mask(mask):
    return jnp.concatenate([mask[i : i + 1] for i in range(ROWS)], axis=1)


def project(normed, mask, w_in):
    proj = lax.dot_general(
        w_in[:, : 4 * WIDTH], normed, (((0,), (1,)), ((), ())), preferred_element_type=F32
    )
    left = proj[:WIDTH] * jax.nn.sigmoid(proj[2 * WIDTH : 3 * WIDTH]) * mask
    right = proj[WIDTH : 2 * WIDTH] * jax.nn.sigmoid(proj[3 * WIDTH : 4 * WIDTH]) * mask
    return [jnp.concatenate([v[:PAIRS], v[PAIRS:]], axis=1).astype(BF16) for v in (left, right)]


def update(pair, tri, norm_gain, w_in, final_gain, w_out):
    final = layer_norm(tri.T, final_gain).astype(BF16)
    normed = layer_norm(pair, norm_gain).astype(BF16)
    gate = jax.nn.sigmoid(jnp.dot(normed, w_in[:, 4 * WIDTH :], preferred_element_type=F32))
    return (pair + jnp.dot(final, w_out, preferred_element_type=F32) * gate).astype(BF16)


def sums_of(tri):
    pair = [tri[:, i, :].astype(F32) for i in range(2)]
    return jnp.concatenate([v[:, zl * TILE : (zl + 1) * TILE] for v in pair for zl in range(4)], axis=0)


def first_kernel(pair_ref, mask_ref, g0, g1, g2, g3, w_in, sent, gains, pair, mask, weights, sems):
    copies = [
        pltpu.make_async_copy(pair_ref, pair, sems.at[0]),
        pltpu.make_async_copy(mask_ref, mask, sems.at[1]),
        pltpu.make_async_copy(w_in.at[:, pl.ds(0, 4 * WIDTH)], weights, sems.at[2]),
    ]
    for i, gain in enumerate((g0, g1, g2, g3)):
        copies.append(pltpu.make_async_copy(gain, gains.at[pl.ds(i, 1)], sems.at[3 + i]))
    for copy in copies:
        copy.start()
    for copy in copies:
        copy.wait()
    normed = layer_norm(pair[...].astype(F32), gains[0:1]).astype(BF16)
    sent[:, 0, :], sent[:, 1, :] = project(normed, flat_mask(mask[...].astype(F32)), weights[...])


def middle_kernel(pair_ref, mask, tri, gains, w_in, w_out, next_w_in, middle, sent):
    pair = pair_ref[...].astype(F32)
    new = update(pair, sums_of(tri), gains[0:1], w_in, gains[1:2], w_out[...])
    middle[...] = new
    normed = layer_norm(new.astype(F32), gains[2:3]).astype(BF16)
    sent[:, 0, :], sent[:, 1, :] = project(normed, flat_mask(mask[...].astype(F32)), next_w_in)


def last_kernel(pair_ref, tri, gains, w_in, w_out, out):
    pair = pair_ref[...].astype(F32)
    sums = jnp.concatenate([tri[:, i, :].astype(F32) for i in range(2)], axis=0)
    out[...] = update(pair, sums, gains[2:3], w_in, gains[3:4], w_out[...])


def chunks(side, wide):
    return jnp.concatenate(
        [
            jnp.concatenate([side[x * 32 : (x + 1) * 32, i * wide : (i + 1) * wide] for x in range(4)], axis=1)
            for i in range(ROWS)
        ],
        axis=0,
    )


def fold(strip):
    n = strip.shape[0] // 4
    rest = jnp.concatenate([strip[g * n : (g + 1) * n, 256:] for g in range(4)], axis=1)
    return jnp.concatenate([strip[:, :128], strip[:, 128:256], rest], axis=0)


def unfold(folded):
    n = folded.shape[0] // 9
    rest = jnp.concatenate([folded[8 * n :, g * 32 : (g + 1) * 32] for g in range(4)], axis=0)
    return jnp.concatenate([folded[: 4 * n], folded[4 * n : 8 * n], rest], axis=1)


def outgoing_kernel(core, own, both, left_order, right_order, rows, out):
    left = own[:, 0, :].astype(F32)
    left = jnp.concatenate([left[:, :TILE], left[:, TILE:]], axis=0).astype(BF16)
    left = chunks(jnp.dot(left_order[...], left, preferred_element_type=F32), COLS)
    first = lax.broadcasted_iota(jnp.int32, left.shape, 0) % 8 < 4
    left = jnp.concatenate([jnp.where(first, left, 0.0), jnp.where(first, 0.0, left)], axis=1).astype(BF16)
    right = jnp.dot(right_order[...], both[:, 1, :], preferred_element_type=F32)
    right = jnp.concatenate([chunks(right[:, :TILE], COLS), chunks(right[:, TILE:], COLS)], axis=1)
    right = jnp.dot(rows[...], right.astype(BF16), preferred_element_type=F32).astype(BF16)
    sums = lax.dot_general(left, right, (((1,), (1,)), ((), ())), preferred_element_type=F32)
    for zh in range(4):
        strips = []
        for x in range(4):
            at = (x * 4 + zh) * COLS
            strips.append(
                jnp.concatenate([sums[i * 32 : (i + 1) * 32, at : at + COLS] for i in range(ROWS)], axis=1)
            )
        for zl in range(4):
            piece = jnp.concatenate([s[zl * 8 : (zl + 1) * 8] for s in strips], axis=0)
            out[zl * 4 + zh] = fold(piece).astype(BF16)


def add_kernel(got, order, out):
    parts = []
    for zl in range(4):
        total = got[zl * 4].astype(F32)
        for zh in range(1, 4):
            total += got[zl * 4 + zh].astype(F32)
        parts.append(unfold(total))
    total = jnp.concatenate(parts, axis=1).astype(BF16)
    total = jnp.dot(order[...], total, preferred_element_type=F32).astype(BF16)
    for i in range(2):
        out[:, i, :] = total[i * 16 : (i + 1) * 16]


def by_x(side):
    return jnp.concatenate(
        [side[c * PAIRS + x * 16 : c * PAIRS + (x + 1) * 16] for x in range(4) for c in range(2)], axis=0
    )


def split_kernel(core, both, halves, rows, left):
    side = by_x(jnp.dot(both[:, 0, :], halves[core[0]], preferred_element_type=F32))
    terms = [
        lax.dot_general(
            rows[i],
            chunks(side[:, i * TILE // 2 : (i + 1) * TILE // 2], COLS // 2).astype(BF16),
            (((1,), (1,)), ((), ())),
            preferred_element_type=F32,
        )
        for i in range(2)
    ]
    left[...] = (terms[0] + terms[1]).astype(BF16)


def incoming_kernel(both, lefts, out):
    right = by_x(both[:, 1, :].astype(F32))
    right = jnp.concatenate([chunks(right[:, :TILE], COLS), chunks(right[:, TILE:], COLS)], axis=1)
    sums = jnp.dot(lefts[...], right.astype(BF16), preferred_element_type=F32)
    first = lax.broadcasted_iota(jnp.int32, (N, 4 * COLS), 0) % 8 < 4
    sums = jnp.where(first, sums[:, : 4 * COLS], sums[:, 4 * COLS :])
    for zh in range(4):
        for x in range(4):
            piece = jnp.concatenate(
                [
                    sums[zh * 96 + i * 8 : zh * 96 + (i + 1) * 8, x * COLS : (x + 1) * COLS]
                    for i in range(ROWS)
                ],
                axis=1,
            ).astype(BF16)
            at = x * 16 + zh * 4
            for i in range(2):
                out[at : at + 4, i, :] = piece[i * 4 : (i + 1) * 4]


def call(kernel, name, n_in, *shapes, scalars=0):
    out = [jax.ShapeDtypeStruct(s, BF16) for s in shapes]
    spaces = [pltpu.SMEM] * scalars + [pltpu.VMEM] * (n_in - scalars)
    return pl.pallas_call(
        kernel,
        in_specs=[pl.BlockSpec(memory_space=space) for space in spaces],
        out_shape=out if len(out) > 1 else out[0],
        name=name,
        compiler_params=pltpu.CompilerParams(vmem_limit_bytes=32 * 1024 * 1024),
    )


def call_first(*operands):
    return pl.pallas_call(
        first_kernel,
        in_specs=[pl.BlockSpec(memory_space=pltpu.HBM)] * len(operands),
        out_shape=[
            jax.ShapeDtypeStruct((PAIRS, 2, 2 * TILE), BF16),
            jax.ShapeDtypeStruct((4, WIDTH), F32),
        ],
        scratch_shapes=[
            pltpu.VMEM((TILE, WIDTH), BF16),
            pltpu.VMEM((ROWS, COLS), jnp.int32),
            pltpu.VMEM((WIDTH, 4 * WIDTH), BF16),
            pltpu.SemaphoreType.DMA((7,)),
        ],
        name="project_first",
        compiler_params=pltpu.CompilerParams(vmem_limit_bytes=60 * 1024 * 1024),
    )(*operands)


def per_device(
    pair_input,
    pair_mask,
    out_norm_gain,
    out_w_in,
    out_final_gain,
    out_w_out,
    in_norm_gain,
    in_w_in,
    in_final_gain,
    in_w_out,
):
    out_norm_gain, out_final_gain, in_norm_gain, in_final_gain = (
        g.reshape(1, WIDTH) for g in (out_norm_gain, out_final_gain, in_norm_gain, in_final_gain)
    )
    left_order = one_hot(reorder((2, 4, 4, 4), (2, 1, 0, 3)))
    right_order = one_hot(reorder((2, 4, 4, 4), (2, 1, 3, 0)))
    out_rows = one_hot(reorder((ROWS, 32), (1, 0)))
    piece_order = one_hot(reorder((4, 2, 4), (1, 0, 2)))
    halves = np.stack(
        [one_hot(reorder((2 * ROWS, 2, ROWS), (1, 0, 2))[core], 2 * TILE).T for core in range(2)]
    )
    place = np.full((2, ROWS, 2, 4), -1)
    for i in range(2):
        place[i, :, i, :] = reorder((4, ROWS), (1, 0))
    in_rows = np.stack([one_hot(place[i], 4 * ROWS) for i in range(2)])
    left_order, right_order, out_rows, piece_order, halves, in_rows = (
        jnp.asarray(t) for t in (left_order, right_order, out_rows, piece_order, halves, in_rows)
    )
    core = lax.axis_index("core").reshape(1).astype(jnp.int32)

    def spread(sent, order):
        got = lax.all_to_all(sent, order, 0, 0, tiled=True)
        return got, lax.all_gather(got, "core", tiled=True)

    pair = pair_input.reshape(TILE, WIDTH)
    sent, gains = call_first(
        pair,
        pair_mask,
        out_norm_gain,
        out_final_gain,
        in_norm_gain,
        in_final_gain,
        out_w_in,
    )
    own, both = spread(sent, OUT_CHANNEL)
    pieces = call(outgoing_kernel, "outgoing", 6, (16, 72, 128), scalars=1)(core, own, both, left_order, right_order, out_rows)
    got = lax.all_to_all(pieces, LINE, 0, 0, tiled=True)
    sums = call(add_kernel, "add_parts", 2, (16, 2, 4 * TILE))(got, piece_order)
    tri = lax.all_to_all(sums, PLANE, 0, 0, tiled=True)

    middle, sent = call(middle_kernel, "middle", 7, (TILE, WIDTH), (PAIRS, 2, 2 * TILE))(
        pair, pair_mask, tri, gains, out_w_in, out_w_out, in_w_in
    )
    _, both = spread(sent, IN_CHANNEL)
    left = call(split_kernel, "split", 4, (96, N), scalars=1)(core, both, halves, in_rows)
    lefts = lax.all_gather(left, "zh", tiled=True)
    sums = call(incoming_kernel, "incoming", 2, (PAIRS, 2, TILE))(both, lefts)
    tri = lax.all_to_all(sums, IN_CHANNEL, 0, 0, tiled=True)
    out = call(last_kernel, "last", 5, (TILE, WIDTH))(middle, tri, gains, in_w_in, in_w_out)
    return out.reshape(ROWS, COLS, WIDTH)


def solution(mesh):
    fine = Mesh(
        mesh.devices.reshape([SIZES[a] for a in ROW + COL]), ROW + COL
    )
    placed = (P(ROW, COL, None), P(ROW, COL), P(), P(), P(), P(), P(), P(), P(), P())
    return jax.shard_map(
        per_device, mesh=fine, in_specs=placed, out_specs=P(ROW, COL, None), check_vma=False
    )
```

time: 136 us -> 133 us (0.978)
  blocking collectives: 127 us -> 101 us
  starting transfers between devices: 0 us -> 12.6 us
  waiting for transfers between devices: 0 us -> 9.88 us
    all_to_all x2 -> x1, blocking collectives: 47.4 us -> 21.2 us  [spread(): got = lax.all_to_all(sent, order, 0, 0, tiled=True)]
    all_to_all x0 -> x1, starting transfers between devices: none -> 12.6 us  [spread(): got = lax.all_to_all(sent, order, 0, 0, tiled=True)]
    all_gather x1 -> x3, blocking collectives: 18 us -> 29.5 us  [the longest x1 21 us: per_device(): lefts = lax.all_gather(left, 'zh', tiled=True)]
    all_to_all x0 -> x1, waiting for transfers between devices: none -> 9.88 us  [spread(): got = lax.all_to_all(sent, order, 0, 0, tiled=True)]
    all_to_all x1, blocking collectives: 19.5 us -> 12.9 us  [per_device(): tri = lax.all_to_all(sums, IN_CHANNEL, 0, 0, tiled=True)]
    all_to_all x1, blocking collectives: 14.7 us -> 9.09 us  [per_device(): tri = lax.all_to_all(sums, PLANE, 0, 0, tiled=True)]
  transfers between devices with their start and end apart: 0 -> 1, of which waited for: 0 -> 1; matrix products, arithmetic and copies ran while one was open for 0% -> 0% of each run, Pallas kernels for 0% -> 0%
where the time goes in v5:
time: 133 us
  blocking collectives  101 us (76%)
  starting transfers between devices  12.6 us (9%)
  waiting for transfers between devices  9.88 us (7%)
  Pallas kernels  8.85 us (7%)
    all_to_all x1, blocking collectives, per_device(): got = lax.all_to_all(pieces, LINE, 0, 0, tiled=True)  28.7 us
    all_to_all x1, blocking collectives, spread(): got = lax.all_to_all(sent, order, 0, 0, tiled=True)  21.2 us
    all_gather x1, blocking collectives, per_device(): lefts = lax.all_gather(left, 'zh', tiled=True)  21 us
    all_to_all x1, blocking collectives, per_device(): tri = lax.all_to_all(sums, IN_CHANNEL, 0, 0, tiled=True)  12.9 us
    all_to_all x1, starting transfers between devices, spread(): got = lax.all_to_all(sent, order, 0, 0, tiled=True)  12.6 us
    all_to_all x1, waiting for transfers between devices, spread(): got = lax.all_to_all(sent, order, 0, 0, tiled=True)  9.88 us
    all_to_all x1, blocking collectives, per_device(): tri = lax.all_to_all(sums, PLANE, 0, 0, tiled=True)  9.09 us
    all_gather x2, blocking collectives, spread(): return (got, lax.all_gather(got, 'core', tiled=True))  8.49 us
  transfers between devices with their start and end apart: 1, of which 1 were waited for; matrix products, arithmetic and copies ran while one was open for 0% of the time, Pallas kernels for 0%

profile of v5, /device:TPU:1, one launch (start us, length us, event | category | flops | bytes accessed | tf_op | source)
XLA Modules:
  0.0 132.9 jit_solution(2222896569400829880)
XLA Ops:
  0.0 2.3 %project_first.1 = (bf16[64,2,576]{2,1,0:T(2,128)(2,1)}, f32[4,128]{1,0:T(4,128)}) custom-call(bf16[288,128]{1,0:T(8,128)(2,1)} %bitcast.7, s32[12,24]{1,0:T(8,128)} %mask.1, f32[1,128]{1,0:T(1,128)} %bitcast.9, f32[1,128]{1,0:T(1,128)} %bitcast.10, f32[1,128]{1,0:T(1,128)} %bitcast.11, f32[1,128]{1,0:T(1,128)} %bitcast.12, bf16[128,640]{1,0:T(8,128)(2,1)} %w_in.4), custom_call_target="tpu_custom_call" | custom-call | tf_op jit(solution)/shard_map/project_first/pallas_call | solution.py:208
  2.3 12.6 %all-to-all-start = ((bf16[64,2,576]{2,1,0:T(2,128)(2,1)}), bf16[64,2,576]{2,1,0:T(2,128)(2,1)S(1)}, u32[]{:S(2)}, u32[]{:S(2)}) async-start(bf16[64,2,576]{2,1,0:T(2,128)(2,1)} %get-tuple-element.9), calls=%async_computation | async-start | bytes 327680 | tf_op jit(solution)/shard_map/all_to_all | solution.py:258
  14.9 0.0 copy-start.3
  14.9 0.0 copy-start.9
  14.9 0.0 copy-start.10
  14.9 9.9 %all-to-all-done.own = bf16[64,2,576]{2,1,0:T(2,128)(2,1)S(1)} async-done(((bf16[64,2,576]{2,1,0:T(2,128)(2,1)}), bf16[64,2,576]{2,1,0:T(2,128)(2,1)S(1)}, u32[]{:S(2)}, u32[]{:S(2)}) %all-to-all-start) | async-done | bytes 147488 | tf_op jit(solution)/shard_map/all_to_all | solution.py:258
  24.8 3.8 %all_gather.9.both = bf16[128,2,576]{2,1,0:T(2,128)(2,1)S(1)} all-gather(bf16[64,2,576]{2,1,0:T(2,128)(2,1)S(1)} %all-to-all-done.own), channel_id=1, replica_groups=mesh['zl'=4,'y'=4,'core'=2,'x'=4,'zh'=4] {'core'}, dimensions={0}, use_global_device_ids=true | all-gather | bytes 442368 | tf_op jit(solution)/shard_map/all_gather | solution.py:259
  28.6 0.0 copy-done.3
  28.6 0.0 copy-done.9
  28.6 0.0 copy-done.10
  28.6 2.0 %outgoing.1 = bf16[16,72,128]{2,1,0:T(8,128)(2,1)S(1)} custom-call(s32[1]{0:T(128)} %bitcast.1.core, bf16[64,2,576]{2,1,0:T(2,128)(2,1)S(1)} %all-to-all-done.own, bf16[128,2,576]{2,1,0:T(2,128)(2,1)S(1)} %all_gather.9.both, bf16[128,128]{1,0:T(8,128)(2,1)S(1)} %copy-done.10, bf16[128,128]{1,0:T(8,128)(2,1)S(1)} %copy-done.9, bf16[384,384]{1,0:T(8,128)(2,1)S(1)} %copy-done.3), custom_call_target="tpu_custom_call" | custom-call | tf_op jit(solution)/shard_map/outgoing/pallas_call | solution.py:272
  30.6 0.0 copy-start.12
  30.6 0.0 copy-start.1
  30.6 0.0 copy-start.2
  30.6 0.0 copy-start.4
  30.6 0.0 copy-start.6
  30.7 0.0 copy-start.7
  30.7 0.0 copy-start.11
  30.7 28.7 %all_to_all.25.got = bf16[16,72,128]{2,1,0:T(8,128)(2,1)S(1)} all-to-all(bf16[16,72,128]{2,1,0:T(8,128)(2,1)S(1)} %outgoing.1), channel_id=1, replica_groups=mesh['zl'=4,'y'=4,'core'=2,'x'=4,'zh'=4] {'zl','zh'}, dimensions={0} | all-to-all | bytes 589824 | tf_op jit(solution)/shard_map/all_to_all | solution.py:273
  59.4 0.0 copy-done.12
  59.4 0.0 copy-start
  59.4 0.3 add_parts.1
  59.7 9.1 %all_to_all.26.tri = bf16[16,2,1152]{2,1,0:T(2,128)(2,1)S(1)} all-to-all(bf16[16,2,1152]{2,1,0:T(2,128)(2,1)S(1)} %add_parts.1), channel_id=1, replica_groups=mesh['zl'=4,'y'=4,'core'=2,'x'=4,'zh'=4] {'x','y'}, dimensions={0} | all-to-all | bytes 147456 | tf_op jit(solution)/shard_map/all_to_all | solution.py:275
  68.8 0.0 copy-done.1
  68.8 0.0 copy-done.2
  68.8 0.0 copy-done.4
  68.8 0.0 copy-done.6
  68.8 0.0 copy-done.7
  68.8 0.0 copy-done.11
  68.8 1.2 middle.1
  70.1 21.2 %all_to_all.27 = bf16[64,2,576]{2,1,0:T(2,128)(2,1)S(1)} all-to-all(bf16[64,2,576]{2,1,0:T(2,128)(2,1)S(1)} %get-tuple-element.12), channel_id=1, replica_groups=mesh['zl'=4,'y'=4,'core'=2,'x'=4,'zh'=4] {'x','y','zl'}, dimensions={0} | all-to-all | bytes 294912 | tf_op jit(solution)/shard_map/all_to_all | solution.py:258
  91.3 0.0 copy-start.5
  91.3 4.7 %all_gather.10.both = bf16[128,2,576]{2,1,0:T(2,128)(2,1)S(1)} all-gather(bf16[64,2,576]{2,1,0:T(2,128)(2,1)S(1)} %all_to_all.27), channel_id=1, replica_groups=mesh['zl'=4,'y'=4,'core'=2,'x'=4,'zh'=4] {'core'}, dimensions={0}, use_global_device_ids=true | all-gather | bytes 442368 | tf_op jit(solution)/shard_map/all_gather | solution.py:259
  96.0 0.0 copy-done
  96.0 0.0 copy-done.5
  96.0 1.0 split.1
  97.0 21.0 %all_gather.11.lefts = bf16[384,384]{1,0:T(8,128)(2,1)S(1)} all-gather(bf16[96,384]{1,0:T(8,128)(2,1)S(1)} %split.1), channel_id=1, replica_groups=mesh['zl'=4,'y'=4,'core'=2,'x'=4,'zh'=4] {'zh'}, dimensions={0}, use_global_device_ids=true | all-gather | bytes 368640 | tf_op jit(solution)/shard_map/all_gather | solution.py:282
  117.9 0.9 incoming.1
  118.8 0.0 copy-start.8
  118.8 12.9 %all_to_all.28.tri = bf16[64,2,288]{2,1,0:T(2,128)(2,1)S(1)} all-to-all(bf16[64,2,288]{2,1,0:T(2,128)(2,1)S(1)} %incoming.1), channel_id=1, replica_groups=mesh['zl'=4,'y'=4,'core'=2,'x'=4,'zh'=4] {'x','y','zl'}, dimensions={0} | all-to-all | bytes 147456 | tf_op jit(solution)/shard_map/all_to_all | solution.py:284
  131.7 0.0 copy-done.8
  131.7 1.1 last.1
Async XLA Ops:
  2.3 22.5 %all-to-all-start = ((bf16[64,2,576]{2,1,0:T(2,128)(2,1)}), bf16[64,2,576]{2,1,0:T(2,128)(2,1)S(1)}, u32[]{:S(2)}, u32[]{:S(2)}) async-start(bf16[64,2,576]{2,1,0:T(2,128)(2,1)} %get-tuple-element.9), calls=%async_computation | async-start | bytes 327680 | tf_op jit(solution)/shard_map/all_to_all | solution.py:258
  14.9 13.7 %copy-start.3 = (bf16[384,384]{1,0:T(8,128)(2,1)S(1)}, bf16[384,384]{1,0:T(8,128)(2,1)}, u32[]{:S(2)}) copy-start(bf16[384,384]{1,0:T(8,128)(2,1)} %constant.20.clone.rows) | copy-start | bytes 884740
  14.9 13.7 %copy-start.9 = (bf16[128,128]{1,0:T(8,128)(2,1)S(1)}, bf16[128,128]{1,0:T(8,128)(2,1)}, u32[]{:S(2)}) copy-start(bf16[128,128]{1,0:T(8,128)(2,1)} %constant.19.clone.right_order) | copy-start | bytes 98308
  14.9 13.7 %copy-start.10 = (bf16[128,128]{1,0:T(8,128)(2,1)S(1)}, bf16[128,128]{1,0:T(8,128)(2,1)}, u32[]{:S(2)}) copy-start(bf16[128,128]{1,0:T(8,128)(2,1)} %constant.18.clone.left_order) | copy-start | bytes 98308
  30.6 28.8 %copy-start.12 = (bf16[32,32]{1,0:T(8,128)(2,1)S(1)}, bf16[32,32]{1,0:T(8,128)(2,1)}, u32[]{:S(2)}) copy-start(bf16[32,32]{1,0:T(8,128)(2,1)} %constant.21.clone.order) | copy-start | bytes 6148
  30.6 38.2 %copy-start.1 = (bf16[128,640]{1,0:T(8,128)(2,1)S(1)}, bf16[128,640]{1,0:T(8,128)(2,1)}, u32[]{:S(2)}) copy-start(bf16[128,640]{1,0:T(8,128)(2,1)} %w_in.5) | copy-start | bytes 491524
  30.6 38.2 %copy-start.2 = (bf16[128,640]{1,0:T(8,128)(2,1)S(1)}, bf16[128,640]{1,0:T(8,128)(2,1)}, u32[]{:S(2)}) copy-start(bf16[128,640]{1,0:T(8,128)(2,1)} %w_in.4) | copy-start | bytes 491524
  30.6 38.2 %copy-start.4 = (bf16[12,24,128]{2,1,0:T(8,128)(2,1)S(1)}, bf16[12,24,128]{2,1,0:T(8,128)(2,1)}, u32[]{:S(2)}) copy-start(bf16[12,24,128]{2,1,0:T(8,128)(2,1)} %param.16) | copy-start | bytes 221188
  30.6 38.1 %copy-start.6 = (s32[12,24]{1,0:T(8,128)S(1)}, s32[12,24]{1,0:T(8,128)}, u32[]{:S(2)}) copy-start(s32[12,24]{1,0:T(8,128)} %mask.1) | copy-start | bytes 3460
  30.7 38.1 %copy-start.7 = (bf16[128,128]{1,0:T(8,128)(2,1)S(1)}, bf16[128,128]{1,0:T(8,128)(2,1)}, u32[]{:S(2)}) copy-start(bf16[128,128]{1,0:T(8,128)(2,1)} %w_out.2) | copy-start | bytes 98308
  30.7 38.1 %copy-start.11 = (f32[4,128]{1,0:T(4,128)S(1)}, f32[4,128]{1,0:T(4,128)}, u32[]{:S(2)}) copy-start(f32[4,128]{1,0:T(4,128)} %get-tuple-element.10.gains) | copy-start | bytes 6148
  59.4 36.6 %copy-start = (bf16[2,576,288]{2,1,0:T(8,128)(2,1)S(1)}, bf16[2,576,288]{2,1,0:T(8,128)(2,1)}, u32[]{:S(2)}) copy-start(bf16[2,576,288]{2,1,0:T(8,128)(2,1)} %constant.22.clone.halves) | copy-start | bytes 1990660
  91.3 4.7 %copy-start.5 = (bf16[2,96,48]{2,1,0:T(8,128)(2,1)S(1)}, bf16[2,96,48]{2,1,0:T(8,128)(2,1)}, u32[]{:S(2)}) copy-start(bf16[2,96,48]{2,1,0:T(8,128)(2,1)} %constant.23.clone.rows) | copy-start | bytes 55300
  118.8 12.9 %copy-start.8 = (bf16[128,128]{1,0:T(8,128)(2,1)S(1)}, bf16[128,128]{1,0:T(8,128)(2,1)}, u32[]{:S(2)}) copy-start(bf16[128,128]{1,0:T(8,128)(2,1)} %w_out.3) | copy-start | bytes 98308

commit v6 on v5

--- a/solution.py
+++ b/solution.py
@@ -1,3 +1,5 @@
+import functools
+
 import jax
 import jax.numpy as jnp
 import ml_dtypes
@@ -11,8 +13,8 @@
 ROW = ("zl", "y", "core")
 COL = ("x", "zh")
 SIZES = {"zl": 4, "y": 4, "core": 2, "x": 4, "zh": 4}
-OUT_CHANNEL = ("zl", "x", "y")
-IN_CHANNEL = ("x", "y", "zl")
+OUT_CHANNEL = ("y", "zl", "zh")
+IN_CHANNEL = ("x", "zl", "zh")
 LINE = ("zl", "zh")
 PLANE = ("x", "y")
 
@@ -62,7 +64,7 @@
 
 def sums_of(tri):
     pair = [tri[:, i, :].astype(F32) for i in range(2)]
-    return jnp.concatenate([v[:, zl * TILE : (zl + 1) * TILE] for v in pair for zl in range(4)], axis=0)
+    return jnp.concatenate([v[:, i * TILE : (i + 1) * TILE] for v in pair for i in range(4)], axis=0)
 
 
 def first_kernel(pair_ref, mask_ref, g0, g1, g2, g3, w_in, sent, gains, pair, mask, weights, sems):
@@ -91,8 +93,7 @@
 
 def last_kernel(pair_ref, tri, gains, w_in, w_out, out):
     pair = pair_ref[...].astype(F32)
-    sums = jnp.concatenate([tri[:, i, :].astype(F32) for i in range(2)], axis=0)
-    out[...] = update(pair, sums, gains[2:3], w_in, gains[3:4], w_out[...])
+    out[...] = update(pair, sums_of(tri), gains[2:3], w_in, gains[3:4], w_out[...])
 
 
 def chunks(side, wide):
@@ -115,6 +116,19 @@
     n = folded.shape[0] // 9
     rest = jnp.concatenate([folded[8 * n :, g * 32 : (g + 1) * 32] for g in range(4)], axis=0)
     return jnp.concatenate([folded[: 4 * n], folded[4 * n : 8 * n], rest], axis=1)
+
+
+def pack(sums, out):
+    for x in range(4):
+        strips = []
+        for zh in range(4):
+            at = (x * 4 + zh) * COLS
+            strips.append(
+                jnp.concatenate([sums[i * 32 : (i + 1) * 32, at : at + COLS] for i in range(ROWS)], axis=1)
+            )
+        for y in range(4):
+            piece = jnp.concatenate([s[y * 8 : (y + 1) * 8] for s in strips], axis=0)
+            out[x * 4 + y] = fold(piece).astype(BF16)
 
 
 def outgoing_kernel(core, own, both, left_order, right_order, rows, out):
@@ -127,69 +141,46 @@
     right = jnp.concatenate([chunks(right[:, :TILE], COLS), chunks(right[:, TILE:], COLS)], axis=1)
     right = jnp.dot(rows[...], right.astype(BF16), preferred_element_type=F32).astype(BF16)
     sums = lax.dot_general(left, right, (((1,), (1,)), ((), ())), preferred_element_type=F32)
-    for zh in range(4):
-        strips = []
-        for x in range(4):
-            at = (x * 4 + zh) * COLS
-            strips.append(
-                jnp.concatenate([sums[i * 32 : (i + 1) * 32, at : at + COLS] for i in range(ROWS)], axis=1)
-            )
-        for zl in range(4):
-            piece = jnp.concatenate([s[zl * 8 : (zl + 1) * 8] for s in strips], axis=0)
-            out[zl * 4 + zh] = fold(piece).astype(BF16)
-
-
-def add_kernel(got, order, out):
+    pack(sums, out)
+
+
+def incoming_kernel(core, both, order, rows, out):
+    def operand(side, wide):
+        return jnp.concatenate(
+            [
+                jnp.concatenate(
+                    [side[g * 8 : (g + 1) * 8, k * COLS : k * COLS + wide] for g in range(16)], axis=1
+                )
+                for k in range(ROWS)
+            ],
+            axis=0,
+        ).astype(BF16)
+
+    left = jnp.dot(order[...], both[:, 0, :], preferred_element_type=F32)
+    left = jnp.where(core[0] == 0, left, jnp.concatenate([left[:, ROWS:], left[:, :ROWS]], axis=1))
+    left = [operand(left[:, i * TILE : (i + 1) * TILE], COLS // 2) for i in range(2)]
+    left = [
+        lax.dot_general(rows[i], left[i], (((1,), (1,)), ((), ())), preferred_element_type=F32)
+        for i in range(2)
+    ]
+    left = jnp.concatenate(left, axis=1).astype(BF16)
+    right = jnp.dot(order[...], both[:, 1, :], preferred_element_type=F32)
+    right = [operand(right[:, i * TILE : (i + 1) * TILE], COLS) for i in range(2)]
+    sums = jnp.dot(left, jnp.concatenate(right, axis=0), preferred_element_type=F32)
+    pack(sums, out)
+
+
+def add_kernel(added, got, order, out):
     parts = []
-    for zl in range(4):
-        total = got[zl * 4].astype(F32)
-        for zh in range(1, 4):
-            total += got[zl * 4 + zh].astype(F32)
+    for i in range(4):
+        total = 0.0
+        for j in range(4):
+            total += got[j * 4 + i if added == 0 else i * 4 + j].astype(F32)
         parts.append(unfold(total))
     total = jnp.concatenate(parts, axis=1).astype(BF16)
     total = jnp.dot(order[...], total, preferred_element_type=F32).astype(BF16)
     for i in range(2):
         out[:, i, :] = total[i * 16 : (i + 1) * 16]
-
-
-def by_x(side):
-    return jnp.concatenate(
-        [side[c * PAIRS + x * 16 : c * PAIRS + (x + 1) * 16] for x in range(4) for c in range(2)], axis=0
-    )
-
-
-def split_kernel(core, both, halves, rows, left):
-    side = by_x(jnp.dot(both[:, 0, :], halves[core[0]], preferred_element_type=F32))
-    terms = [
-        lax.dot_general(
-            rows[i],
-            chunks(side[:, i * TILE // 2 : (i + 1) * TILE // 2], COLS // 2).astype(BF16),
-            (((1,), (1,)), ((), ())),
-            preferred_element_type=F32,
-        )
-        for i in range(2)
-    ]
-    left[...] = (terms[0] + terms[1]).astype(BF16)
-
-
-def incoming_kernel(both, lefts, out):
-    right = by_x(both[:, 1, :].astype(F32))
-    right = jnp.concatenate([chunks(right[:, :TILE], COLS), chunks(right[:, TILE:], COLS)], axis=1)
-    sums = jnp.dot(lefts[...], right.astype(BF16), preferred_element_type=F32)
-    first = lax.broadcasted_iota(jnp.int32, (N, 4 * COLS), 0) % 8 < 4
-    sums = jnp.where(first, sums[:, : 4 * COLS], sums[:, 4 * COLS :])
-    for zh in range(4):
-        for x in range(4):
-            piece = jnp.concatenate(
-                [
-                    sums[zh * 96 + i * 8 : zh * 96 + (i + 1) * 8, x * COLS : (x + 1) * COLS]
-                    for i in range(ROWS)
-                ],
-                axis=1,
-            ).astype(BF16)
-            at = x * 16 + zh * 4
-            for i in range(2):
-                out[at : at + 4, i, :] = piece[i * 4 : (i + 1) * 4]
 
 
 def call(kernel, name, n_in, *shapes, scalars=0):
@@ -238,25 +229,29 @@
     out_norm_gain, out_final_gain, in_norm_gain, in_final_gain = (
         g.reshape(1, WIDTH) for g in (out_norm_gain, out_final_gain, in_norm_gain, in_final_gain)
     )
-    left_order = one_hot(reorder((2, 4, 4, 4), (2, 1, 0, 3)))
-    right_order = one_hot(reorder((2, 4, 4, 4), (2, 1, 3, 0)))
+    left_order = one_hot(reorder((2, 4, 4, 4), (3, 1, 0, 2)))
+    right_order = one_hot(reorder((2, 4, 4, 4), (3, 2, 1, 0)))
     out_rows = one_hot(reorder((ROWS, 32), (1, 0)))
-    piece_order = one_hot(reorder((4, 2, 4), (1, 0, 2)))
-    halves = np.stack(
-        [one_hot(reorder((2 * ROWS, 2, ROWS), (1, 0, 2))[core], 2 * TILE).T for core in range(2)]
-    )
-    place = np.full((2, ROWS, 2, 4), -1)
+    piece_order = one_hot(reorder((4, 2, 4), (1, 2, 0)))
+    in_order = one_hot(reorder((2, 4, 4, 4), (1, 3, 0, 2)))
+    place = np.full((2, ROWS, 4, 2, 4), -1)
     for i in range(2):
-        place[i, :, i, :] = reorder((4, ROWS), (1, 0))
-    in_rows = np.stack([one_hot(place[i], 4 * ROWS) for i in range(2)])
-    left_order, right_order, out_rows, piece_order, halves, in_rows = (
-        jnp.asarray(t) for t in (left_order, right_order, out_rows, piece_order, halves, in_rows)
+        place[i, :, :, i, :] = reorder((4, 4, ROWS), (2, 1, 0))
+    in_rows = np.stack([one_hot(place[i], 16 * ROWS) for i in range(2)])
+    left_order, right_order, out_rows, piece_order, in_order, in_rows = (
+        jnp.asarray(t) for t in (left_order, right_order, out_rows, piece_order, in_order, in_rows)
     )
     core = lax.axis_index("core").reshape(1).astype(jnp.int32)
 
     def spread(sent, order):
         got = lax.all_to_all(sent, order, 0, 0, tiled=True)
         return got, lax.all_gather(got, "core", tiled=True)
+
+    def collect(pieces, added):
+        got = lax.all_to_all(pieces, PLANE, 0, 0, tiled=True)
+        add = functools.partial(add_kernel, added)
+        sums = call(add, "add_parts", 2, (16, 2, 4 * TILE))(got, piece_order)
+        return lax.all_to_all(sums, LINE, 0, 0, tiled=True)
 
     pair = pair_input.reshape(TILE, WIDTH)
     sent, gains = call_first(
@@ -270,18 +265,16 @@
     )
     own, both = spread(sent, OUT_CHANNEL)
     pieces = call(outgoing_kernel, "outgoing", 6, (16, 72, 128), scalars=1)(core, own, both, left_order, right_order, out_rows)
-    got = lax.all_to_all(pieces, LINE, 0, 0, tiled=True)
-    sums = call(add_kernel, "add_parts", 2, (16, 2, 4 * TILE))(got, piece_order)
-    tri = lax.all_to_all(sums, PLANE, 0, 0, tiled=True)
+    tri = collect(pieces, 0)
 
     middle, sent = call(middle_kernel, "middle", 7, (TILE, WIDTH), (PAIRS, 2, 2 * TILE))(
         pair, pair_mask, tri, gains, out_w_in, out_w_out, in_w_in
     )
     _, both = spread(sent, IN_CHANNEL)
-    left = call(split_kernel, "split", 4, (96, N), scalars=1)(core, both, halves, in_rows)
-    lefts = lax.all_gather(left, "zh", tiled=True)
-    sums = call(incoming_kernel, "incoming", 2, (PAIRS, 2, TILE))(both, lefts)
-    tri = lax.all_to_all(sums, IN_CHANNEL, 0, 0, tiled=True)
+    pieces = call(incoming_kernel, "incoming", 4, (16, 72, 128), scalars=1)(
+        core, both, in_order, in_rows
+    )
+    tri = collect(pieces, 1)
     out = call(last_kernel, "last", 5, (TILE, WIDTH))(middle, tri, gains, in_w_in, in_w_out)
     return out.reshape(ROWS, COLS, WIDTH)
 

time: 133 us -> 132 us (level); the launches traced: 133 us -> 130 us
  blocking collectives: 101 us -> 83.4 us
  waiting for transfers between devices: 9.88 us -> 16.7 us
  starting transfers between devices: 12.6 us -> 19.3 us
    all_gather x1 -> x0, blocking collectives: 21 us -> none  [per_device(): lefts = lax.all_gather(left, 'zh', tiled=True)]
    all_to_all x1, waiting for transfers between devices: 9.88 us -> 16.7 us  [spread(): got = lax.all_to_all(sent, order, 0, 0, tiled=True)]
    all_to_all x1, starting transfers between devices: 12.6 us -> 19.3 us  [spread(): got = lax.all_to_all(sent, order, 0, 0, tiled=True)]
    all_gather x2, blocking collectives: 8.49 us -> 10.8 us  [spread(): return (got, lax.all_gather(got, 'core', tiled=True))]
    all_to_all x3 -> x4, blocking collectives: 50.7 us -> 51.6 us  [the longest x2 28.7 us: collect(): return lax.all_to_all(sums, LINE, 0, 0, tiled=True)]
where the time goes in v6:
time: 132 us; the launch traced here: 130 us
  blocking collectives  83.4 us (63%)
  starting transfers between devices  19.3 us (15%)
  waiting for transfers between devices  16.7 us (13%)
  Pallas kernels  10.1 us (8%)
    all_to_all x2, blocking collectives, collect(): return lax.all_to_all(sums, LINE, 0, 0, tiled=True)  28.7 us
    all_to_all x2, blocking collectives, collect(): got = lax.all_to_all(pieces, PLANE, 0, 0, tiled=True)  23 us
    all_to_all x1, blocking collectives, spread(): got = lax.all_to_all(sent, order, 0, 0, tiled=True)  20.9 us
    all_to_all x1, starting transfers between devices, spread(): got = lax.all_to_all(sent, order, 0, 0, tiled=True)  19.3 us
    all_to_all x1, waiting for transfers between devices, spread(): got = lax.all_to_all(sent, order, 0, 0, tiled=True)  16.7 us
    all_gather x2, blocking collectives, spread(): return (got, lax.all_gather(got, 'core', tiled=True))  10.8 us
    pallas_call x1, Pallas kernels, per_device(): call(incoming_kernel, 'incoming', 4, (16, 72, 128), scalars=1)  2.8 us
  transfers between devices with their start and end apart: 1, of which 1 were waited for; matrix products, arithmetic and copies ran while one was open for 0% of the time, Pallas kernels for 0%

profile of v6, /device:TPU:1, one launch (start us, length us, event | category | flops | bytes accessed | tf_op | source)
XLA Modules:
  0.0 129.8 jit_solution(5872725410410083527)
XLA Ops:
  0.0 2.3 %project_first.1 = (bf16[64,2,576]{2,1,0:T(2,128)(2,1)}, f32[4,128]{1,0:T(4,128)}) custom-call(bf16[288,128]{1,0:T(8,128)(2,1)} %bitcast.7, s32[12,24]{1,0:T(8,128)} %mask.1, f32[1,128]{1,0:T(1,128)} %bitcast.9, f32[1,128]{1,0:T(1,128)} %bitcast.10, f32[1,128]{1,0:T(1,128)} %bitcast.11, f32[1,128]{1,0:T(1,128)} %bitcast.12, bf16[128,640]{1,0:T(8,128)(2,1)} %w_in.4), custom_call_target="tpu_custom_call" | custom-call | tf_op jit(solution)/shard_map/project_first/pallas_call | solution.py:199
  2.3 19.3 %all-to-all-start = ((bf16[64,2,576]{2,1,0:T(2,128)(2,1)}), bf16[64,2,576]{2,1,0:T(2,128)(2,1)S(1)}, u32[]{:S(2)}, u32[]{:S(2)}) async-start(bf16[64,2,576]{2,1,0:T(2,128)(2,1)} %get-tuple-element.9), calls=%async_computation | async-start | bytes 327680 | tf_op jit(solution)/shard_map/all_to_all | solution.py:247
  21.6 0.0 copy-start.3
  21.6 0.0 copy-start.8
  21.6 0.0 copy-start.9
  21.7 16.7 %all-to-all-done.own = bf16[64,2,576]{2,1,0:T(2,128)(2,1)S(1)} async-done(((bf16[64,2,576]{2,1,0:T(2,128)(2,1)}), bf16[64,2,576]{2,1,0:T(2,128)(2,1)S(1)}, u32[]{:S(2)}, u32[]{:S(2)}) %all-to-all-start) | async-done | bytes 147488 | tf_op jit(solution)/shard_map/all_to_all | solution.py:247
  38.4 5.0 %all_gather.6.both = bf16[128,2,576]{2,1,0:T(2,128)(2,1)S(1)} all-gather(bf16[64,2,576]{2,1,0:T(2,128)(2,1)S(1)} %all-to-all-done.own), channel_id=1, replica_groups=mesh['zl'=4,'y'=4,'core'=2,'x'=4,'zh'=4] {'core'}, dimensions={0}, use_global_device_ids=true | all-gather | bytes 442368 | tf_op jit(solution)/shard_map/all_gather | solution.py:248
  43.4 0.0 copy-done.3
  43.4 0.0 copy-done.8
  43.4 0.0 copy-done.9
  43.4 2.0 %outgoing.1 = bf16[16,72,128]{2,1,0:T(8,128)(2,1)S(1)} custom-call(s32[1]{0:T(128)} %bitcast.1.core, bf16[64,2,576]{2,1,0:T(2,128)(2,1)S(1)} %all-to-all-done.own, bf16[128,2,576]{2,1,0:T(2,128)(2,1)S(1)} %all_gather.6.both, bf16[128,128]{1,0:T(8,128)(2,1)S(1)} %copy-done.9, bf16[128,128]{1,0:T(8,128)(2,1)S(1)} %copy-done.8, bf16[384,384]{1,0:T(8,128)(2,1)S(1)} %copy-done.3), custom_call_target="tpu_custom_call" | custom-call | tf_op jit(solution)/shard_map/outgoing/pallas_call | solution.py:267
  45.4 0.0 copy-start.10
  45.5 12.0 %all_to_all.30.got = bf16[16,72,128]{2,1,0:T(8,128)(2,1)S(1)} all-to-all(bf16[16,72,128]{2,1,0:T(8,128)(2,1)S(1)} %outgoing.1), channel_id=1, replica_groups=mesh['zl'=4,'y'=4,'core'=2,'x'=4,'zh'=4] {'x','y'}, dimensions={0} | all-to-all | bytes 589824 | tf_op jit(solution)/shard_map/all_to_all | solution.py:251
  57.4 0.0 copy-done.10
  57.4 0.0 copy-start
  57.4 0.0 copy-start.1
  57.4 0.3 add_parts.2
  57.8 0.0 copy-start.4
  57.8 0.0 copy-start.5
  57.8 0.0 copy-start.6
  57.8 0.0 copy-start.12
  57.8 14.4 %all_to_all.31.tri = bf16[16,2,1152]{2,1,0:T(2,128)(2,1)S(1)} all-to-all(bf16[16,2,1152]{2,1,0:T(2,128)(2,1)S(1)} %add_parts.2), channel_id=1, replica_groups=mesh['zl'=4,'y'=4,'core'=2,'x'=4,'zh'=4] {'zl','zh'}, dimensions={0} | all-to-all | bytes 147456 | tf_op jit(solution)/shard_map/all_to_all | solution.py:254
  72.2 0.0 copy-done
  72.2 0.0 copy-done.1
  72.2 0.0 copy-done.4
  72.2 0.0 copy-done.5
  72.2 0.0 copy-done.6
  72.2 0.0 copy-done.12
  72.2 1.2 middle.1
  73.5 0.0 copy-start.2
  73.5 20.9 %all_to_all.32 = bf16[64,2,576]{2,1,0:T(2,128)(2,1)S(1)} all-to-all(bf16[64,2,576]{2,1,0:T(2,128)(2,1)S(1)} %get-tuple-element.12), channel_id=1, replica_groups=mesh['zl'=4,'y'=4,'core'=2,'x'=4,'zh'=4] {'x','zl','zh'}, dimensions={0} | all-to-all | bytes 294912 | tf_op jit(solution)/shard_map/all_to_all | solution.py:247
  94.4 0.0 copy-start.11
  94.4 5.8 %all_gather.7.both = bf16[128,2,576]{2,1,0:T(2,128)(2,1)S(1)} all-gather(bf16[64,2,576]{2,1,0:T(2,128)(2,1)S(1)} %all_to_all.32), channel_id=1, replica_groups=mesh['zl'=4,'y'=4,'core'=2,'x'=4,'zh'=4] {'core'}, dimensions={0}, use_global_device_ids=true | all-gather | bytes 442368 | tf_op jit(solution)/shard_map/all_gather | solution.py:248
  100.2 0.0 copy-done.2
  100.2 0.0 copy-done.11
  100.2 2.8 %incoming.1 = bf16[16,72,128]{2,1,0:T(8,128)(2,1)S(1)} custom-call(s32[1]{0:T(128)} %bitcast.1.core, bf16[128,2,576]{2,1,0:T(2,128)(2,1)S(1)} %all_gather.7.both, bf16[128,128]{1,0:T(8,128)(2,1)S(1)} %copy-done.11, bf16[2,384,192]{2,1,0:T(8,128)(2,1)S(1)} %copy-done.2), custom_call_target="tpu_custom_call" | custom-call | tf_op jit(solution)/shard_map/incoming/pallas_call | solution.py:274
  103.0 11.0 %all_to_all.33.got = bf16[16,72,128]{2,1,0:T(8,128)(2,1)S(1)} all-to-all(bf16[16,72,128]{2,1,0:T(8,128)(2,1)S(1)} %incoming.1), channel_id=1, replica_groups=mesh['zl'=4,'y'=4,'core'=2,'x'=4,'zh'=4] {'x','y'}, dimensions={0} | all-to-all | bytes 589824 | tf_op jit(solution)/shard_map/all_to_all | solution.py:251
  114.1 0.3 add_parts.3
  114.4 0.0 copy-start.7
  114.4 14.3 %all_to_all.34.tri = bf16[16,2,1152]{2,1,0:T(2,128)(2,1)S(1)} all-to-all(bf16[16,2,1152]{2,1,0:T(2,128)(2,1)S(1)} %add_parts.3), channel_id=1, replica_groups=mesh['zl'=4,'y'=4,'core'=2,'x'=4,'zh'=4] {'zl','zh'}, dimensions={0} | all-to-all | bytes 147456 | tf_op jit(solution)/shard_map/all_to_all | solution.py:254
  128.6 0.0 copy-done.7
  128.6 1.2 last.1
Async XLA Ops:
  2.3 36.1 %all-to-all-start = ((bf16[64,2,576]{2,1,0:T(2,128)(2,1)}), bf16[64,2,576]{2,1,0:T(2,128)(2,1)S(1)}, u32[]{:S(2)}, u32[]{:S(2)}) async-start(bf16[64,2,576]{2,1,0:T(2,128)(2,1)} %get-tuple-element.9), calls=%async_computation | async-start | bytes 327680 | tf_op jit(solution)/shard_map/all_to_all | solution.py:247
  21.6 21.8 %copy-start.3 = (bf16[384,384]{1,0:T(8,128)(2,1)S(1)}, bf16[384,384]{1,0:T(8,128)(2,1)}, u32[]{:S(2)}) copy-start(bf16[384,384]{1,0:T(8,128)(2,1)} %constant.20.clone.rows) | copy-start | bytes 884740
  21.6 21.8 %copy-start.8 = (bf16[128,128]{1,0:T(8,128)(2,1)S(1)}, bf16[128,128]{1,0:T(8,128)(2,1)}, u32[]{:S(2)}) copy-start(bf16[128,128]{1,0:T(8,128)(2,1)} %constant.19.clone.right_order) | copy-start | bytes 98308
  21.6 21.8 %copy-start.9 = (bf16[128,128]{1,0:T(8,128)(2,1)S(1)}, bf16[128,128]{1,0:T(8,128)(2,1)}, u32[]{:S(2)}) copy-start(bf16[128,128]{1,0:T(8,128)(2,1)} %constant.18.clone.left_order) | copy-start | bytes 98308
  45.4 12.0 %copy-start.10 = (bf16[32,32]{1,0:T(8,128)(2,1)S(1)}, bf16[32,32]{1,0:T(8,128)(2,1)}, u32[]{:S(2)}) copy-start(bf16[32,32]{1,0:T(8,128)(2,1)} %constant.21.clone.order) | copy-start | bytes 6148
  57.4 14.8 %copy-start = (bf16[128,640]{1,0:T(8,128)(2,1)S(1)}, bf16[128,640]{1,0:T(8,128)(2,1)}, u32[]{:S(2)}) copy-start(bf16[128,640]{1,0:T(8,128)(2,1)} %w_in.5) | copy-start | bytes 491524
  57.4 14.8 %copy-start.1 = (bf16[128,640]{1,0:T(8,128)(2,1)S(1)}, bf16[128,640]{1,0:T(8,128)(2,1)}, u32[]{:S(2)}) copy-start(bf16[128,640]{1,0:T(8,128)(2,1)} %w_in.4) | copy-start | bytes 491524
  57.8 14.5 %copy-start.4 = (bf16[12,24,128]{2,1,0:T(8,128)(2,1)S(1)}, bf16[12,24,128]{2,1,0:T(8,128)(2,1)}, u32[]{:S(2)}) copy-start(bf16[12,24,128]{2,1,0:T(8,128)(2,1)} %param.16) | copy-start | bytes 221188
  57.8 14.4 %copy-start.5 = (s32[12,24]{1,0:T(8,128)S(1)}, s32[12,24]{1,0:T(8,128)}, u32[]{:S(2)}) copy-start(s32[12,24]{1,0:T(8,128)} %mask.1) | copy-start | bytes 3460
  57.8 14.4 %copy-start.6 = (bf16[128,128]{1,0:T(8,128)(2,1)S(1)}, bf16[128,128]{1,0:T(8,128)(2,1)}, u32[]{:S(2)}) copy-start(bf16[128,128]{1,0:T(8,128)(2,1)} %w_out.2) | copy-start | bytes 98308
  57.8 14.4 %copy-start.12 = (f32[4,128]{1,0:T(4,128)S(1)}, f32[4,128]{1,0:T(4,128)}, u32[]{:S(2)}) copy-start(f32[4,128]{1,0:T(4,128)} %get-tuple-element.10.gains) | copy-start | bytes 6148
  73.5 26.8 %copy-start.2 = (bf16[2,384,192]{2,1,0:T(8,128)(2,1)S(1)}, bf16[2,384,192]{2,1,0:T(8,128)(2,1)}, u32[]{:S(2)}) copy-start(bf16[2,384,192]{2,1,0:T(8,128)(2,1)} %constant.23.clone.rows) | copy-start | bytes 884740
  94.4 5.8 %copy-start.11 = (bf16[128,128]{1,0:T(8,128)(2,1)S(1)}, bf16[128,128]{1,0:T(8,128)(2,1)}, u32[]{:S(2)}) copy-start(bf16[128,128]{1,0:T(8,128)(2,1)} %constant.22.clone.order) | copy-start | bytes 98308
  114.4 14.3 %copy-start.7 = (bf16[128,128]{1,0:T(8,128)(2,1)S(1)}, bf16[128,128]{1,0:T(8,128)(2,1)}, u32[]{:S(2)}) copy-start(bf16[128,128]{1,0:T(8,128)(2,1)} %w_out.3) | copy-start | bytes 98308

commit v7 on v6

--- a/solution.py
+++ b/solution.py
@@ -13,9 +13,9 @@
 ROW = ("zl", "y", "core")
 COL = ("x", "zh")
 SIZES = {"zl": 4, "y": 4, "core": 2, "x": 4, "zh": 4}
-OUT_CHANNEL = ("y", "zl", "zh")
-IN_CHANNEL = ("x", "zl", "zh")
-LINE = ("zl", "zh")
+OUT_CHANNEL = ("y", "zh", "zl")
+IN_CHANNEL = ("x", "zh", "zl")
+LINE = ("zh", "zl")
 PLANE = ("x", "y")
 
 ROWS, COLS, WIDTH = 12, 24, 128
@@ -229,11 +229,11 @@
     out_norm_gain, out_final_gain, in_norm_gain, in_final_gain = (
         g.reshape(1, WIDTH) for g in (out_norm_gain, out_final_gain, in_norm_gain, in_final_gain)
     )
-    left_order = one_hot(reorder((2, 4, 4, 4), (3, 1, 0, 2)))
-    right_order = one_hot(reorder((2, 4, 4, 4), (3, 2, 1, 0)))
+    left_order = one_hot(reorder((2, 4, 4, 4), (2, 1, 0, 3)))
+    right_order = one_hot(reorder((2, 4, 4, 4), (2, 3, 1, 0)))
     out_rows = one_hot(reorder((ROWS, 32), (1, 0)))
-    piece_order = one_hot(reorder((4, 2, 4), (1, 2, 0)))
-    in_order = one_hot(reorder((2, 4, 4, 4), (1, 3, 0, 2)))
+    piece_order = one_hot(reorder((4, 2, 4), (1, 0, 2)))
+    in_order = one_hot(reorder((2, 4, 4, 4), (1, 2, 0, 3)))
     place = np.full((2, ROWS, 4, 2, 4), -1)
     for i in range(2):
         place[i, :, :, i, :] = reorder((4, 4, ROWS), (2, 1, 0))

time: 132 us -> 131 us (level)
  waiting for transfers between devices: 16.7 us -> 15.1 us
    all_to_all x2, blocking collectives: 23 us -> 26.3 us  [collect(): got = lax.all_to_all(pieces, PLANE, 0, 0, tiled=True)]
    all_to_all x1, blocking collectives: 20.9 us -> 19.1 us  [spread(): got = lax.all_to_all(sent, order, 0, 0, tiled=True)]
    all_to_all x1, waiting for transfers between devices: 16.7 us -> 15.1 us  [spread(): got = lax.all_to_all(sent, order, 0, 0, tiled=True)]
where the time goes in v7:
time: 131 us; the launch traced here: 129 us
  blocking collectives  84.7 us (65%)
  starting transfers between devices  19.3 us (15%)
  waiting for transfers between devices  15.1 us (12%)
  Pallas kernels  10.1 us (8%)
    all_to_all x2, blocking collectives, collect(): return lax.all_to_all(sums, LINE, 0, 0, tiled=True)  28.6 us
    all_to_all x2, blocking collectives, collect(): got = lax.all_to_all(pieces, PLANE, 0, 0, tiled=True)  26.3 us
    all_to_all x1, starting transfers between devices, spread(): got = lax.all_to_all(sent, order, 0, 0, tiled=True)  19.3 us
    all_to_all x1, blocking collectives, spread(): got = lax.all_to_all(sent, order, 0, 0, tiled=True)  19.1 us
    all_to_all x1, waiting for transfers between devices, spread(): got = lax.all_to_all(sent, order, 0, 0, tiled=True)  15.1 us
    all_gather x2, blocking collectives, spread(): return (got, lax.all_gather(got, 'core', tiled=True))  10.7 us
    pallas_call x1, Pallas kernels, per_device(): call(incoming_kernel, 'incoming', 4, (16, 72, 128), scalars=1)  2.8 us
  transfers between devices with their start and end apart: 1, of which 1 were waited for; matrix products, arithmetic and copies ran while one was open for 0% of the time, Pallas kernels for 0%

profile of v7, /device:TPU:1, one launch (start us, length us, event | category | flops | bytes accessed | tf_op | source)
XLA Modules:
  0.0 129.4 jit_solution(5126769330775545490)
XLA Ops:
  0.0 2.3 %project_first.1 = (bf16[64,2,576]{2,1,0:T(2,128)(2,1)}, f32[4,128]{1,0:T(4,128)}) custom-call(bf16[288,128]{1,0:T(8,128)(2,1)} %bitcast.7, s32[12,24]{1,0:T(8,128)} %mask.1, f32[1,128]{1,0:T(1,128)} %bitcast.9, f32[1,128]{1,0:T(1,128)} %bitcast.10, f32[1,128]{1,0:T(1,128)} %bitcast.11, f32[1,128]{1,0:T(1,128)} %bitcast.12, bf16[128,640]{1,0:T(8,128)(2,1)} %w_in.4), custom_call_target="tpu_custom_call" | custom-call | tf_op jit(solution)/shard_map/project_first/pallas_call | solution.py:199
  2.3 19.3 %all-to-all-start = ((bf16[64,2,576]{2,1,0:T(2,128)(2,1)}), bf16[64,2,576]{2,1,0:T(2,128)(2,1)S(1)}, u32[]{:S(2)}, u32[]{:S(2)}) async-start(bf16[64,2,576]{2,1,0:T(2,128)(2,1)} %get-tuple-element.9), calls=%async_computation | async-start | bytes 327680 | tf_op jit(solution)/shard_map/all_to_all | solution.py:247
  21.6 0.0 copy-start.3
  21.6 0.0 copy-start.8
  21.6 0.0 copy-start.9
  21.7 15.1 %all-to-all-done.own = bf16[64,2,576]{2,1,0:T(2,128)(2,1)S(1)} async-done(((bf16[64,2,576]{2,1,0:T(2,128)(2,1)}), bf16[64,2,576]{2,1,0:T(2,128)(2,1)S(1)}, u32[]{:S(2)}, u32[]{:S(2)}) %all-to-all-start) | async-done | bytes 147488 | tf_op jit(solution)/shard_map/all_to_all | solution.py:247
  36.7 4.4 %all_gather.6.both = bf16[128,2,576]{2,1,0:T(2,128)(2,1)S(1)} all-gather(bf16[64,2,576]{2,1,0:T(2,128)(2,1)S(1)} %all-to-all-done.own), channel_id=1, replica_groups=mesh['zl'=4,'y'=4,'core'=2,'x'=4,'zh'=4] {'core'}, dimensions={0}, use_global_device_ids=true | all-gather | bytes 442368 | tf_op jit(solution)/shard_map/all_gather | solution.py:248
  41.1 0.0 copy-done.3
  41.1 0.0 copy-done.8
  41.1 0.0 copy-done.9
  41.1 2.0 %outgoing.1 = bf16[16,72,128]{2,1,0:T(8,128)(2,1)S(1)} custom-call(s32[1]{0:T(128)} %bitcast.1.core, bf16[64,2,576]{2,1,0:T(2,128)(2,1)S(1)} %all-to-all-done.own, bf16[128,2,576]{2,1,0:T(2,128)(2,1)S(1)} %all_gather.6.both, bf16[128,128]{1,0:T(8,128)(2,1)S(1)} %copy-done.9, bf16[128,128]{1,0:T(8,128)(2,1)S(1)} %copy-done.8, bf16[384,384]{1,0:T(8,128)(2,1)S(1)} %copy-done.3), custom_call_target="tpu_custom_call" | custom-call | tf_op jit(solution)/shard_map/outgoing/pallas_call | solution.py:267
  43.1 0.0 copy-start.10
  43.2 14.1 %all_to_all.30.got = bf16[16,72,128]{2,1,0:T(8,128)(2,1)S(1)} all-to-all(bf16[16,72,128]{2,1,0:T(8,128)(2,1)S(1)} %outgoing.1), channel_id=1, replica_groups=mesh['zl'=4,'y'=4,'core'=2,'x'=4,'zh'=4] {'x','y'}, dimensions={0} | all-to-all | bytes 589824 | tf_op jit(solution)/shard_map/all_to_all | solution.py:251
  57.3 0.0 copy-done.10
  57.3 0.0 copy-start
  57.3 0.0 copy-start.1
  57.3 0.3 add_parts.2
  57.6 0.0 copy-start.4
  57.6 0.0 copy-start.5
  57.6 0.0 copy-start.6
  57.6 0.0 copy-start.12
  57.7 14.4 %all_to_all.31.tri = bf16[16,2,1152]{2,1,0:T(2,128)(2,1)S(1)} all-to-all(bf16[16,2,1152]{2,1,0:T(2,128)(2,1)S(1)} %add_parts.2), channel_id=1, replica_groups=mesh['zl'=4,'y'=4,'core'=2,'x'=4,'zh'=4] {'zh','zl'}, dimensions={0} | all-to-all | bytes 147456 | tf_op jit(solution)/shard_map/all_to_all | solution.py:254
  72.1 0.0 copy-done
  72.1 0.0 copy-done.1
  72.1 0.0 copy-done.4
  72.1 0.0 copy-done.5
  72.1 0.0 copy-done.6
  72.1 0.0 copy-done.12
  72.1 1.2 middle.1
  73.3 0.0 copy-start.2
  73.3 19.1 %all_to_all.32 = bf16[64,2,576]{2,1,0:T(2,128)(2,1)S(1)} all-to-all(bf16[64,2,576]{2,1,0:T(2,128)(2,1)S(1)} %get-tuple-element.12), channel_id=1, replica_groups=mesh['zl'=4,'y'=4,'core'=2,'x'=4,'zh'=4] {'x','zh','zl'}, dimensions={0} | all-to-all | bytes 294912 | tf_op jit(solution)/shard_map/all_to_all | solution.py:247
  92.5 0.0 copy-start.11
  92.5 6.3 %all_gather.7.both = bf16[128,2,576]{2,1,0:T(2,128)(2,1)S(1)} all-gather(bf16[64,2,576]{2,1,0:T(2,128)(2,1)S(1)} %all_to_all.32), channel_id=1, replica_groups=mesh['zl'=4,'y'=4,'core'=2,'x'=4,'zh'=4] {'core'}, dimensions={0}, use_global_device_ids=true | all-gather | bytes 442368 | tf_op jit(solution)/shard_map/all_gather | solution.py:248
  98.7 0.0 copy-done.2
  98.7 0.0 copy-done.11
  98.7 2.8 %incoming.1 = bf16[16,72,128]{2,1,0:T(8,128)(2,1)S(1)} custom-call(s32[1]{0:T(128)} %bitcast.1.core, bf16[128,2,576]{2,1,0:T(2,128)(2,1)S(1)} %all_gather.7.both, bf16[128,128]{1,0:T(8,128)(2,1)S(1)} %copy-done.11, bf16[2,384,192]{2,1,0:T(8,128)(2,1)S(1)} %copy-done.2), custom_call_target="tpu_custom_call" | custom-call | tf_op jit(solution)/shard_map/incoming/pallas_call | solution.py:274
  101.5 12.2 %all_to_all.33.got = bf16[16,72,128]{2,1,0:T(8,128)(2,1)S(1)} all-to-all(bf16[16,72,128]{2,1,0:T(8,128)(2,1)S(1)} %incoming.1), channel_id=1, replica_groups=mesh['zl'=4,'y'=4,'core'=2,'x'=4,'zh'=4] {'x','y'}, dimensions={0} | all-to-all | bytes 589824 | tf_op jit(solution)/shard_map/all_to_all | solution.py:251
  113.7 0.3 add_parts.3
  114.0 0.0 copy-start.7
  114.0 14.2 %all_to_all.34.tri = bf16[16,2,1152]{2,1,0:T(2,128)(2,1)S(1)} all-to-all(bf16[16,2,1152]{2,1,0:T(2,128)(2,1)S(1)} %add_parts.3), channel_id=1, replica_groups=mesh['zl'=4,'y'=4,'core'=2,'x'=4,'zh'=4] {'zh','zl'}, dimensions={0} | all-to-all | bytes 147456 | tf_op jit(solution)/shard_map/all_to_all | solution.py:254
  128.3 0.0 copy-done.7
  128.3 1.2 last.1
Async XLA Ops:
  2.3 34.4 %all-to-all-start = ((bf16[64,2,576]{2,1,0:T(2,128)(2,1)}), bf16[64,2,576]{2,1,0:T(2,128)(2,1)S(1)}, u32[]{:S(2)}, u32[]{:S(2)}) async-start(bf16[64,2,576]{2,1,0:T(2,128)(2,1)} %get-tuple-element.9), calls=%async_computation | async-start | bytes 327680 | tf_op jit(solution)/shard_map/all_to_all | solution.py:247
  21.6 19.5 %copy-start.3 = (bf16[384,384]{1,0:T(8,128)(2,1)S(1)}, bf16[384,384]{1,0:T(8,128)(2,1)}, u32[]{:S(2)}) copy-start(bf16[384,384]{1,0:T(8,128)(2,1)} %constant.20.clone.rows) | copy-start | bytes 884740
  21.6 19.5 %copy-start.8 = (bf16[128,128]{1,0:T(8,128)(2,1)S(1)}, bf16[128,128]{1,0:T(8,128)(2,1)}, u32[]{:S(2)}) copy-start(bf16[128,128]{1,0:T(8,128)(2,1)} %constant.19.clone.right_order) | copy-start | bytes 98308
  21.6 19.5 %copy-start.9 = (bf16[128,128]{1,0:T(8,128)(2,1)S(1)}, bf16[128,128]{1,0:T(8,128)(2,1)}, u32[]{:S(2)}) copy-start(bf16[128,128]{1,0:T(8,128)(2,1)} %constant.18.clone.left_order) | copy-start | bytes 98308
  43.1 14.1 %copy-start.10 = (bf16[32,32]{1,0:T(8,128)(2,1)S(1)}, bf16[32,32]{1,0:T(8,128)(2,1)}, u32[]{:S(2)}) copy-start(bf16[32,32]{1,0:T(8,128)(2,1)} %constant.21.clone.order) | copy-start | bytes 6148
  57.3 14.8 %copy-start = (bf16[128,640]{1,0:T(8,128)(2,1)S(1)}, bf16[128,640]{1,0:T(8,128)(2,1)}, u32[]{:S(2)}) copy-start(bf16[128,640]{1,0:T(8,128)(2,1)} %w_in.5) | copy-start | bytes 491524
  57.3 14.8 %copy-start.1 = (bf16[128,640]{1,0:T(8,128)(2,1)S(1)}, bf16[128,640]{1,0:T(8,128)(2,1)}, u32[]{:S(2)}) copy-start(bf16[128,640]{1,0:T(8,128)(2,1)} %w_in.4) | copy-start | bytes 491524
  57.6 14.5 %copy-start.4 = (bf16[12,24,128]{2,1,0:T(8,128)(2,1)S(1)}, bf16[12,24,128]{2,1,0:T(8,128)(2,1)}, u32[]{:S(2)}) copy-start(bf16[12,24,128]{2,1,0:T(8,128)(2,1)} %param.16) | copy-start | bytes 221188
  57.6 14.5 %copy-start.5 = (s32[12,24]{1,0:T(8,128)S(1)}, s32[12,24]{1,0:T(8,128)}, u32[]{:S(2)}) copy-start(s32[12,24]{1,0:T(8,128)} %mask.1) | copy-start | bytes 3460
  57.6 14.5 %copy-start.6 = (bf16[128,128]{1,0:T(8,128)(2,1)S(1)}, bf16[128,128]{1,0:T(8,128)(2,1)}, u32[]{:S(2)}) copy-start(bf16[128,128]{1,0:T(8,128)(2,1)} %w_out.2) | copy-start | bytes 98308
  57.6 14.5 %copy-start.12 = (f32[4,128]{1,0:T(4,128)S(1)}, f32[4,128]{1,0:T(4,128)}, u32[]{:S(2)}) copy-start(f32[4,128]{1,0:T(4,128)} %get-tuple-element.10.gains) | copy-start | bytes 6148
  73.3 25.4 %copy-start.2 = (bf16[2,384,192]{2,1,0:T(8,128)(2,1)S(1)}, bf16[2,384,192]{2,1,0:T(8,128)(2,1)}, u32[]{:S(2)}) copy-start(bf16[2,384,192]{2,1,0:T(8,128)(2,1)} %constant.23.clone.rows) | copy-start | bytes 884740
  92.5 6.3 %copy-start.11 = (bf16[128,128]{1,0:T(8,128)(2,1)S(1)}, bf16[128,128]{1,0:T(8,128)(2,1)}, u32[]{:S(2)}) copy-start(bf16[128,128]{1,0:T(8,128)(2,1)} %constant.22.clone.order) | copy-start | bytes 98308
  114.0 14.2 %copy-start.7 = (bf16[128,128]{1,0:T(8,128)(2,1)S(1)}, bf16[128,128]{1,0:T(8,128)(2,1)}, u32[]{:S(2)}) copy-start(bf16[128,128]{1,0:T(8,128)(2,1)} %w_out.3) | copy-start | bytes 98308

commit v8 on v7

--- a/solution.py
+++ b/solution.py
@@ -139,12 +139,23 @@
     left = jnp.concatenate([jnp.where(first, left, 0.0), jnp.where(first, 0.0, left)], axis=1).astype(BF16)
     right = jnp.dot(right_order[...], both[:, 1, :], preferred_element_type=F32)
     right = jnp.concatenate([chunks(right[:, :TILE], COLS), chunks(right[:, TILE:], COLS)], axis=1)
-    right = jnp.dot(rows[...], right.astype(BF16), preferred_element_type=F32).astype(BF16)
+    blocks = []
+    for zl in range(4):
+        block = [right[i * 32 + zl * 8 : i * 32 + (zl + 1) * 8] for i in range(ROWS)]
+        block = jnp.concatenate(block, axis=0).astype(BF16)
+        blocks.append(jnp.dot(rows[...], block, preferred_element_type=F32))
+    right = jnp.concatenate(blocks, axis=0).astype(BF16)
     sums = lax.dot_general(left, right, (((1,), (1,)), ((), ())), preferred_element_type=F32)
     pack(sums, out)
 
 
-def incoming_kernel(core, both, order, rows, out):
+def by_column(side):
+    return jnp.concatenate(
+        [side[c * PAIRS + g * 4 : c * PAIRS + (g + 1) * 4] for g in range(16) for c in range(2)], axis=0
+    )
+
+
+def incoming_kernel(core, both, rows, out):
     def operand(side, wide):
         return jnp.concatenate(
             [
@@ -156,7 +167,7 @@
             axis=0,
         ).astype(BF16)
 
-    left = jnp.dot(order[...], both[:, 0, :], preferred_element_type=F32)
+    left = by_column(both[:, 0, :].astype(F32))
     left = jnp.where(core[0] == 0, left, jnp.concatenate([left[:, ROWS:], left[:, :ROWS]], axis=1))
     left = [operand(left[:, i * TILE : (i + 1) * TILE], COLS // 2) for i in range(2)]
     left = [
@@ -164,7 +175,7 @@
         for i in range(2)
     ]
     left = jnp.concatenate(left, axis=1).astype(BF16)
-    right = jnp.dot(order[...], both[:, 1, :], preferred_element_type=F32)
+    right = by_column(both[:, 1, :].astype(F32))
     right = [operand(right[:, i * TILE : (i + 1) * TILE], COLS) for i in range(2)]
     sums = jnp.dot(left, jnp.concatenate(right, axis=0), preferred_element_type=F32)
     pack(sums, out)
@@ -231,15 +242,14 @@
     )
     left_order = one_hot(reorder((2, 4, 4, 4), (2, 1, 0, 3)))
     right_order = one_hot(reorder((2, 4, 4, 4), (2, 3, 1, 0)))
-    out_rows = one_hot(reorder((ROWS, 32), (1, 0)))
+    out_rows = one_hot(reorder((ROWS, 8), (1, 0)))
     piece_order = one_hot(reorder((4, 2, 4), (1, 0, 2)))
-    in_order = one_hot(reorder((2, 4, 4, 4), (1, 2, 0, 3)))
     place = np.full((2, ROWS, 4, 2, 4), -1)
     for i in range(2):
         place[i, :, :, i, :] = reorder((4, 4, ROWS), (2, 1, 0))
     in_rows = np.stack([one_hot(place[i], 16 * ROWS) for i in range(2)])
-    left_order, right_order, out_rows, piece_order, in_order, in_rows = (
-        jnp.asarray(t) for t in (left_order, right_order, out_rows, piece_order, in_order, in_rows)
+    left_order, right_order, out_rows, piece_order, in_rows = (
+        jnp.asarray(t) for t in (left_order, right_order, out_rows, piece_order, in_rows)
     )
     core = lax.axis_index("core").reshape(1).astype(jnp.int32)
 
@@ -271,8 +281,8 @@
         pair, pair_mask, tri, gains, out_w_in, out_w_out, in_w_in
     )
     _, both = spread(sent, IN_CHANNEL)
-    pieces = call(incoming_kernel, "incoming", 4, (16, 72, 128), scalars=1)(
-        core, both, in_order, in_rows
+    pieces = call(incoming_kernel, "incoming", 3, (16, 72, 128), scalars=1)(
+        core, both, in_rows
     )
     tri = collect(pieces, 1)
     out = call(last_kernel, "last", 5, (TILE, WIDTH))(middle, tri, gains, in_w_in, in_w_out)

time: 131 us -> 130 us (level)
  no operation moved by 1% of the time
where the time goes in v8:
time: 130 us; the launch traced here: 128 us
  blocking collectives  84.6 us (65%)
  starting transfers between devices  19.3 us (15%)
  waiting for transfers between devices  15.1 us (12%)
  Pallas kernels  9.29 us (7%)
    all_to_all x2, blocking collectives, collect(): return lax.all_to_all(sums, LINE, 0, 0, tiled=True)  28.6 us
    all_to_all x2, blocking collectives, collect(): got = lax.all_to_all(pieces, PLANE, 0, 0, tiled=True)  26.3 us
    all_to_all x1, starting transfers between devices, spread(): got = lax.all_to_all(sent, order, 0, 0, tiled=True)  19.3 us
    all_to_all x1, blocking collectives, spread(): got = lax.all_to_all(sent, order, 0, 0, tiled=True)  19.1 us
    all_to_all x1, waiting for transfers between devices, spread(): got = lax.all_to_all(sent, order, 0, 0, tiled=True)  15.1 us
    all_gather x2, blocking collectives, spread(): return (got, lax.all_gather(got, 'core', tiled=True))  10.5 us
  transfers between devices with their start and end apart: 1, of which 1 were waited for; matrix products, arithmetic and copies ran while one was open for 0% of the time, Pallas kernels for 0%

profile of v8, /device:TPU:1, one launch (start us, length us, event | category | flops | bytes accessed | tf_op | source)
XLA Modules:
  0.0 128.4 jit_solution(4885525959610446238)
XLA Ops:
  0.0 2.3 %project_first.1 = (bf16[64,2,576]{2,1,0:T(2,128)(2,1)}, f32[4,128]{1,0:T(4,128)}) custom-call(bf16[288,128]{1,0:T(8,128)(2,1)} %bitcast.7, s32[12,24]{1,0:T(8,128)} %mask.1, f32[1,128]{1,0:T(1,128)} %bitcast.9, f32[1,128]{1,0:T(1,128)} %bitcast.10, f32[1,128]{1,0:T(1,128)} %bitcast.11, f32[1,128]{1,0:T(1,128)} %bitcast.12, bf16[128,640]{1,0:T(8,128)(2,1)} %w_in.4), custom_call_target="tpu_custom_call" | custom-call | tf_op jit(solution)/shard_map/project_first/pallas_call | solution.py:210
  2.3 19.3 %all-to-all-start = ((bf16[64,2,576]{2,1,0:T(2,128)(2,1)}), bf16[64,2,576]{2,1,0:T(2,128)(2,1)S(1)}, u32[]{:S(2)}, u32[]{:S(2)}) async-start(bf16[64,2,576]{2,1,0:T(2,128)(2,1)} %get-tuple-element.9), calls=%async_computation | async-start | bytes 327680 | tf_op jit(solution)/shard_map/all_to_all | solution.py:257
  21.6 0.0 copy-start.7
  21.6 0.0 copy-start.8
  21.6 0.0 copy-start.10
  21.6 15.1 %all-to-all-done.own = bf16[64,2,576]{2,1,0:T(2,128)(2,1)S(1)} async-done(((bf16[64,2,576]{2,1,0:T(2,128)(2,1)}), bf16[64,2,576]{2,1,0:T(2,128)(2,1)S(1)}, u32[]{:S(2)}, u32[]{:S(2)}) %all-to-all-start) | async-done | bytes 147488 | tf_op jit(solution)/shard_map/all_to_all | solution.py:257
  36.7 4.4 %all_gather.6.both = bf16[128,2,576]{2,1,0:T(2,128)(2,1)S(1)} all-gather(bf16[64,2,576]{2,1,0:T(2,128)(2,1)S(1)} %all-to-all-done.own), channel_id=1, replica_groups=mesh['zl'=4,'y'=4,'core'=2,'x'=4,'zh'=4] {'core'}, dimensions={0}, use_global_device_ids=true | all-gather | bytes 442368 | tf_op jit(solution)/shard_map/all_gather | solution.py:258
  41.1 0.0 copy-done.7
  41.1 0.0 copy-done.8
  41.1 0.0 copy-done.10
  41.1 2.0 %outgoing.1 = bf16[16,72,128]{2,1,0:T(8,128)(2,1)S(1)} custom-call(s32[1]{0:T(128)} %bitcast.1.core, bf16[64,2,576]{2,1,0:T(2,128)(2,1)S(1)} %all-to-all-done.own, bf16[128,2,576]{2,1,0:T(2,128)(2,1)S(1)} %all_gather.6.both, bf16[128,128]{1,0:T(8,128)(2,1)S(1)} %copy-done.8, bf16[128,128]{1,0:T(8,128)(2,1)S(1)} %copy-done.7, bf16[96,96]{1,0:T(8,128)(2,1)S(1)} %copy-done.10), custom_call_target="tpu_custom_call" | custom-call | tf_op jit(solution)/shard_map/outgoing/pallas_call | solution.py:277
  43.1 0.0 copy-start.9
  43.1 14.1 %all_to_all.30.got = bf16[16,72,128]{2,1,0:T(8,128)(2,1)S(1)} all-to-all(bf16[16,72,128]{2,1,0:T(8,128)(2,1)S(1)} %outgoing.1), channel_id=1, replica_groups=mesh['zl'=4,'y'=4,'core'=2,'x'=4,'zh'=4] {'x','y'}, dimensions={0} | all-to-all | bytes 589824 | tf_op jit(solution)/shard_map/all_to_all | solution.py:261
  57.3 0.0 copy-done.9
  57.3 0.0 copy-start
  57.3 0.0 copy-start.1
  57.3 0.3 add_parts.2
  57.6 0.0 copy-start.3
  57.6 0.0 copy-start.4
  57.6 0.0 copy-start.5
  57.6 0.0 copy-start.11
  57.6 14.4 %all_to_all.31.tri = bf16[16,2,1152]{2,1,0:T(2,128)(2,1)S(1)} all-to-all(bf16[16,2,1152]{2,1,0:T(2,128)(2,1)S(1)} %add_parts.2), channel_id=1, replica_groups=mesh['zl'=4,'y'=4,'core'=2,'x'=4,'zh'=4] {'zh','zl'}, dimensions={0} | all-to-all | bytes 147456 | tf_op jit(solution)/shard_map/all_to_all | solution.py:264
  72.0 0.0 copy-done
  72.0 0.0 copy-done.1
  72.0 0.0 copy-done.3
  72.0 0.0 copy-done.4
  72.0 0.0 copy-done.5
  72.1 0.0 copy-done.11
  72.1 1.2 middle.1
  73.3 0.0 copy-start.2
  73.3 19.1 %all_to_all.32 = bf16[64,2,576]{2,1,0:T(2,128)(2,1)S(1)} all-to-all(bf16[64,2,576]{2,1,0:T(2,128)(2,1)S(1)} %get-tuple-element.12), channel_id=1, replica_groups=mesh['zl'=4,'y'=4,'core'=2,'x'=4,'zh'=4] {'x','zh','zl'}, dimensions={0} | all-to-all | bytes 294912 | tf_op jit(solution)/shard_map/all_to_all | solution.py:257
  92.5 6.1 %all_gather.7.both = bf16[128,2,576]{2,1,0:T(2,128)(2,1)S(1)} all-gather(bf16[64,2,576]{2,1,0:T(2,128)(2,1)S(1)} %all_to_all.32), channel_id=1, replica_groups=mesh['zl'=4,'y'=4,'core'=2,'x'=4,'zh'=4] {'core'}, dimensions={0}, use_global_device_ids=true | all-gather | bytes 442368 | tf_op jit(solution)/shard_map/all_gather | solution.py:258
  98.6 0.0 copy-done.2
  98.6 2.0 %incoming.1 = bf16[16,72,128]{2,1,0:T(8,128)(2,1)S(1)} custom-call(s32[1]{0:T(128)} %bitcast.1.core, bf16[128,2,576]{2,1,0:T(2,128)(2,1)S(1)} %all_gather.7.both, bf16[2,384,192]{2,1,0:T(8,128)(2,1)S(1)} %copy-done.2), custom_call_target="tpu_custom_call" | custom-call | tf_op jit(solution)/shard_map/incoming/pallas_call | solution.py:284
  100.5 12.2 %all_to_all.33.got = bf16[16,72,128]{2,1,0:T(8,128)(2,1)S(1)} all-to-all(bf16[16,72,128]{2,1,0:T(8,128)(2,1)S(1)} %incoming.1), channel_id=1, replica_groups=mesh['zl'=4,'y'=4,'core'=2,'x'=4,'zh'=4] {'x','y'}, dimensions={0} | all-to-all | bytes 589824 | tf_op jit(solution)/shard_map/all_to_all | solution.py:261
  112.7 0.3 add_parts.3
  113.0 0.0 copy-start.6
  113.0 14.2 %all_to_all.34.tri = bf16[16,2,1152]{2,1,0:T(2,128)(2,1)S(1)} all-to-all(bf16[16,2,1152]{2,1,0:T(2,128)(2,1)S(1)} %add_parts.3), channel_id=1, replica_groups=mesh['zl'=4,'y'=4,'core'=2,'x'=4,'zh'=4] {'zh','zl'}, dimensions={0} | all-to-all | bytes 147456 | tf_op jit(solution)/shard_map/all_to_all | solution.py:264
  127.3 0.0 copy-done.6
  127.3 1.2 last.1
Async XLA Ops:
  2.3 34.4 %all-to-all-start = ((bf16[64,2,576]{2,1,0:T(2,128)(2,1)}), bf16[64,2,576]{2,1,0:T(2,128)(2,1)S(1)}, u32[]{:S(2)}, u32[]{:S(2)}) async-start(bf16[64,2,576]{2,1,0:T(2,128)(2,1)} %get-tuple-element.9), calls=%async_computation | async-start | bytes 327680 | tf_op jit(solution)/shard_map/all_to_all | solution.py:257
  21.6 19.5 %copy-start.7 = (bf16[128,128]{1,0:T(8,128)(2,1)S(1)}, bf16[128,128]{1,0:T(8,128)(2,1)}, u32[]{:S(2)}) copy-start(bf16[128,128]{1,0:T(8,128)(2,1)} %constant.17.clone.right_order) | copy-start | bytes 98308
  21.6 19.5 %copy-start.8 = (bf16[128,128]{1,0:T(8,128)(2,1)S(1)}, bf16[128,128]{1,0:T(8,128)(2,1)}, u32[]{:S(2)}) copy-start(bf16[128,128]{1,0:T(8,128)(2,1)} %constant.16.clone.left_order) | copy-start | bytes 98308
  21.6 19.5 %copy-start.10 = (bf16[96,96]{1,0:T(8,128)(2,1)S(1)}, bf16[96,96]{1,0:T(8,128)(2,1)}, u32[]{:S(2)}) copy-start(bf16[96,96]{1,0:T(8,128)(2,1)} %constant.18.clone.rows) | copy-start | bytes 55300
  43.1 14.2 %copy-start.9 = (bf16[32,32]{1,0:T(8,128)(2,1)S(1)}, bf16[32,32]{1,0:T(8,128)(2,1)}, u32[]{:S(2)}) copy-start(bf16[32,32]{1,0:T(8,128)(2,1)} %constant.19.clone.order) | copy-start | bytes 6148
  57.3 14.7 %copy-start = (bf16[128,640]{1,0:T(8,128)(2,1)S(1)}, bf16[128,640]{1,0:T(8,128)(2,1)}, u32[]{:S(2)}) copy-start(bf16[128,640]{1,0:T(8,128)(2,1)} %w_in.5) | copy-start | bytes 491524
  57.3 14.7 %copy-start.1 = (bf16[128,640]{1,0:T(8,128)(2,1)S(1)}, bf16[128,640]{1,0:T(8,128)(2,1)}, u32[]{:S(2)}) copy-start(bf16[128,640]{1,0:T(8,128)(2,1)} %w_in.4) | copy-start | bytes 491524
  57.6 14.4 %copy-start.3 = (bf16[12,24,128]{2,1,0:T(8,128)(2,1)S(1)}, bf16[12,24,128]{2,1,0:T(8,128)(2,1)}, u32[]{:S(2)}) copy-start(bf16[12,24,128]{2,1,0:T(8,128)(2,1)} %param.15) | copy-start | bytes 221188
  57.6 14.4 %copy-start.4 = (s32[12,24]{1,0:T(8,128)S(1)}, s32[12,24]{1,0:T(8,128)}, u32[]{:S(2)}) copy-start(s32[12,24]{1,0:T(8,128)} %mask.1) | copy-start | bytes 3460
  57.6 14.4 %copy-start.5 = (bf16[128,128]{1,0:T(8,128)(2,1)S(1)}, bf16[128,128]{1,0:T(8,128)(2,1)}, u32[]{:S(2)}) copy-start(bf16[128,128]{1,0:T(8,128)(2,1)} %w_out.2) | copy-start | bytes 98308
  57.6 14.4 %copy-start.11 = (f32[4,128]{1,0:T(4,128)S(1)}, f32[4,128]{1,0:T(4,128)}, u32[]{:S(2)}) copy-start(f32[4,128]{1,0:T(4,128)} %get-tuple-element.10.gains) | copy-start | bytes 6148
  73.3 25.3 %copy-start.2 = (bf16[2,384,192]{2,1,0:T(8,128)(2,1)S(1)}, bf16[2,384,192]{2,1,0:T(8,128)(2,1)}, u32[]{:S(2)}) copy-start(bf16[2,384,192]{2,1,0:T(8,128)(2,1)} %constant.20.clone.rows) | copy-start | bytes 884740
  113.0 14.2 %copy-start.6 = (bf16[128,128]{1,0:T(8,128)(2,1)S(1)}, bf16[128,128]{1,0:T(8,128)(2,1)}, u32[]{:S(2)}) copy-start(bf16[128,128]{1,0:T(8,128)(2,1)} %w_out.3) | copy-start | bytes 98308

commit v9 on v8

--- a/solution.py
+++ b/solution.py
@@ -131,20 +131,20 @@
             out[x * 4 + y] = fold(piece).astype(BF16)
 
 
-def outgoing_kernel(core, own, both, left_order, right_order, rows, out):
+def by_zh(side):
+    starts = [c * PAIRS + y * 16 + zh * 4 for zh in range(4) for y in range(4) for c in range(2)]
+    return jnp.concatenate([side[i : i + 4] for i in starts], axis=0)
+
+
+def outgoing_kernel(core, own, both, rows, out):
     left = own[:, 0, :].astype(F32)
-    left = jnp.concatenate([left[:, :TILE], left[:, TILE:]], axis=0).astype(BF16)
-    left = chunks(jnp.dot(left_order[...], left, preferred_element_type=F32), COLS)
+    left = by_zh(jnp.concatenate([left[:, :TILE], left[:, TILE:]], axis=0))
+    left = chunks(left, COLS)
     first = lax.broadcasted_iota(jnp.int32, left.shape, 0) % 8 < 4
     left = jnp.concatenate([jnp.where(first, left, 0.0), jnp.where(first, 0.0, left)], axis=1).astype(BF16)
-    right = jnp.dot(right_order[...], both[:, 1, :], preferred_element_type=F32)
+    right = by_zh(both[:, 1, :].astype(F32))
     right = jnp.concatenate([chunks(right[:, :TILE], COLS), chunks(right[:, TILE:], COLS)], axis=1)
-    blocks = []
-    for zl in range(4):
-        block = [right[i * 32 + zl * 8 : i * 32 + (zl + 1) * 8] for i in range(ROWS)]
-        block = jnp.concatenate(block, axis=0).astype(BF16)
-        blocks.append(jnp.dot(rows[...], block, preferred_element_type=F32))
-    right = jnp.concatenate(blocks, axis=0).astype(BF16)
+    right = jnp.dot(rows[...], right.astype(BF16), preferred_element_type=F32).astype(BF16)
     sums = lax.dot_general(left, right, (((1,), (1,)), ((), ())), preferred_element_type=F32)
     pack(sums, out)
 
@@ -181,17 +181,17 @@
     pack(sums, out)
 
 
-def add_kernel(added, got, order, out):
+def add_kernel(added, got, out):
     parts = []
     for i in range(4):
         total = 0.0
         for j in range(4):
             total += got[j * 4 + i if added == 0 else i * 4 + j].astype(F32)
         parts.append(unfold(total))
-    total = jnp.concatenate(parts, axis=1).astype(BF16)
-    total = jnp.dot(order[...], total, preferred_element_type=F32).astype(BF16)
+    total = jnp.concatenate(parts, axis=1)
     for i in range(2):
-        out[:, i, :] = total[i * 16 : (i + 1) * 16]
+        rows = [total[zh * 8 + i * 4 : zh * 8 + i * 4 + 4] for zh in range(4)]
+        out[:, i, :] = jnp.concatenate(rows, axis=0).astype(BF16)
 
 
 def call(kernel, name, n_in, *shapes, scalars=0):
@@ -240,16 +240,13 @@
     out_norm_gain, out_final_gain, in_norm_gain, in_final_gain = (
         g.reshape(1, WIDTH) for g in (out_norm_gain, out_final_gain, in_norm_gain, in_final_gain)
     )
-    left_order = one_hot(reorder((2, 4, 4, 4), (2, 1, 0, 3)))
-    right_order = one_hot(reorder((2, 4, 4, 4), (2, 3, 1, 0)))
-    out_rows = one_hot(reorder((ROWS, 8), (1, 0)))
-    piece_order = one_hot(reorder((4, 2, 4), (1, 0, 2)))
+    out_rows = one_hot(reorder((ROWS, 4, 2, 4), (3, 1, 2, 0)))
     place = np.full((2, ROWS, 4, 2, 4), -1)
     for i in range(2):
         place[i, :, :, i, :] = reorder((4, 4, ROWS), (2, 1, 0))
     in_rows = np.stack([one_hot(place[i], 16 * ROWS) for i in range(2)])
-    left_order, right_order, out_rows, piece_order, in_rows = (
-        jnp.asarray(t) for t in (left_order, right_order, out_rows, piece_order, in_rows)
+    out_rows, in_rows = (
+        jnp.asarray(t) for t in (out_rows, in_rows)
     )
     core = lax.axis_index("core").reshape(1).astype(jnp.int32)
 
@@ -260,7 +257,7 @@
     def collect(pieces, added):
         got = lax.all_to_all(pieces, PLANE, 0, 0, tiled=True)
         add = functools.partial(add_kernel, added)
-        sums = call(add, "add_parts", 2, (16, 2, 4 * TILE))(got, piece_order)
+        sums = call(add, "add_parts", 1, (16, 2, 4 * TILE))(got)
         return lax.all_to_all(sums, LINE, 0, 0, tiled=True)
 
     pair = pair_input.reshape(TILE, WIDTH)
@@ -274,7 +271,7 @@
         out_w_in,
     )
     own, both = spread(sent, OUT_CHANNEL)
-    pieces = call(outgoing_kernel, "outgoing", 6, (16, 72, 128), scalars=1)(core, own, both, left_order, right_order, out_rows)
+    pieces = call(outgoing_kernel, "outgoing", 4, (16, 72, 128), scalars=1)(core, own, both, out_rows)
     tri = collect(pieces, 0)
 
     middle, sent = call(middle_kernel, "middle", 7, (TILE, WIDTH), (PAIRS, 2, 2 * TILE))(

time: 130 us -> 129 us (level)
  no operation moved by 1% of the time
where the time goes in v9:
time: 129 us; the launch traced here: 128 us
  blocking collectives  84.6 us (66%)
  starting transfers between devices  19.3 us (15%)
  waiting for transfers between devices  15.1 us (12%)
  Pallas kernels  8.79 us (7%)
    all_to_all x2, blocking collectives, collect(): return lax.all_to_all(sums, LINE, 0, 0, tiled=True)  28.6 us
    all_to_all x2, blocking collectives, collect(): got = lax.all_to_all(pieces, PLANE, 0, 0, tiled=True)  26.3 us
    all_to_all x1, starting transfers between devices, spread(): got = lax.all_to_all(sent, order, 0, 0, tiled=True)  19.3 us
    all_to_all x1, blocking collectives, spread(): got = lax.all_to_all(sent, order, 0, 0, tiled=True)  19.2 us
    all_to_all x1, waiting for transfers between devices, spread(): got = lax.all_to_all(sent, order, 0, 0, tiled=True)  15.1 us
    all_gather x2, blocking collectives, spread(): return (got, lax.all_gather(got, 'core', tiled=True))  10.4 us
  transfers between devices with their start and end apart: 1, of which 1 were waited for; matrix products, arithmetic and copies ran while one was open for 0% of the time, Pallas kernels for 0%

profile of v9, /device:TPU:1, one launch (start us, length us, event | category | flops | bytes accessed | tf_op | source)
XLA Modules:
  0.0 127.9 jit_solution(9955278355223772125)
XLA Ops:
  0.0 2.3 %project_first.1 = (bf16[64,2,576]{2,1,0:T(2,128)(2,1)}, f32[4,128]{1,0:T(4,128)}) custom-call(bf16[288,128]{1,0:T(8,128)(2,1)} %bitcast.7, s32[12,24]{1,0:T(8,128)} %mask.1, f32[1,128]{1,0:T(1,128)} %bitcast.9, f32[1,128]{1,0:T(1,128)} %bitcast.10, f32[1,128]{1,0:T(1,128)} %bitcast.11, f32[1,128]{1,0:T(1,128)} %bitcast.12, bf16[128,640]{1,0:T(8,128)(2,1)} %w_in.4), custom_call_target="tpu_custom_call" | custom-call | tf_op jit(solution)/shard_map/project_first/pallas_call | solution.py:210
  2.3 19.3 %all-to-all-start = ((bf16[64,2,576]{2,1,0:T(2,128)(2,1)}), bf16[64,2,576]{2,1,0:T(2,128)(2,1)S(1)}, u32[]{:S(2)}, u32[]{:S(2)}) async-start(bf16[64,2,576]{2,1,0:T(2,128)(2,1)} %get-tuple-element.9), calls=%async_computation | async-start | bytes 327680 | tf_op jit(solution)/shard_map/all_to_all | solution.py:254
  21.6 0.0 copy-start.3
  21.6 15.1 %all-to-all-done.own = bf16[64,2,576]{2,1,0:T(2,128)(2,1)S(1)} async-done(((bf16[64,2,576]{2,1,0:T(2,128)(2,1)}), bf16[64,2,576]{2,1,0:T(2,128)(2,1)S(1)}, u32[]{:S(2)}, u32[]{:S(2)}) %all-to-all-start) | async-done | bytes 147488 | tf_op jit(solution)/shard_map/all_to_all | solution.py:254
  36.7 4.4 %all_gather.6.both = bf16[128,2,576]{2,1,0:T(2,128)(2,1)S(1)} all-gather(bf16[64,2,576]{2,1,0:T(2,128)(2,1)S(1)} %all-to-all-done.own), channel_id=1, replica_groups=mesh['zl'=4,'y'=4,'core'=2,'x'=4,'zh'=4] {'core'}, dimensions={0}, use_global_device_ids=true | all-gather | bytes 442368 | tf_op jit(solution)/shard_map/all_gather | solution.py:255
  41.1 0.0 copy-done.3
  41.1 1.7 %outgoing.1 = bf16[16,72,128]{2,1,0:T(8,128)(2,1)S(1)} custom-call(s32[1]{0:T(128)} %bitcast.1.core, bf16[64,2,576]{2,1,0:T(2,128)(2,1)S(1)} %all-to-all-done.own, bf16[128,2,576]{2,1,0:T(2,128)(2,1)S(1)} %all_gather.6.both, bf16[384,384]{1,0:T(8,128)(2,1)S(1)} %copy-done.3), custom_call_target="tpu_custom_call" | custom-call | tf_op jit(solution)/shard_map/outgoing/pallas_call | solution.py:274
  42.8 14.1 %all_to_all.30.got = bf16[16,72,128]{2,1,0:T(8,128)(2,1)S(1)} all-to-all(bf16[16,72,128]{2,1,0:T(8,128)(2,1)S(1)} %outgoing.1), channel_id=1, replica_groups=mesh['zl'=4,'y'=4,'core'=2,'x'=4,'zh'=4] {'x','y'}, dimensions={0} | all-to-all | bytes 589824 | tf_op jit(solution)/shard_map/all_to_all | solution.py:258
  56.9 0.0 copy-start
  57.0 0.0 copy-start.1
  57.0 0.2 add_parts.2
  57.2 0.0 copy-start.4
  57.2 0.0 copy-start.5
  57.2 0.0 copy-start.6
  57.2 0.0 copy-start.8
  57.2 14.4 %all_to_all.31.tri = bf16[16,2,1152]{2,1,0:T(2,128)(2,1)S(1)} all-to-all(bf16[16,2,1152]{2,1,0:T(2,128)(2,1)S(1)} %add_parts.2), channel_id=1, replica_groups=mesh['zl'=4,'y'=4,'core'=2,'x'=4,'zh'=4] {'zh','zl'}, dimensions={0} | all-to-all | bytes 147456 | tf_op jit(solution)/shard_map/all_to_all | solution.py:261
  71.6 0.0 copy-done
  71.6 0.0 copy-done.1
  71.6 0.0 copy-done.4
  71.6 0.0 copy-done.5
  71.6 0.0 copy-done.6
  71.6 0.0 copy-done.8
  71.6 1.2 middle.1
  72.9 0.0 copy-start.2
  72.9 19.2 %all_to_all.32 = bf16[64,2,576]{2,1,0:T(2,128)(2,1)S(1)} all-to-all(bf16[64,2,576]{2,1,0:T(2,128)(2,1)S(1)} %get-tuple-element.12), channel_id=1, replica_groups=mesh['zl'=4,'y'=4,'core'=2,'x'=4,'zh'=4] {'x','zh','zl'}, dimensions={0} | all-to-all | bytes 294912 | tf_op jit(solution)/shard_map/all_to_all | solution.py:254
  92.1 6.1 %all_gather.7.both = bf16[128,2,576]{2,1,0:T(2,128)(2,1)S(1)} all-gather(bf16[64,2,576]{2,1,0:T(2,128)(2,1)S(1)} %all_to_all.32), channel_id=1, replica_groups=mesh['zl'=4,'y'=4,'core'=2,'x'=4,'zh'=4] {'core'}, dimensions={0}, use_global_device_ids=true | all-gather | bytes 442368 | tf_op jit(solution)/shard_map/all_gather | solution.py:255
  98.1 0.0 copy-done.2
  98.1 2.0 %incoming.1 = bf16[16,72,128]{2,1,0:T(8,128)(2,1)S(1)} custom-call(s32[1]{0:T(128)} %bitcast.1.core, bf16[128,2,576]{2,1,0:T(2,128)(2,1)S(1)} %all_gather.7.both, bf16[2,384,192]{2,1,0:T(8,128)(2,1)S(1)} %copy-done.2), custom_call_target="tpu_custom_call" | custom-call | tf_op jit(solution)/shard_map/incoming/pallas_call | solution.py:281
  100.1 12.2 %all_to_all.33.got = bf16[16,72,128]{2,1,0:T(8,128)(2,1)S(1)} all-to-all(bf16[16,72,128]{2,1,0:T(8,128)(2,1)S(1)} %incoming.1), channel_id=1, replica_groups=mesh['zl'=4,'y'=4,'core'=2,'x'=4,'zh'=4] {'x','y'}, dimensions={0} | all-to-all | bytes 589824 | tf_op jit(solution)/shard_map/all_to_all | solution.py:258
  112.3 0.2 add_parts.3
  112.5 0.0 copy-start.7
  112.5 14.2 %all_to_all.34.tri = bf16[16,2,1152]{2,1,0:T(2,128)(2,1)S(1)} all-to-all(bf16[16,2,1152]{2,1,0:T(2,128)(2,1)S(1)} %add_parts.3), channel_id=1, replica_groups=mesh['zl'=4,'y'=4,'core'=2,'x'=4,'zh'=4] {'zh','zl'}, dimensions={0} | all-to-all | bytes 147456 | tf_op jit(solution)/shard_map/all_to_all | solution.py:261
  126.7 0.0 copy-done.7
  126.7 1.2 last.1
Async XLA Ops:
  2.3 34.4 %all-to-all-start = ((bf16[64,2,576]{2,1,0:T(2,128)(2,1)}), bf16[64,2,576]{2,1,0:T(2,128)(2,1)S(1)}, u32[]{:S(2)}, u32[]{:S(2)}) async-start(bf16[64,2,576]{2,1,0:T(2,128)(2,1)} %get-tuple-element.9), calls=%async_computation | async-start | bytes 327680 | tf_op jit(solution)/shard_map/all_to_all | solution.py:254
  21.6 19.5 %copy-start.3 = (bf16[384,384]{1,0:T(8,128)(2,1)S(1)}, bf16[384,384]{1,0:T(8,128)(2,1)}, u32[]{:S(2)}) copy-start(bf16[384,384]{1,0:T(8,128)(2,1)} %constant.10.clone.rows) | copy-start | bytes 884740
  56.9 14.6 %copy-start = (bf16[128,640]{1,0:T(8,128)(2,1)S(1)}, bf16[128,640]{1,0:T(8,128)(2,1)}, u32[]{:S(2)}) copy-start(bf16[128,640]{1,0:T(8,128)(2,1)} %w_in.5) | copy-start | bytes 491524
  57.0 14.6 %copy-start.1 = (bf16[128,640]{1,0:T(8,128)(2,1)S(1)}, bf16[128,640]{1,0:T(8,128)(2,1)}, u32[]{:S(2)}) copy-start(bf16[128,640]{1,0:T(8,128)(2,1)} %w_in.4) | copy-start | bytes 491524
  57.2 14.4 %copy-start.4 = (bf16[12,24,128]{2,1,0:T(8,128)(2,1)S(1)}, bf16[12,24,128]{2,1,0:T(8,128)(2,1)}, u32[]{:S(2)}) copy-start(bf16[12,24,128]{2,1,0:T(8,128)(2,1)} %param.12) | copy-start | bytes 221188
  57.2 14.4 %copy-start.5 = (s32[12,24]{1,0:T(8,128)S(1)}, s32[12,24]{1,0:T(8,128)}, u32[]{:S(2)}) copy-start(s32[12,24]{1,0:T(8,128)} %mask.1) | copy-start | bytes 3460
  57.2 14.4 %copy-start.6 = (bf16[128,128]{1,0:T(8,128)(2,1)S(1)}, bf16[128,128]{1,0:T(8,128)(2,1)}, u32[]{:S(2)}) copy-start(bf16[128,128]{1,0:T(8,128)(2,1)} %w_out.2) | copy-start | bytes 98308
  57.2 14.4 %copy-start.8 = (f32[4,128]{1,0:T(4,128)S(1)}, f32[4,128]{1,0:T(4,128)}, u32[]{:S(2)}) copy-start(f32[4,128]{1,0:T(4,128)} %get-tuple-element.10.gains) | copy-start | bytes 6148
  72.9 25.3 %copy-start.2 = (bf16[2,384,192]{2,1,0:T(8,128)(2,1)S(1)}, bf16[2,384,192]{2,1,0:T(8,128)(2,1)}, u32[]{:S(2)}) copy-start(bf16[2,384,192]{2,1,0:T(8,128)(2,1)} %constant.11.clone.rows) | copy-start | bytes 884740
  112.5 14.3 %copy-start.7 = (bf16[128,128]{1,0:T(8,128)(2,1)S(1)}, bf16[128,128]{1,0:T(8,128)(2,1)}, u32[]{:S(2)}) copy-start(bf16[128,128]{1,0:T(8,128)(2,1)} %w_out.3) | copy-start | bytes 98308

commit v10 on v9

--- a/solution.py
+++ b/solution.py
@@ -171,10 +171,13 @@
     left = jnp.where(core[0] == 0, left, jnp.concatenate([left[:, ROWS:], left[:, :ROWS]], axis=1))
     left = [operand(left[:, i * TILE : (i + 1) * TILE], COLS // 2) for i in range(2)]
     left = [
-        lax.dot_general(rows[i], left[i], (((1,), (1,)), ((), ())), preferred_element_type=F32)
+        lax.dot_general(rows[...], left[i], (((1,), (1,)), ((), ())), preferred_element_type=F32)
         for i in range(2)
     ]
-    left = jnp.concatenate(left, axis=1).astype(BF16)
+    zero = jnp.zeros_like(left[0])
+    left = [jnp.concatenate([left[0], zero], axis=1), jnp.concatenate([zero, left[1]], axis=1)]
+    left = [v[g * 4 : (g + 1) * 4] for g in range(4 * ROWS) for v in left]
+    left = jnp.concatenate(left, axis=0).astype(BF16)
     right = by_column(both[:, 1, :].astype(F32))
     right = [operand(right[:, i * TILE : (i + 1) * TILE], COLS) for i in range(2)]
     sums = jnp.dot(left, jnp.concatenate(right, axis=0), preferred_element_type=F32)
@@ -241,10 +244,7 @@
         g.reshape(1, WIDTH) for g in (out_norm_gain, out_final_gain, in_norm_gain, in_final_gain)
     )
     out_rows = one_hot(reorder((ROWS, 4, 2, 4), (3, 1, 2, 0)))
-    place = np.full((2, ROWS, 4, 2, 4), -1)
-    for i in range(2):
-        place[i, :, :, i, :] = reorder((4, 4, ROWS), (2, 1, 0))
-    in_rows = np.stack([one_hot(place[i], 16 * ROWS) for i in range(2)])
+    in_rows = one_hot(reorder((4, 4, ROWS), (2, 1, 0)))
     out_rows, in_rows = (
         jnp.asarray(t) for t in (out_rows, in_rows)
     )

time: 129 us -> 129 us (level)
  no operation moved by 1% of the time
where the time goes in v10:
time: 129 us; the launch traced here: 128 us
  blocking collectives  84.6 us (66%)
  starting transfers between devices  19.3 us (15%)
  waiting for transfers between devices  15.1 us (12%)
  Pallas kernels  8.73 us (7%)
    all_to_all x2, blocking collectives, collect(): return lax.all_to_all(sums, LINE, 0, 0, tiled=True)  28.6 us
    all_to_all x2, blocking collectives, collect(): got = lax.all_to_all(pieces, PLANE, 0, 0, tiled=True)  26.3 us
    all_to_all x1, starting transfers between devices, spread(): got = lax.all_to_all(sent, order, 0, 0, tiled=True)  19.3 us
    all_to_all x1, blocking collectives, spread(): got = lax.all_to_all(sent, order, 0, 0, tiled=True)  19.1 us
    all_to_all x1, waiting for transfers between devices, spread(): got = lax.all_to_all(sent, order, 0, 0, tiled=True)  15.1 us
    all_gather x2, blocking collectives, spread(): return (got, lax.all_gather(got, 'core', tiled=True))  10.6 us
  transfers between devices with their start and end apart: 1, of which 1 were waited for; matrix products, arithmetic and copies ran while one was open for 0% of the time, Pallas kernels for 0%

profile of v10, /device:TPU:1, one launch (start us, length us, event | category | flops | bytes accessed | tf_op | source)
XLA Modules:
  0.0 127.9 jit_solution(10539461224740049990)
XLA Ops:
  0.0 2.3 %project_first.1 = (bf16[64,2,576]{2,1,0:T(2,128)(2,1)}, f32[4,128]{1,0:T(4,128)}) custom-call(bf16[288,128]{1,0:T(8,128)(2,1)} %bitcast.7, s32[12,24]{1,0:T(8,128)} %mask.1, f32[1,128]{1,0:T(1,128)} %bitcast.9, f32[1,128]{1,0:T(1,128)} %bitcast.10, f32[1,128]{1,0:T(1,128)} %bitcast.11, f32[1,128]{1,0:T(1,128)} %bitcast.12, bf16[128,640]{1,0:T(8,128)(2,1)} %w_in.4), custom_call_target="tpu_custom_call" | custom-call | tf_op jit(solution)/shard_map/project_first/pallas_call | solution.py:213
  2.3 19.3 %all-to-all-start = ((bf16[64,2,576]{2,1,0:T(2,128)(2,1)}), bf16[64,2,576]{2,1,0:T(2,128)(2,1)S(1)}, u32[]{:S(2)}, u32[]{:S(2)}) async-start(bf16[64,2,576]{2,1,0:T(2,128)(2,1)} %get-tuple-element.9), calls=%async_computation | async-start | bytes 327680 | tf_op jit(solution)/shard_map/all_to_all | solution.py:254
  21.6 0.0 copy-start.2
  21.6 15.1 %all-to-all-done.own = bf16[64,2,576]{2,1,0:T(2,128)(2,1)S(1)} async-done(((bf16[64,2,576]{2,1,0:T(2,128)(2,1)}), bf16[64,2,576]{2,1,0:T(2,128)(2,1)S(1)}, u32[]{:S(2)}, u32[]{:S(2)}) %all-to-all-start) | async-done | bytes 147488 | tf_op jit(solution)/shard_map/all_to_all | solution.py:254
  36.7 4.4 %all_gather.6.both = bf16[128,2,576]{2,1,0:T(2,128)(2,1)S(1)} all-gather(bf16[64,2,576]{2,1,0:T(2,128)(2,1)S(1)} %all-to-all-done.own), channel_id=1, replica_groups=mesh['zl'=4,'y'=4,'core'=2,'x'=4,'zh'=4] {'core'}, dimensions={0}, use_global_device_ids=true | all-gather | bytes 442368 | tf_op jit(solution)/shard_map/all_gather | solution.py:255
  41.1 0.0 copy-done.2
  41.1 1.7 %outgoing.1 = bf16[16,72,128]{2,1,0:T(8,128)(2,1)S(1)} custom-call(s32[1]{0:T(128)} %bitcast.1.core, bf16[64,2,576]{2,1,0:T(2,128)(2,1)S(1)} %all-to-all-done.own, bf16[128,2,576]{2,1,0:T(2,128)(2,1)S(1)} %all_gather.6.both, bf16[384,384]{1,0:T(8,128)(2,1)S(1)} %copy-done.2), custom_call_target="tpu_custom_call" | custom-call | tf_op jit(solution)/shard_map/outgoing/pallas_call | solution.py:274
  42.8 14.1 %all_to_all.30.got = bf16[16,72,128]{2,1,0:T(8,128)(2,1)S(1)} all-to-all(bf16[16,72,128]{2,1,0:T(8,128)(2,1)S(1)} %outgoing.1), channel_id=1, replica_groups=mesh['zl'=4,'y'=4,'core'=2,'x'=4,'zh'=4] {'x','y'}, dimensions={0} | all-to-all | bytes 589824 | tf_op jit(solution)/shard_map/all_to_all | solution.py:258
  56.9 0.0 copy-start
  57.0 0.0 copy-start.1
  57.0 0.2 add_parts.2
  57.2 0.0 copy-start.3
  57.2 0.0 copy-start.5
  57.2 0.0 copy-start.6
  57.2 0.0 copy-start.8
  57.2 14.4 %all_to_all.31.tri = bf16[16,2,1152]{2,1,0:T(2,128)(2,1)S(1)} all-to-all(bf16[16,2,1152]{2,1,0:T(2,128)(2,1)S(1)} %add_parts.2), channel_id=1, replica_groups=mesh['zl'=4,'y'=4,'core'=2,'x'=4,'zh'=4] {'zh','zl'}, dimensions={0} | all-to-all | bytes 147456 | tf_op jit(solution)/shard_map/all_to_all | solution.py:261
  71.6 0.0 copy-done
  71.6 0.0 copy-done.1
  71.6 0.0 copy-done.3
  71.6 0.0 copy-done.5
  71.6 0.0 copy-done.6
  71.6 0.0 copy-done.8
  71.6 1.2 middle.1
  72.9 19.1 %all_to_all.32 = bf16[64,2,576]{2,1,0:T(2,128)(2,1)S(1)} all-to-all(bf16[64,2,576]{2,1,0:T(2,128)(2,1)S(1)} %get-tuple-element.12), channel_id=1, replica_groups=mesh['zl'=4,'y'=4,'core'=2,'x'=4,'zh'=4] {'x','zh','zl'}, dimensions={0} | all-to-all | bytes 294912 | tf_op jit(solution)/shard_map/all_to_all | solution.py:254
  91.9 0.0 copy-start.4
  91.9 6.2 %all_gather.7.both = bf16[128,2,576]{2,1,0:T(2,128)(2,1)S(1)} all-gather(bf16[64,2,576]{2,1,0:T(2,128)(2,1)S(1)} %all_to_all.32), channel_id=1, replica_groups=mesh['zl'=4,'y'=4,'core'=2,'x'=4,'zh'=4] {'core'}, dimensions={0}, use_global_device_ids=true | all-gather | bytes 442368 | tf_op jit(solution)/shard_map/all_gather | solution.py:255
  98.1 0.0 copy-done.4
  98.1 1.9 %incoming.1 = bf16[16,72,128]{2,1,0:T(8,128)(2,1)S(1)} custom-call(s32[1]{0:T(128)} %bitcast.1.core, bf16[128,2,576]{2,1,0:T(2,128)(2,1)S(1)} %all_gather.7.both, bf16[192,192]{1,0:T(8,128)(2,1)S(1)} %copy-done.4), custom_call_target="tpu_custom_call" | custom-call | tf_op jit(solution)/shard_map/incoming/pallas_call | solution.py:281
  100.0 12.2 %all_to_all.33.got = bf16[16,72,128]{2,1,0:T(8,128)(2,1)S(1)} all-to-all(bf16[16,72,128]{2,1,0:T(8,128)(2,1)S(1)} %incoming.1), channel_id=1, replica_groups=mesh['zl'=4,'y'=4,'core'=2,'x'=4,'zh'=4] {'x','y'}, dimensions={0} | all-to-all | bytes 589824 | tf_op jit(solution)/shard_map/all_to_all | solution.py:258
  112.2 0.2 add_parts.3
  112.4 0.0 copy-start.7
  112.4 14.2 %all_to_all.34.tri = bf16[16,2,1152]{2,1,0:T(2,128)(2,1)S(1)} all-to-all(bf16[16,2,1152]{2,1,0:T(2,128)(2,1)S(1)} %add_parts.3), channel_id=1, replica_groups=mesh['zl'=4,'y'=4,'core'=2,'x'=4,'zh'=4] {'zh','zl'}, dimensions={0} | all-to-all | bytes 147456 | tf_op jit(solution)/shard_map/all_to_all | solution.py:261
  126.7 0.0 copy-done.7
  126.7 1.2 last.1
Async XLA Ops:
  2.3 34.4 %all-to-all-start = ((bf16[64,2,576]{2,1,0:T(2,128)(2,1)}), bf16[64,2,576]{2,1,0:T(2,128)(2,1)S(1)}, u32[]{:S(2)}, u32[]{:S(2)}) async-start(bf16[64,2,576]{2,1,0:T(2,128)(2,1)} %get-tuple-element.9), calls=%async_computation | async-start | bytes 327680 | tf_op jit(solution)/shard_map/all_to_all | solution.py:254
  21.6 19.5 %copy-start.2 = (bf16[384,384]{1,0:T(8,128)(2,1)S(1)}, bf16[384,384]{1,0:T(8,128)(2,1)}, u32[]{:S(2)}) copy-start(bf16[384,384]{1,0:T(8,128)(2,1)} %constant.10.clone.rows) | copy-start | bytes 884740
  56.9 14.6 %copy-start = (bf16[128,640]{1,0:T(8,128)(2,1)S(1)}, bf16[128,640]{1,0:T(8,128)(2,1)}, u32[]{:S(2)}) copy-start(bf16[128,640]{1,0:T(8,128)(2,1)} %w_in.5) | copy-start | bytes 491524
  57.0 14.6 %copy-start.1 = (bf16[128,640]{1,0:T(8,128)(2,1)S(1)}, bf16[128,640]{1,0:T(8,128)(2,1)}, u32[]{:S(2)}) copy-start(bf16[128,640]{1,0:T(8,128)(2,1)} %w_in.4) | copy-start | bytes 491524
  57.2 14.4 %copy-start.3 = (bf16[12,24,128]{2,1,0:T(8,128)(2,1)S(1)}, bf16[12,24,128]{2,1,0:T(8,128)(2,1)}, u32[]{:S(2)}) copy-start(bf16[12,24,128]{2,1,0:T(8,128)(2,1)} %param.12) | copy-start | bytes 221188
  57.2 14.4 %copy-start.5 = (s32[12,24]{1,0:T(8,128)S(1)}, s32[12,24]{1,0:T(8,128)}, u32[]{:S(2)}) copy-start(s32[12,24]{1,0:T(8,128)} %mask.1) | copy-start | bytes 3460
  57.2 14.4 %copy-start.6 = (bf16[128,128]{1,0:T(8,128)(2,1)S(1)}, bf16[128,128]{1,0:T(8,128)(2,1)}, u32[]{:S(2)}) copy-start(bf16[128,128]{1,0:T(8,128)(2,1)} %w_out.2) | copy-start | bytes 98308
  57.2 14.4 %copy-start.8 = (f32[4,128]{1,0:T(4,128)S(1)}, f32[4,128]{1,0:T(4,128)}, u32[]{:S(2)}) copy-start(f32[4,128]{1,0:T(4,128)} %get-tuple-element.10.gains) | copy-start | bytes 6148
  91.9 6.2 %copy-start.4 = (bf16[192,192]{1,0:T(8,128)(2,1)S(1)}, bf16[192,192]{1,0:T(8,128)(2,1)}, u32[]{:S(2)}) copy-start(bf16[192,192]{1,0:T(8,128)(2,1)} %constant.11.clone.rows) | copy-start | bytes 221188
  112.4 14.3 %copy-start.7 = (bf16[128,128]{1,0:T(8,128)(2,1)S(1)}, bf16[128,128]{1,0:T(8,128)(2,1)}, u32[]{:S(2)}) copy-start(bf16[128,128]{1,0:T(8,128)(2,1)} %w_out.3) | copy-start | bytes 98308

commit v11 on v10

--- a/solution.py
+++ b/solution.py
@@ -144,7 +144,13 @@
     left = jnp.concatenate([jnp.where(first, left, 0.0), jnp.where(first, 0.0, left)], axis=1).astype(BF16)
     right = by_zh(both[:, 1, :].astype(F32))
     right = jnp.concatenate([chunks(right[:, :TILE], COLS), chunks(right[:, TILE:], COLS)], axis=1)
-    right = jnp.dot(rows[...], right.astype(BF16), preferred_element_type=F32).astype(BF16)
+    blocks = []
+    for y in range(4):
+        block = [right[i * 32 + y * 8 : i * 32 + (y + 1) * 8] for i in range(ROWS)]
+        block = jnp.concatenate(block, axis=0).astype(BF16)
+        blocks.append(jnp.dot(rows[...], block, preferred_element_type=F32))
+    right = [b[zl * 24 : (zl + 1) * 24] for zl in range(4) for b in blocks]
+    right = jnp.concatenate(right, axis=0).astype(BF16)
     sums = lax.dot_general(left, right, (((1,), (1,)), ((), ())), preferred_element_type=F32)
     pack(sums, out)
 
@@ -243,7 +249,7 @@
     out_norm_gain, out_final_gain, in_norm_gain, in_final_gain = (
         g.reshape(1, WIDTH) for g in (out_norm_gain, out_final_gain, in_norm_gain, in_final_gain)
     )
-    out_rows = one_hot(reorder((ROWS, 4, 2, 4), (3, 1, 2, 0)))
+    out_rows = one_hot(reorder((ROWS, 2, 4), (2, 1, 0)))
     in_rows = one_hot(reorder((4, 4, ROWS), (2, 1, 0)))
     out_rows, in_rows = (
         jnp.asarray(t) for t in (out_rows, in_rows)

time: 129 us -> 129 us (level)
  no operation moved by 1% of the time
where the time goes in v11:
time: 129 us; the launch traced here: 128 us
  blocking collectives  84.6 us (66%)
  starting transfers between devices  19.3 us (15%)
  waiting for transfers between devices  15.1 us (12%)
  Pallas kernels  8.78 us (7%)
    all_to_all x2, blocking collectives, collect(): return lax.all_to_all(sums, LINE, 0, 0, tiled=True)  28.6 us
    all_to_all x2, blocking collectives, collect(): got = lax.all_to_all(pieces, PLANE, 0, 0, tiled=True)  26.3 us
    all_to_all x1, starting transfers between devices, spread(): got = lax.all_to_all(sent, order, 0, 0, tiled=True)  19.3 us
    all_to_all x1, blocking collectives, spread(): got = lax.all_to_all(sent, order, 0, 0, tiled=True)  19 us
    all_to_all x1, waiting for transfers between devices, spread(): got = lax.all_to_all(sent, order, 0, 0, tiled=True)  15.1 us
    all_gather x2, blocking collectives, spread(): return (got, lax.all_gather(got, 'core', tiled=True))  10.6 us
  transfers between devices with their start and end apart: 1, of which 1 were waited for; matrix products, arithmetic and copies ran while one was open for 0% of the time, Pallas kernels for 0%

profile of v11, /device:TPU:1, one launch (start us, length us, event | category | flops | bytes accessed | tf_op | source)
XLA Modules:
  0.0 127.9 jit_solution(5574471908064625187)
XLA Ops:
  0.0 2.3 %project_first.1 = (bf16[64,2,576]{2,1,0:T(2,128)(2,1)}, f32[4,128]{1,0:T(4,128)}) custom-call(bf16[288,128]{1,0:T(8,128)(2,1)} %bitcast.7, s32[12,24]{1,0:T(8,128)} %mask.1, f32[1,128]{1,0:T(1,128)} %bitcast.9, f32[1,128]{1,0:T(1,128)} %bitcast.10, f32[1,128]{1,0:T(1,128)} %bitcast.11, f32[1,128]{1,0:T(1,128)} %bitcast.12, bf16[128,640]{1,0:T(8,128)(2,1)} %w_in.4), custom_call_target="tpu_custom_call" | custom-call | tf_op jit(solution)/shard_map/project_first/pallas_call | solution.py:219
  2.3 19.3 %all-to-all-start = ((bf16[64,2,576]{2,1,0:T(2,128)(2,1)}), bf16[64,2,576]{2,1,0:T(2,128)(2,1)S(1)}, u32[]{:S(2)}, u32[]{:S(2)}) async-start(bf16[64,2,576]{2,1,0:T(2,128)(2,1)} %get-tuple-element.9), calls=%async_computation | async-start | bytes 327680 | tf_op jit(solution)/shard_map/all_to_all | solution.py:260
  21.6 0.0 copy-start.7
  21.6 15.1 %all-to-all-done.own = bf16[64,2,576]{2,1,0:T(2,128)(2,1)S(1)} async-done(((bf16[64,2,576]{2,1,0:T(2,128)(2,1)}), bf16[64,2,576]{2,1,0:T(2,128)(2,1)S(1)}, u32[]{:S(2)}, u32[]{:S(2)}) %all-to-all-start) | async-done | bytes 147488 | tf_op jit(solution)/shard_map/all_to_all | solution.py:260
  36.7 4.4 %all_gather.6.both = bf16[128,2,576]{2,1,0:T(2,128)(2,1)S(1)} all-gather(bf16[64,2,576]{2,1,0:T(2,128)(2,1)S(1)} %all-to-all-done.own), channel_id=1, replica_groups=mesh['zl'=4,'y'=4,'core'=2,'x'=4,'zh'=4] {'core'}, dimensions={0}, use_global_device_ids=true | all-gather | bytes 442368 | tf_op jit(solution)/shard_map/all_gather | solution.py:261
  41.1 0.0 copy-done.7
  41.1 1.8 %outgoing.1 = bf16[16,72,128]{2,1,0:T(8,128)(2,1)S(1)} custom-call(s32[1]{0:T(128)} %bitcast.1.core, bf16[64,2,576]{2,1,0:T(2,128)(2,1)S(1)} %all-to-all-done.own, bf16[128,2,576]{2,1,0:T(2,128)(2,1)S(1)} %all_gather.6.both, bf16[96,96]{1,0:T(8,128)(2,1)S(1)} %copy-done.7), custom_call_target="tpu_custom_call" | custom-call | tf_op jit(solution)/shard_map/outgoing/pallas_call | solution.py:280
  42.9 14.1 %all_to_all.30.got = bf16[16,72,128]{2,1,0:T(8,128)(2,1)S(1)} all-to-all(bf16[16,72,128]{2,1,0:T(8,128)(2,1)S(1)} %outgoing.1), channel_id=1, replica_groups=mesh['zl'=4,'y'=4,'core'=2,'x'=4,'zh'=4] {'x','y'}, dimensions={0} | all-to-all | bytes 589824 | tf_op jit(solution)/shard_map/all_to_all | solution.py:264
  57.0 0.0 copy-start
  57.0 0.0 copy-start.1
  57.0 0.2 add_parts.2
  57.2 0.0 copy-start.2
  57.2 0.0 copy-start.4
  57.2 0.0 copy-start.5
  57.2 0.0 copy-start.8
  57.3 14.4 %all_to_all.31.tri = bf16[16,2,1152]{2,1,0:T(2,128)(2,1)S(1)} all-to-all(bf16[16,2,1152]{2,1,0:T(2,128)(2,1)S(1)} %add_parts.2), channel_id=1, replica_groups=mesh['zl'=4,'y'=4,'core'=2,'x'=4,'zh'=4] {'zh','zl'}, dimensions={0} | all-to-all | bytes 147456 | tf_op jit(solution)/shard_map/all_to_all | solution.py:267
  71.6 0.0 copy-done
  71.6 0.0 copy-done.1
  71.6 0.0 copy-done.2
  71.6 0.0 copy-done.4
  71.7 0.0 copy-done.5
  71.7 0.0 copy-done.8
  71.7 1.2 middle.1
  72.9 19.0 %all_to_all.32 = bf16[64,2,576]{2,1,0:T(2,128)(2,1)S(1)} all-to-all(bf16[64,2,576]{2,1,0:T(2,128)(2,1)S(1)} %get-tuple-element.12), channel_id=1, replica_groups=mesh['zl'=4,'y'=4,'core'=2,'x'=4,'zh'=4] {'x','zh','zl'}, dimensions={0} | all-to-all | bytes 294912 | tf_op jit(solution)/shard_map/all_to_all | solution.py:260
  91.9 0.0 copy-start.3
  91.9 6.2 %all_gather.7.both = bf16[128,2,576]{2,1,0:T(2,128)(2,1)S(1)} all-gather(bf16[64,2,576]{2,1,0:T(2,128)(2,1)S(1)} %all_to_all.32), channel_id=1, replica_groups=mesh['zl'=4,'y'=4,'core'=2,'x'=4,'zh'=4] {'core'}, dimensions={0}, use_global_device_ids=true | all-gather | bytes 442368 | tf_op jit(solution)/shard_map/all_gather | solution.py:261
  98.2 0.0 copy-done.3
  98.2 1.9 %incoming.1 = bf16[16,72,128]{2,1,0:T(8,128)(2,1)S(1)} custom-call(s32[1]{0:T(128)} %bitcast.1.core, bf16[128,2,576]{2,1,0:T(2,128)(2,1)S(1)} %all_gather.7.both, bf16[192,192]{1,0:T(8,128)(2,1)S(1)} %copy-done.3), custom_call_target="tpu_custom_call" | custom-call | tf_op jit(solution)/shard_map/incoming/pallas_call | solution.py:287
  100.1 12.2 %all_to_all.33.got = bf16[16,72,128]{2,1,0:T(8,128)(2,1)S(1)} all-to-all(bf16[16,72,128]{2,1,0:T(8,128)(2,1)S(1)} %incoming.1), channel_id=1, replica_groups=mesh['zl'=4,'y'=4,'core'=2,'x'=4,'zh'=4] {'x','y'}, dimensions={0} | all-to-all | bytes 589824 | tf_op jit(solution)/shard_map/all_to_all | solution.py:264
  112.3 0.2 add_parts.3
  112.5 0.0 copy-start.6
  112.5 14.2 %all_to_all.34.tri = bf16[16,2,1152]{2,1,0:T(2,128)(2,1)S(1)} all-to-all(bf16[16,2,1152]{2,1,0:T(2,128)(2,1)S(1)} %add_parts.3), channel_id=1, replica_groups=mesh['zl'=4,'y'=4,'core'=2,'x'=4,'zh'=4] {'zh','zl'}, dimensions={0} | all-to-all | bytes 147456 | tf_op jit(solution)/shard_map/all_to_all | solution.py:267
  126.7 0.0 copy-done.6
  126.7 1.2 last.1
Async XLA Ops:
  2.3 34.4 %all-to-all-start = ((bf16[64,2,576]{2,1,0:T(2,128)(2,1)}), bf16[64,2,576]{2,1,0:T(2,128)(2,1)S(1)}, u32[]{:S(2)}, u32[]{:S(2)}) async-start(bf16[64,2,576]{2,1,0:T(2,128)(2,1)} %get-tuple-element.9), calls=%async_computation | async-start | bytes 327680 | tf_op jit(solution)/shard_map/all_to_all | solution.py:260
  21.6 19.5 %copy-start.7 = (bf16[96,96]{1,0:T(8,128)(2,1)S(1)}, bf16[96,96]{1,0:T(8,128)(2,1)}, u32[]{:S(2)}) copy-start(bf16[96,96]{1,0:T(8,128)(2,1)} %constant.10.clone.rows) | copy-start | bytes 55300
  57.0 14.6 %copy-start = (bf16[128,640]{1,0:T(8,128)(2,1)S(1)}, bf16[128,640]{1,0:T(8,128)(2,1)}, u32[]{:S(2)}) copy-start(bf16[128,640]{1,0:T(8,128)(2,1)} %w_in.5) | copy-start | bytes 491524
  57.0 14.6 %copy-start.1 = (bf16[128,640]{1,0:T(8,128)(2,1)S(1)}, bf16[128,640]{1,0:T(8,128)(2,1)}, u32[]{:S(2)}) copy-start(bf16[128,640]{1,0:T(8,128)(2,1)} %w_in.4) | copy-start | bytes 491524
  57.2 14.4 %copy-start.2 = (bf16[12,24,128]{2,1,0:T(8,128)(2,1)S(1)}, bf16[12,24,128]{2,1,0:T(8,128)(2,1)}, u32[]{:S(2)}) copy-start(bf16[12,24,128]{2,1,0:T(8,128)(2,1)} %param.12) | copy-start | bytes 221188
  57.2 14.4 %copy-start.4 = (s32[12,24]{1,0:T(8,128)S(1)}, s32[12,24]{1,0:T(8,128)}, u32[]{:S(2)}) copy-start(s32[12,24]{1,0:T(8,128)} %mask.1) | copy-start | bytes 3460
  57.2 14.4 %copy-start.5 = (bf16[128,128]{1,0:T(8,128)(2,1)S(1)}, bf16[128,128]{1,0:T(8,128)(2,1)}, u32[]{:S(2)}) copy-start(bf16[128,128]{1,0:T(8,128)(2,1)} %w_out.2) | copy-start | bytes 98308
  57.2 14.4 %copy-start.8 = (f32[4,128]{1,0:T(4,128)S(1)}, f32[4,128]{1,0:T(4,128)}, u32[]{:S(2)}) copy-start(f32[4,128]{1,0:T(4,128)} %get-tuple-element.10.gains) | copy-start | bytes 6148
  91.9 6.3 %copy-start.3 = (bf16[192,192]{1,0:T(8,128)(2,1)S(1)}, bf16[192,192]{1,0:T(8,128)(2,1)}, u32[]{:S(2)}) copy-start(bf16[192,192]{1,0:T(8,128)(2,1)} %constant.11.clone.rows) | copy-start | bytes 221188
  112.5 14.2 %copy-start.6 = (bf16[128,128]{1,0:T(8,128)(2,1)S(1)}, bf16[128,128]{1,0:T(8,128)(2,1)}, u32[]{:S(2)}) copy-start(bf16[128,128]{1,0:T(8,128)(2,1)} %w_out.3) | copy-start | bytes 98308
